TPU v7x, 32 devices: a whole 2x2x4 slice. The times are simulated.
32 devices in a mesh: replica: 16 (over z, y, core), fsdp: 2 (over x).
Axes of the slice: x: 2, y: 2, z: 4, core: 2. Of those that a mesh axis runs over, the one named last changes fastest.
Arguments:
- params: float32 [16, 32, 5120], P('replica', 'fsdp'), may hold values from -0.012 to 0.012
- tracker: float32 [16, 32, 5120], P('replica', 'fsdp'), may hold values from -2.1 to 2.1
- last_grad: float32 [16, 32, 5120], P('replica', 'fsdp'), may hold values from -2.1 to 2.1
- first_moment: float32 [16, 32, 5120], P('replica', 'fsdp'), may hold values from -1.8 to 1.8
- second_moment: float32 [16, 32, 5120], P('replica', 'fsdp'), may hold values from 0.02 to 0.5
- local_grads: bfloat16 [4, 16, 2, 32, 5120], P(None, 'replica', 'fsdp'), may hold values from -6 to 6
Outputs:
- param_change: float32 [16, 32, 5120], P('replica', 'fsdp')
- moment_one: float32 [16, 32, 5120], P('replica', 'fsdp')
- moment_two: float32 [16, 32, 5120], P('replica', 'fsdp')
All inputs are finite; a program needn't handle non-finite values.
Results may differ from a plain program's by a relative error of at most 0.0003.
Values sent between devices are 32-bit elements; how exact they have to be, the bound alone decides.
No kernel may reach another device: no remote copies, remote signals or barrier semaphores. Data moves between devices by JAX's collectives and lax.ppermute only.
A program may use at most 64 MiB of HBM per device.

v0:
```python
import jax
import jax.numpy as jnp
from jax import lax
from jax.sharding import PartitionSpec as P

LEARNING_RATE = 0.001
BETA_ONE = 0.9
BETA_TWO = 0.999
EPSILON = 1e-08


def shifted(value, axis, steps):
    count = lax.axis_size(axis)
    pairs = [(source, (source + steps) % count) for source in range(count)]
    return lax.ppermute(value, axis, pairs)


def per_device(params, tracker, last_grad, first_moment, second_moment, local_grads):
    initial = params[0]
    weights = initial
    tracking = tracker[0]
    previous = last_grad[0]
    moment_one = first_moment[0]
    moment_two = second_moment[0]
    span_bits = lax.axis_size("replica").bit_length() - 1
    inverse_count = 1.0 / lax.axis_size("fsdp")
    step_count = local_grads.shape[0]
    for iteration in range(step_count):
        grad_total = lax.psum_scatter(
            local_grads[iteration, 0, 0].astype(jnp.float32),
            "fsdp",
            scatter_dimension=0,
            tiled=True,
        )
        mean_grad = grad_total * inverse_count
        distance = 2 ** (iteration % span_bits)
        remote_weights, remote_tracking = shifted((weights, tracking), "replica", distance)
        weights = 0.5 * (weights + remote_weights)
        tracking = 0.5 * (tracking + remote_tracking) + mean_grad - previous
        previous = mean_grad
        moment_one = BETA_ONE * moment_one + (1.0 - BETA_ONE) * tracking
        moment_two = BETA_TWO * moment_two + (1.0 - BETA_TWO) * tracking * tracking
        weights = weights - LEARNING_RATE * moment_one / (jnp.sqrt(moment_two) + EPSILON)
    change = (weights - initial) / LEARNING_RATE
    return (change[None], moment_one[None], moment_two[None])


def solution(mesh):
    in_specs = (
        P("replica", "fsdp", None),
        P("replica", "fsdp", None),
        P("replica", "fsdp", None),
        P("replica", "fsdp", None),
        P("replica", "fsdp", None),
        P(None, "replica", "fsdp", None, None),
    )
    out_specs = (P("replica", "fsdp", None), P("replica", "fsdp", None), P("replica", "fsdp", None))
    return jax.shard_map(
        per_device, mesh=mesh, in_specs=in_specs, out_specs=out_specs, check_vma=False
    )
```

profile of v0, /device:TPU:0, one launch (start us, length us, event | category | flops | bytes accessed | tf_op | source)
XLA Modules:
  0.0 116.5 jit_solution(3058717405162337304)
XLA Ops:
  7.2 0.0 copy-start.2
  7.2 0.0 copy-start.7
  7.2 0.0 reduce-scatter.5.cloned.1.call-start
  7.2 2.9 %bitcast_convert_fusion.2 = (f32[32,5120]{1,0:T(8,128)}, f32[32,5120]{1,0:T(8,128)}, f32[32,5120]{1,0:T(8,128)}, f32[32,5120]{1,0:T(8,128)}) fusion(bf16[4,1,1,32,5120]{4,3,2,1,0:T(8,128)(2,1)} %param.11), kind=kLoop, calls=%fused_computation.10 | loop fusion | flops 655360 | bytes 3932160 | tf_op jit(solution)/shard_map/convert_element_type | solution.py:30
  10.1 0.0 copy-start
  10.1 0.0 copy-start.1
  10.1 0.0 reduce-scatter.5.cloned.1.call-update
  10.2 0.0 reduce-scatter.7.cloned.1.call-start
  10.2 0.0 copy-done.2
  10.2 0.5 collective-permute-start
  10.7 0.0 copy-done.7
  10.7 2.6 %collective-permute-start.1 = (f32[16,5120]{1,0:T(8,128)S(1)}, f32[16,5120]{1,0:T(8,128)S(1)}, u32[]{:S(2)}, u32[]{:S(2)}) collective-permute-start(f32[16,5120]{1,0:T(8,128)S(1)} %bitcast.46), channel_id=1, source_target_pairs={{0,2},{2,4},{4,6},{6,8},{8,10},{10,12},{12,14},{14,16},{16,18},{18... | collective-permute-start | bytes 983048 | tf_op jit(solution)/shard_map/ppermute | solution.py:15
  13.3 0.0 reduce-scatter.7.cloned.1.call-update
  13.4 0.0 reduce-scatter.9.cloned.1.call-start
  13.4 7.0 %collective-permute-done = f32[16,5120]{1,0:T(8,128)S(1)} collective-permute-done((f32[16,5120]{1,0:T(8,128)S(1)}, f32[16,5120]{1,0:T(8,128)S(1)}, u32[]{:S(2)}, u32[]{:S(2)}) %collective-permute-start) | collective-permute-done | bytes 327712 | tf_op jit(solution)/shard_map/ppermute | solution.py:15
  20.5 3.5 %collective-permute-done.1 = f32[16,5120]{1,0:T(8,128)S(1)} collective-permute-done((f32[16,5120]{1,0:T(8,128)S(1)}, f32[16,5120]{1,0:T(8,128)S(1)}, u32[]{:S(2)}, u32[]{:S(2)}) %collective-permute-start.1) | collective-permute-done | bytes 327712 | tf_op jit(solution)/shard_map/ppermute | solution.py:15
  24.0 5.0 %reduce-scatter.5.cloned.1.call-done = f32[16,5120]{1,0:T(8,128)} async-done(((f32[32,5120]{1,0:T(8,128)}), f32[16,5120]{1,0:T(8,128)}) %reduce-scatter.5.cloned.1.call-update) | async-done | bytes 327696 | tf_op jit(solution)/shard_map/reduce_scatter | solution.py:29
  29.0 0.0 copy-done
  29.0 0.0 copy-done.1
  29.0 0.0 copy-done.6
  29.0 1.3 %divide_subtract_fusion.2 = (f32[16,5120]{1,0:T(8,128)S(1)}, f32[16,5120]{1,0:T(8,128)S(1)}) fusion(f32[16,5120]{1,0:T(8,128)S(1)} %collective-permute-done, f32[1,16,5120]{2,1,0:T(8,128)S(1)} %copy-done.2, f32[1,16,5120]{2,1,0:T(8,128)S(1)} %copy-done.1, f32[1,16,5120]{2,1,0:T(8,128)S(1)} %copy-done, f32[1,16,5120]{2,1,0:T(8,128)S(1)} %copy-done.6, ...), kind=kLoop, calls=%fused_computation.23 | loop fusion | flops 1474560 | bytes 3276800 | tf_op jit(solution)/shard_map/sub | solution.py:43
  30.3 1.5 %collective-permute-start.2 = (f32[16,5120]{1,0:T(8,128)S(1)}, f32[16,5120]{1,0:T(8,128)S(1)}, u32[]{:S(2)}, u32[]{:S(2)}) collective-permute-start(f32[16,5120]{1,0:T(8,128)S(1)} %get-tuple-element.10), channel_id=1, source_target_pairs={{0,4},{2,6},{4,8},{6,10},{8,12},{10,14},{12,16},{14,18},{16,20},{1... | collective-permute-start | bytes 983048 | tf_op jit(solution)/shard_map/ppermute | solution.py:15
  31.9 1.5 %collective-permute-start.3 = (f32[16,5120]{1,0:T(8,128)S(1)}, f32[16,5120]{1,0:T(8,128)}, u32[]{:S(2)}, u32[]{:S(2)}) collective-permute-start(f32[16,5120]{1,0:T(8,128)S(1)} %get-tuple-element.11), channel_id=1, source_target_pairs={{0,4},{2,6},{4,8},{6,10},{8,12},{10,14},{12,16},{14,18},{16,20},{1... | collective-permute-start | bytes 983048 | tf_op jit(solution)/shard_map/ppermute | solution.py:15
  33.3 0.0 reduce-scatter.9.cloned.1.call-update
  33.4 0.0 reduce-scatter.11.cloned.1.call-start
  33.4 14.0 %reduce-scatter.7.cloned.1.call-done = f32[16,5120]{1,0:T(8,128)} async-done(((f32[32,5120]{1,0:T(8,128)}), f32[16,5120]{1,0:T(8,128)}) %reduce-scatter.7.cloned.1.call-update) | async-done | bytes 327696 | tf_op jit(solution)/shard_map/reduce_scatter | solution.py:29
  47.4 0.0 collective-permute-done.2
  47.4 2.3 %collective-permute-done.3 = f32[16,5120]{1,0:T(8,128)} collective-permute-done((f32[16,5120]{1,0:T(8,128)S(1)}, f32[16,5120]{1,0:T(8,128)}, u32[]{:S(2)}, u32[]{:S(2)}) %collective-permute-start.3) | collective-permute-done | bytes 327712 | tf_op jit(solution)/shard_map/ppermute | solution.py:15
  49.7 0.0 copy-done.3
  49.7 1.4 %divide_subtract_fusion.1 = (f32[16,5120]{1,0:T(8,128)S(1)}, f32[16,5120]{1,0:T(8,128)S(1)}) fusion(f32[16,5120]{1,0:T(8,128)S(1)} %get-tuple-element.10, f32[16,5120]{1,0:T(8,128)S(1)} %collective-permute-done.2, f32[16,5120]{1,0:T(8,128)S(1)} %get-tuple-element.11, f32[1,16,5120]{2,1,0:T(8,128)S(1)} %copy-done.1, f32[1,16,5120]{2,1,0:T(8,128)S(1)} %copy-done, ...), kind=kLoop, calls=%fused_computation.20 | loop fusion | flops 2129920 | bytes 3276800 | tf_op jit(solution)/shard_map/sub | solution.py:43
  51.1 0.1 collective-permute-start.5
  51.2 0.0 reduce-scatter.11.cloned.1.call-update
  51.2 14.4 %reduce-scatter.9.cloned.1.call-done = f32[16,5120]{1,0:T(8,128)} async-done(((f32[32,5120]{1,0:T(8,128)}), f32[16,5120]{1,0:T(8,128)}) %reduce-scatter.9.cloned.1.call-update) | async-done | bytes 327696 | tf_op jit(solution)/shard_map/reduce_scatter | solution.py:29
  65.6 0.0 collective-permute-done.5
  65.6 0.0 copy-done.4
  65.6 1.1 add_subtract_fusion
  66.8 2.5 %collective-permute-start.7 = (f32[16,5120]{1,0:T(8,128)S(1)}, f32[16,5120]{1,0:T(8,128)S(1)}, u32[]{:S(2)}, u32[]{:S(2)}) collective-permute-start(f32[16,5120]{1,0:T(8,128)S(1)} %add_subtract_fusion), channel_id=1, source_target_pairs={{0,16},{2,18},{4,20},{6,22},{8,24},{10,26},{12,28},{14,30},{16,0},... | collective-permute-start | bytes 983048 | tf_op jit(solution)/shard_map/ppermute | solution.py:15
  69.2 1.5 %collective-permute-start.4 = (f32[16,5120]{1,0:T(8,128)S(1)}, f32[16,5120]{1,0:T(8,128)S(1)}, u32[]{:S(2)}, u32[]{:S(2)}) collective-permute-start(f32[16,5120]{1,0:T(8,128)S(1)} %get-tuple-element.8), channel_id=1, source_target_pairs={{0,8},{2,10},{4,12},{6,14},{8,16},{10,18},{12,20},{14,22},{16,24},... | collective-permute-start | bytes 983048 | tf_op jit(solution)/shard_map/ppermute | solution.py:15
  70.7 13.1 %reduce-scatter.11.cloned.1.call-done = f32[16,5120]{1,0:T(8,128)} async-done(((f32[32,5120]{1,0:T(8,128)}), f32[16,5120]{1,0:T(8,128)}) %reduce-scatter.11.cloned.1.call-update) | async-done | bytes 327696 | tf_op jit(solution)/shard_map/reduce_scatter | solution.py:29
  83.9 7.3 %collective-permute-done.7 = f32[16,5120]{1,0:T(8,128)S(1)} collective-permute-done((f32[16,5120]{1,0:T(8,128)S(1)}, f32[16,5120]{1,0:T(8,128)S(1)}, u32[]{:S(2)}, u32[]{:S(2)}) %collective-permute-start.7) | collective-permute-done | bytes 327712 | tf_op jit(solution)/shard_map/ppermute | solution.py:15
  91.2 0.0 copy-done.5
  91.2 1.9 %fusion.5 = (f32[1,16,5120]{2,1,0:T(8,128)}, f32[16,5120]{1,0:T(8,128)S(1)}, f32[16,5120]{1,0:T(8,128)S(1)}) fusion(f32[16,5120]{1,0:T(8,128)S(1)} %copy-done.5, f32[16,5120]{1,0:T(8,128)} %reduce-scatter.11.cloned.1.call-done, f32[16,5120]{1,0:T(8,128)S(1)} %add_subtract_fusion, f32[16,5120]{1,0:T(8,128)S(1)} %collective-permute-done.7, ...), kind=kLoop, calls=%fused_computation.25 | loop fusion | flops 1720320 | bytes 3276800 | tf_op jit(solution)/shard_map/broadcast_in_dim | solution.py:45
  93.1 0.9 fusion.4
  94.0 0.0 collective-permute-done.4
  94.0 0.2 divide_subtract_fusion
  94.2 0.1 collective-permute-start.6
  94.3 14.6 %collective-permute-done.6 = f32[16,5120]{1,0:T(8,128)S(1)} collective-permute-done((f32[16,5120]{1,0:T(8,128)S(1)}, f32[16,5120]{1,0:T(8,128)S(1)}, u32[]{:S(2)}, u32[]{:S(2)}) %collective-permute-start.6) | collective-permute-done | bytes 327712 | tf_op jit(solution)/shard_map/ppermute | solution.py:15
  108.9 1.0 multiply_bitcast_fusion
  (4 shorter events, 0.0 us)
Async XLA Ops:
  7.2 3.0 %copy-start.2 = (f32[1,16,5120]{2,1,0:T(8,128)S(1)}, f32[1,16,5120]{2,1,0:T(8,128)}, u32[]{:S(2)}) copy-start(f32[1,16,5120]{2,1,0:T(8,128)} %param.6) | copy-start | bytes 983044
  7.2 3.5 %copy-start.7 = (f32[1,16,5120]{2,1,0:T(8,128)S(1)}, f32[1,16,5120]{2,1,0:T(8,128)}, u32[]{:S(2)}) copy-start(f32[1,16,5120]{2,1,0:T(8,128)} %param.7) | copy-start | bytes 983044
  7.2 21.8 %reduce-scatter.5.cloned.1.call-start = ((), (), s32[]{:S(2)}) async-start(), calls=%async_computation.4 | async-start | bytes 983040 | tf_op jit(solution)/shard_map/reduce_scatter | solution.py:29
  10.1 18.9 %copy-start = (f32[1,16,5120]{2,1,0:T(8,128)S(1)}, f32[1,16,5120]{2,1,0:T(8,128)}, u32[]{:S(2)}) copy-start(f32[1,16,5120]{2,1,0:T(8,128)} %param.10) | copy-start | bytes 983044
  10.1 18.9 %copy-start.1 = (f32[1,16,5120]{2,1,0:T(8,128)S(1)}, f32[1,16,5120]{2,1,0:T(8,128)}, u32[]{:S(2)}) copy-start(f32[1,16,5120]{2,1,0:T(8,128)} %param.9) | copy-start | bytes 983044
  10.1 18.9 %copy-start.6 = (f32[1,16,5120]{2,1,0:T(8,128)S(1)}, f32[1,16,5120]{2,1,0:T(8,128)}, u32[]{:S(2)}) copy-start(f32[1,16,5120]{2,1,0:T(8,128)} %param.8) | copy-start | bytes 983044
  10.2 37.2 %reduce-scatter.7.cloned.1.call-start = ((), (), s32[]{:S(2)}) async-start(), calls=%async_computation.5 | async-start | bytes 983040 | tf_op jit(solution)/shard_map/reduce_scatter | solution.py:29
  10.2 10.3 %collective-permute-start = (f32[16,5120]{1,0:T(8,128)S(1)}, f32[16,5120]{1,0:T(8,128)S(1)}, u32[]{:S(2)}, u32[]{:S(2)}) collective-permute-start(f32[16,5120]{1,0:T(8,128)S(1)} %bitcast.45), channel_id=1, source_target_pairs={{0,2},{2,4},{4,6},{6,8},{8,10},{10,12},{12,14},{14,16},{16,18},{18... | collective-permute-start | bytes 983048 | tf_op jit(solution)/shard_map/ppermute | solution.py:15
  10.7 13.3 %collective-permute-start.1 = (f32[16,5120]{1,0:T(8,128)S(1)}, f32[16,5120]{1,0:T(8,128)S(1)}, u32[]{:S(2)}, u32[]{:S(2)}) collective-permute-start(f32[16,5120]{1,0:T(8,128)S(1)} %bitcast.46), channel_id=1, source_target_pairs={{0,2},{2,4},{4,6},{6,8},{8,10},{10,12},{12,14},{14,16},{16,18},{18... | collective-permute-start | bytes 983048 | tf_op jit(solution)/shard_map/ppermute | solution.py:15
  13.4 52.3 %reduce-scatter.9.cloned.1.call-start = ((), (), s32[]{:S(2)}) async-start(), calls=%async_computation.6 | async-start | bytes 983040 | tf_op jit(solution)/shard_map/reduce_scatter | solution.py:29
  29.0 20.7 %copy-start.3 = (f32[16,5120]{1,0:T(8,128)S(1)}, f32[16,5120]{1,0:T(8,128)}, u32[]{:S(2)}) copy-start(f32[16,5120]{1,0:T(8,128)} %reduce-scatter.5.cloned.1.call-done) | copy-start | bytes 983044
  30.3 17.0 %collective-permute-start.2 = (f32[16,5120]{1,0:T(8,128)S(1)}, f32[16,5120]{1,0:T(8,128)S(1)}, u32[]{:S(2)}, u32[]{:S(2)}) collective-permute-start(f32[16,5120]{1,0:T(8,128)S(1)} %get-tuple-element.10), channel_id=1, source_target_pairs={{0,4},{2,6},{4,8},{6,10},{8,12},{10,14},{12,16},{14,18},{16,20},{1... | collective-permute-start | bytes 983048 | tf_op jit(solution)/shard_map/ppermute | solution.py:15
  31.9 17.8 %collective-permute-start.3 = (f32[16,5120]{1,0:T(8,128)S(1)}, f32[16,5120]{1,0:T(8,128)}, u32[]{:S(2)}, u32[]{:S(2)}) collective-permute-start(f32[16,5120]{1,0:T(8,128)S(1)} %get-tuple-element.11), channel_id=1, source_target_pairs={{0,4},{2,6},{4,8},{6,10},{8,12},{10,14},{12,16},{14,18},{16,20},{1... | collective-permute-start | bytes 983048 | tf_op jit(solution)/shard_map/ppermute | solution.py:15
  33.4 50.5 %reduce-scatter.11.cloned.1.call-start = ((), (), s32[]{:S(2)}) async-start(), calls=%async_computation.7 | async-start | bytes 983040 | tf_op jit(solution)/shard_map/reduce_scatter | solution.py:29
  47.4 18.3 %copy-start.4 = (f32[16,5120]{1,0:T(8,128)S(1)}, f32[16,5120]{1,0:T(8,128)}, u32[]{:S(2)}) copy-start(f32[16,5120]{1,0:T(8,128)} %reduce-scatter.7.cloned.1.call-done) | copy-start | bytes 983044
  51.1 14.5 %collective-permute-start.5 = (f32[16,5120]{1,0:T(8,128)S(1)}, f32[16,5120]{1,0:T(8,128)S(1)}, u32[]{:S(2)}, u32[]{:S(2)}) collective-permute-start(f32[16,5120]{1,0:T(8,128)S(1)} %get-tuple-element.9), channel_id=1, source_target_pairs={{0,8},{2,10},{4,12},{6,14},{8,16},{10,18},{12,20},{14,22},{16,24},... | collective-permute-start | bytes 983048 | tf_op jit(solution)/shard_map/ppermute | solution.py:15
  65.6 25.6 %copy-start.5 = (f32[16,5120]{1,0:T(8,128)S(1)}, f32[16,5120]{1,0:T(8,128)}, u32[]{:S(2)}) copy-start(f32[16,5120]{1,0:T(8,128)} %reduce-scatter.9.cloned.1.call-done) | copy-start | bytes 983044
  66.8 24.5 %collective-permute-start.7 = (f32[16,5120]{1,0:T(8,128)S(1)}, f32[16,5120]{1,0:T(8,128)S(1)}, u32[]{:S(2)}, u32[]{:S(2)}) collective-permute-start(f32[16,5120]{1,0:T(8,128)S(1)} %add_subtract_fusion), channel_id=1, source_target_pairs={{0,16},{2,18},{4,20},{6,22},{8,24},{10,26},{12,28},{14,30},{16,0},... | collective-permute-start | bytes 983048 | tf_op jit(solution)/shard_map/ppermute | solution.py:15
  69.2 24.8 %collective-permute-start.4 = (f32[16,5120]{1,0:T(8,128)S(1)}, f32[16,5120]{1,0:T(8,128)S(1)}, u32[]{:S(2)}, u32[]{:S(2)}) collective-permute-start(f32[16,5120]{1,0:T(8,128)S(1)} %get-tuple-element.8), channel_id=1, source_target_pairs={{0,8},{2,10},{4,12},{6,14},{8,16},{10,18},{12,20},{14,22},{16,24},... | collective-permute-start | bytes 983048 | tf_op jit(solution)/shard_map/ppermute | solution.py:15
  94.2 14.7 %collective-permute-start.6 = (f32[16,5120]{1,0:T(8,128)S(1)}, f32[16,5120]{1,0:T(8,128)S(1)}, u32[]{:S(2)}, u32[]{:S(2)}) collective-permute-start(f32[16,5120]{1,0:T(8,128)S(1)} %divide_subtract_fusion), channel_id=1, source_target_pairs={{0,16},{2,18},{4,20},{6,22},{8,24},{10,26},{12,28},{14,30},{16,0},... | collective-permute-start | bytes 983048 | tf_op jit(solution)/shard_map/ppermute | solution.py:15
Sparse Core Ops, SparseCore 0:
  10.3 18.6 reduce-scatter.4
  31.3 15.9 reduce-scatter.6
  49.6 15.9 reduce-scatter.8
  67.8 15.9 reduce-scatter.10
where the time goes:
time: 117 us; the launch traced here: 116 us
  waiting for transfers between devices  81.5 us (70%)
  between operations  13.8 us (12%)
  other arithmetic  10.8 us (9%)
  starting transfers between devices  10.4 us (9%)
    reduce_scatter x4, waiting for transfers between devices, per_device(): lax.psum_scatter(local_grads[iteration, 0, 0].astype(jnp.float32), 'fsdp'...  46.6 us
    ppermute x8, waiting for transfers between devices, shifted(): return lax.ppermute(value, axis, pairs)  34.8 us
    ppermute x8, starting transfers between devices, shifted(): return lax.ppermute(value, axis, pairs)  10.2 us
    broadcast_in_dim x3, other arithmetic, per_device(): return (change[None], moment_one[None], moment_two[None])  3.83 us
    sub x3, other arithmetic, per_device(): weights - LEARNING_RATE * moment_one / (jnp.sqrt(moment_two) + EPSILON)  2.94 us
    convert_element_type x1, other arithmetic, per_device(): local_grads[iteration, 0, 0].astype(jnp.float32)  2.89 us
  transfers between devices with their start and end apart: 12, of which 9 were waited for; matrix products, arithmetic and copies ran while one was open for 6% of the time, Pallas kernels for 0%

commit v1 on v0

--- a/solution.py
+++ b/solution.py
@@ -15,6 +15,23 @@
     return lax.ppermute(value, axis, pairs)
 
 
+def swapped(value, axis, distance):
+    count = lax.axis_size(axis)
+    pairs = [(source, source ^ distance) for source in range(count)]
+    return lax.ppermute(value, axis, pairs)
+
+
+def gradient_sum(local, rows):
+    count = lax.axis_size("fsdp")
+    place = lax.axis_index("fsdp")
+    total = lax.dynamic_slice_in_dim(local, place * rows, rows, 1).astype(jnp.float32)
+    for distance in range(1, count):
+        target = (place + distance) % count
+        outgoing = lax.dynamic_slice_in_dim(local, target * rows, rows, 1).astype(jnp.float32)
+        total = total + shifted(outgoing, "fsdp", distance)
+    return total
+
+
 def per_device(params, tracker, last_grad, first_moment, second_moment, local_grads):
     initial = params[0]
     weights = initial
@@ -22,19 +39,21 @@
     previous = last_grad[0]
     moment_one = first_moment[0]
     moment_two = second_moment[0]
-    span_bits = lax.axis_size("replica").bit_length() - 1
+    rows = initial.shape[0]
+    replicas = lax.axis_size("replica")
+    span_bits = replicas.bit_length() - 1
     inverse_count = 1.0 / lax.axis_size("fsdp")
     step_count = local_grads.shape[0]
+    whole_span = step_count == span_bits and replicas == 2**span_bits
+    sums = [gradient_sum(local_grads[k : k + 1, 0, 0], rows)[0] for k in range(step_count)]
     for iteration in range(step_count):
-        grad_total = lax.psum_scatter(
-            local_grads[iteration, 0, 0].astype(jnp.float32),
-            "fsdp",
-            scatter_dimension=0,
-            tiled=True,
-        )
-        mean_grad = grad_total * inverse_count
+        mean_grad = sums[iteration] * inverse_count
         distance = 2 ** (iteration % span_bits)
-        remote_weights, remote_tracking = shifted((weights, tracking), "replica", distance)
+        remote_tracking = shifted(tracking, "replica", distance)
+        if whole_span:
+            remote_weights = swapped(weights, "replica", distance)
+        else:
+            remote_weights = shifted(weights, "replica", distance)
         weights = 0.5 * (weights + remote_weights)
         tracking = 0.5 * (tracking + remote_tracking) + mean_grad - previous
         previous = mean_grad

time: 117 us -> 75.3 us (0.64)
  waiting for transfers between devices: 81.5 us -> 54.8 us
  between operations: 13.8 us -> 0.73 us
  other arithmetic: 10.8 us -> 6.08 us
  starting transfers between devices: 10.4 us -> 12.1 us
  local copies, waits for them, and re-layouts: 0.03 us -> 1.45 us
    reduce_scatter x4 -> x0, waiting for transfers between devices: 46.6 us -> none  [per_device(): lax.psum_scatter(local_grads[iteration, 0, 0].astype(jnp.float32), 'fsdp'...]
    ppermute x0 -> x4, waiting for transfers between devices: none -> 26.5 us  [swapped(): return lax.ppermute(value, axis, pairs)]
    ppermute x8, waiting for transfers between devices: 34.8 us -> 28.3 us  [shifted(): return lax.ppermute(value, axis, pairs)]
    ppermute x0 -> x4, starting transfers between devices: none -> 2.83 us  [swapped(): return lax.ppermute(value, axis, pairs)]
    convert_element_type x1 -> x4, other arithmetic: 2.89 us -> 0.82 us  [gradient_sum(): lax.dynamic_slice_in_dim(local, target * rows, rows, 1).astype(jnp.float32)]
    slice x0 -> x1, local copies, waits for them, and re-layouts: none -> 1.44 us  [per_device(): local_grads[k:k + 1, 0, 0]]
  transfers between devices with their start and end apart: 12 -> 12, of which waited for: 9 -> 7; matrix products, arithmetic and copies ran while one was open for 6% -> 6% of each run, Pallas kernels for 0% -> 0%
where the time goes in v1:
time: 75.3 us; the launch traced here: 75.2 us
  waiting for transfers between devices  54.8 us (73%)
  starting transfers between devices  12.1 us (16%)
  other arithmetic  6.08 us (8%)
  local copies, waits for them, and re-layouts  1.45 us (2%)
    ppermute x8, waiting for transfers between devices, shifted(): return lax.ppermute(value, axis, pairs)  28.3 us
    ppermute x4, waiting for transfers between devices, swapped(): return lax.ppermute(value, axis, pairs)  26.5 us
    ppermute x8, starting transfers between devices, shifted(): return lax.ppermute(value, axis, pairs)  9.31 us
    broadcast_in_dim x3, other arithmetic, per_device(): return (change[None], moment_one[None], moment_two[None])  2.91 us
    ppermute x4, starting transfers between devices, swapped(): return lax.ppermute(value, axis, pairs)  2.83 us
    sub x3, other arithmetic, per_device(): weights - LEARNING_RATE * moment_one / (jnp.sqrt(moment_two) + EPSILON)  2.19 us
  transfers between devices with their start and end apart: 12, of which 7 were waited for; matrix products, arithmetic and copies ran while one was open for 6% of the time, Pallas kernels for 0%

profile of v1, /device:TPU:0, one launch (start us, length us, event | category | flops | bytes accessed | tf_op | source)
XLA Modules:
  0.0 75.2 jit_solution(17845886868244407372)
XLA Ops:
  0.6 0.0 copy-start.2
  0.7 0.0 copy-start
  0.7 0.0 copy-start.1
  0.7 1.4 %fusion.18 = (bf16[1,1,1,32,5120]{4,3,2,1,0:T(8,128)(2,1)S(1)}, bf16[1,1,1,32,5120]{4,3,2,1,0:T(8,128)(2,1)S(1)}, bf16[1,1,1,32,5120]{4,3,2,1,0:T(8,128)(2,1)S(1)}, bf16[1,1,1,32,5120]{4,3,2,1,0:T(8,128)(2,1)S(1)}) fusion(bf16[4,1,1,32,5120]{4,3,2,1,0:T(8,128)(2,1)} %param.11), kind=kLoop, calls=%fused_computation.39 | loop fusion | bytes 2621440 | tf_op jit(solution)/shard_map/slice | solution.py:48
  2.1 0.8 %bitcast_convert_fusion.3 = f32[1,16,5120]{2,1,0:T(8,128)} fusion(bf16[1,1,1,32,5120]{4,3,2,1,0:T(8,128)(2,1)S(1)} %get-tuple-element.13, s32[]{:T(128)S(6)} %select_n.27), kind=kLoop, calls=%fused_computation.36 | loop fusion | flops 81920 | bytes 491524 | tf_op jit(solution)/shard_map/convert_element_type | solution.py:30
  2.9 2.9 %collective-permute-start.2 = (f32[1,16,5120]{2,1,0:T(8,128)}, f32[1,16,5120]{2,1,0:T(8,128)S(1)}, u32[]{:S(2)}, u32[]{:S(2)}) collective-permute-start(f32[1,16,5120]{2,1,0:T(8,128)} %bitcast_convert_fusion.3), channel_id=1, source_target_pairs={{0,1},{1,0},{2,3},{3,2},{4,5},{5,4},{6,7},{7,6},{8,9},{9,8},{10,11... | collective-permute-start | bytes 983048 | tf_op jit(solution)/shard_map/ppermute | solution.py:15
  5.8 0.0 copy-done.2
  5.8 0.0 collective-permute-start
  5.8 0.5 collective-permute-start.1
  6.4 0.1 collective-permute-start.5
  6.4 8.1 %collective-permute-done.2 = f32[1,16,5120]{2,1,0:T(8,128)S(1)} collective-permute-done((f32[1,16,5120]{2,1,0:T(8,128)}, f32[1,16,5120]{2,1,0:T(8,128)S(1)}, u32[]{:S(2)}, u32[]{:S(2)}) %collective-permute-start.2) | collective-permute-done | bytes 327712 | tf_op jit(solution)/shard_map/ppermute | solution.py:15
  14.6 0.0 collective-permute-done
  14.6 1.0 %collective-permute-done.1 = f32[16,5120]{1,0:T(8,128)} collective-permute-done((f32[16,5120]{1,0:T(8,128)}, f32[16,5120]{1,0:T(8,128)}, u32[]{:S(2)}, u32[]{:S(2)}) %collective-permute-start.1) | collective-permute-done | bytes 327712 | tf_op jit(solution)/shard_map/ppermute | solution.py:15
  15.6 0.0 copy-done
  15.6 0.0 copy-done.1
  15.6 1.6 %divide_subtract_fusion.2 = (f32[16,5120]{1,0:T(8,128)S(1)}, f32[16,5120]{1,0:T(8,128)S(1)}) fusion(f32[16,5120]{1,0:T(8,128)} %collective-permute-done, f32[1,16,5120]{2,1,0:T(8,128)S(1)} %copy-done.2, f32[1,16,5120]{2,1,0:T(8,128)S(1)} %copy-done, f32[1,16,5120]{2,1,0:T(8,128)S(1)} %copy-done.1, f32[1,16,5120]{2,1,0:T(8,128)} %param.8, ...), kind=kLoop, calls=%fused_computation.32 | loop fusion | flops 1638400 | bytes 3440644 | tf_op jit(solution)/shard_map/sub | solution.py:62
  17.1 1.2 %collective-permute-start.3 = (f32[16,5120]{1,0:T(8,128)S(1)}, f32[16,5120]{1,0:T(8,128)S(1)}, u32[]{:S(2)}, u32[]{:S(2)}) collective-permute-start(f32[16,5120]{1,0:T(8,128)S(1)} %get-tuple-element.10), channel_id=1, source_target_pairs={{0,4},{2,6},{4,0},{6,2},{8,12},{10,14},{12,8},{14,10},{16,20},{18,... | collective-permute-start | bytes 983048 | tf_op jit(solution)/shard_map/ppermute | solution.py:21
  18.3 0.9 %collective-permute-start.4 = (f32[16,5120]{1,0:T(8,128)S(1)}, f32[16,5120]{1,0:T(8,128)S(1)}, u32[]{:S(2)}, u32[]{:S(2)}) collective-permute-start(f32[16,5120]{1,0:T(8,128)S(1)} %get-tuple-element.11), channel_id=1, source_target_pairs={{0,4},{2,6},{4,8},{6,10},{8,12},{10,14},{12,16},{14,18},{16,20},{1... | collective-permute-start | bytes 983048 | tf_op jit(solution)/shard_map/ppermute | solution.py:15
  19.3 1.1 %collective-permute-start.8 = (f32[1,16,5120]{2,1,0:T(8,128)S(1)}, f32[1,16,5120]{2,1,0:T(8,128)S(1)}, u32[]{:S(2)}, u32[]{:S(2)}) collective-permute-start(f32[1,16,5120]{2,1,0:T(8,128)S(1)} %bitcast_convert_fusion.1), channel_id=1, source_target_pairs={{0,1},{1,0},{2,3},{3,2},{4,5},{5,4},{6,7},{7,6},{8,9},{9,8},{10,11... | collective-permute-start | bytes 983048 | tf_op jit(solution)/shard_map/ppermute | solution.py:15
  20.4 1.2 %collective-permute-done.5 = f32[1,16,5120]{2,1,0:T(8,128)S(1)} collective-permute-done((f32[1,16,5120]{2,1,0:T(8,128)S(1)}, f32[1,16,5120]{2,1,0:T(8,128)S(1)}, u32[]{:S(2)}, u32[]{:S(2)}) %collective-permute-start.5) | collective-permute-done | bytes 327712 | tf_op jit(solution)/shard_map/ppermute | solution.py:15
  21.6 9.9 %collective-permute-done.3 = f32[16,5120]{1,0:T(8,128)S(1)} collective-permute-done((f32[16,5120]{1,0:T(8,128)S(1)}, f32[16,5120]{1,0:T(8,128)S(1)}, u32[]{:S(2)}, u32[]{:S(2)}) %collective-permute-start.3) | collective-permute-done | bytes 327712 | tf_op jit(solution)/shard_map/ppermute | solution.py:21
  31.4 0.0 collective-permute-done.4
  31.4 0.4 divide_subtract_fusion.1
  31.9 1.6 %collective-permute-start.7 = (f32[16,5120]{1,0:T(8,128)S(1)}, f32[16,5120]{1,0:T(8,128)S(1)}, u32[]{:S(2)}, u32[]{:S(2)}) collective-permute-start(f32[16,5120]{1,0:T(8,128)S(1)} %get-tuple-element.9), channel_id=1, source_target_pairs={{0,8},{2,10},{4,12},{6,14},{8,16},{10,18},{12,20},{14,22},{16,24},... | collective-permute-start | bytes 983048 | tf_op jit(solution)/shard_map/ppermute | solution.py:15
  33.5 1.5 %collective-permute-start.11 = (f32[1,16,5120]{2,1,0:T(8,128)S(1)}, f32[1,16,5120]{2,1,0:T(8,128)S(1)}, u32[]{:S(2)}, u32[]{:S(2)}) collective-permute-start(f32[1,16,5120]{2,1,0:T(8,128)S(1)} %bitcast_convert_fusion), channel_id=1, source_target_pairs={{0,1},{1,0},{2,3},{3,2},{4,5},{5,4},{6,7},{7,6},{8,9},{9,8},{10,11... | collective-permute-start | bytes 983048 | tf_op jit(solution)/shard_map/ppermute | solution.py:15
  34.9 0.0 collective-permute-done.8
  34.9 6.4 %collective-permute-done.7 = f32[16,5120]{1,0:T(8,128)S(1)} collective-permute-done((f32[16,5120]{1,0:T(8,128)S(1)}, f32[16,5120]{1,0:T(8,128)S(1)}, u32[]{:S(2)}, u32[]{:S(2)}) %collective-permute-start.7) | collective-permute-done | bytes 327712 | tf_op jit(solution)/shard_map/ppermute | solution.py:15
  41.3 0.2 add_subtract_fusion
  41.5 0.7 collective-permute-start.10
  42.2 1.6 %collective-permute-start.6 = (f32[16,5120]{1,0:T(8,128)S(1)}, f32[16,5120]{1,0:T(8,128)S(1)}, u32[]{:S(2)}, u32[]{:S(2)}) collective-permute-start(f32[16,5120]{1,0:T(8,128)S(1)} %get-tuple-element.8), channel_id=1, source_target_pairs={{0,8},{2,10},{4,12},{6,14},{8,0},{10,2},{12,4},{14,6},{16,24},{18,... | collective-permute-start | bytes 983048 | tf_op jit(solution)/shard_map/ppermute | solution.py:21
  43.8 0.0 collective-permute-done.11
  43.8 11.6 %collective-permute-done.10 = f32[16,5120]{1,0:T(8,128)S(1)} collective-permute-done((f32[16,5120]{1,0:T(8,128)S(1)}, f32[16,5120]{1,0:T(8,128)S(1)}, u32[]{:S(2)}, u32[]{:S(2)}) %collective-permute-start.10) | collective-permute-done | bytes 327712 | tf_op jit(solution)/shard_map/ppermute | solution.py:15
  55.4 1.0 %fusion.15 = (f32[1,16,5120]{2,1,0:T(8,128)}, f32[16,5120]{1,0:T(8,128)S(1)}, f32[16,5120]{1,0:T(8,128)S(1)}) fusion(f32[1,16,5120]{2,1,0:T(8,128)S(1)} %collective-permute-done.8, bf16[1,1,1,32,5120]{4,3,2,1,0:T(8,128)(2,1)S(1)} %get-tuple-element.15, s32[]{:T(128)S(6)} %select_n.25, f32[1,16,5120]{2,1,0:T(8,128)S(1)} %collective-permute-done.11, ...), kind=kLoop, calls=%fused_computation.38 | loop fusion | flops 2048000 | bytes 3604484 | tf_op jit(solution)/shard_map/broadcast_in_dim | solution.py:64
  56.4 0.9 %fusion.14 = (f32[1,16,5120]{2,1,0:T(8,128)}, f32[16,5120]{1,0:T(8,128)S(1)}) fusion(f32[16,5120]{1,0:T(8,128)S(1)} %get-tuple-element.4, f32[16,5120]{1,0:T(8,128)S(1)} %add_subtract_fusion, f32[16,5120]{1,0:T(8,128)S(1)} %get-tuple-element.9, f32[16,5120]{1,0:T(8,128)S(1)} %get-tuple-element.11, f32[1,16,5120]{2,1,0:T(8,128)S(1)} %copy-done), kind=kLoop, calls=%fused_computation.37 | loop fusion | flops 983040 | bytes 2293760 | tf_op jit(solution)/shard_map/broadcast_in_dim | solution.py:64
  57.3 0.0 collective-permute-done.6
  57.3 0.2 divide_subtract_fusion
  57.5 0.1 collective-permute-start.9
  57.5 16.7 %collective-permute-done.9 = f32[16,5120]{1,0:T(8,128)S(1)} collective-permute-done((f32[16,5120]{1,0:T(8,128)S(1)}, f32[16,5120]{1,0:T(8,128)S(1)}, u32[]{:S(2)}, u32[]{:S(2)}) %collective-permute-start.9) | collective-permute-done | bytes 327712 | tf_op jit(solution)/shard_map/ppermute | solution.py:21
  74.2 1.0 %multiply_bitcast_fusion = f32[1,16,5120]{2,1,0:T(8,128)} fusion(f32[16,5120]{1,0:T(8,128)S(1)} %divide_subtract_fusion, f32[16,5120]{1,0:T(8,128)S(1)} %collective-permute-done.9, f32[16,5120]{1,0:T(8,128)S(1)} %get-tuple-element.4, f32[16,5120]{1,0:T(8,128)S(1)} %get-tuple-element.7, f32[16,5120]{1,0:T(8,128)S(1)} %get-tuple-element.5, ...), kind=kLoop, calls=%fused_computation.24 | loop fusion | flops 1228800 | bytes 2293760 | tf_op jit(solution)/shard_map/broadcast_in_dim | solution.py:64
  (3 shorter events, 0.1 us)
Async XLA Ops:
  0.6 5.2 %copy-start.2 = (f32[1,16,5120]{2,1,0:T(8,128)S(1)}, f32[1,16,5120]{2,1,0:T(8,128)}, u32[]{:S(2)}) copy-start(f32[1,16,5120]{2,1,0:T(8,128)} %param.6) | copy-start | bytes 983044
  0.7 14.9 %copy-start = (f32[1,16,5120]{2,1,0:T(8,128)S(1)}, f32[1,16,5120]{2,1,0:T(8,128)}, u32[]{:S(2)}) copy-start(f32[1,16,5120]{2,1,0:T(8,128)} %param.9) | copy-start | bytes 983044
  0.7 14.9 %copy-start.1 = (f32[1,16,5120]{2,1,0:T(8,128)S(1)}, f32[1,16,5120]{2,1,0:T(8,128)}, u32[]{:S(2)}) copy-start(f32[1,16,5120]{2,1,0:T(8,128)} %param.10) | copy-start | bytes 983044
  2.9 11.7 %collective-permute-start.2 = (f32[1,16,5120]{2,1,0:T(8,128)}, f32[1,16,5120]{2,1,0:T(8,128)S(1)}, u32[]{:S(2)}, u32[]{:S(2)}) collective-permute-start(f32[1,16,5120]{2,1,0:T(8,128)} %bitcast_convert_fusion.3), channel_id=1, source_target_pairs={{0,1},{1,0},{2,3},{3,2},{4,5},{5,4},{6,7},{7,6},{8,9},{9,8},{10,11... | collective-permute-start | bytes 983048 | tf_op jit(solution)/shard_map/ppermute | solution.py:15
  5.8 8.7 %collective-permute-start = (f32[16,5120]{1,0:T(8,128)S(1)}, f32[16,5120]{1,0:T(8,128)}, u32[]{:S(2)}, u32[]{:S(2)}) collective-permute-start(f32[16,5120]{1,0:T(8,128)S(1)} %bitcast.96), channel_id=1, source_target_pairs={{0,2},{2,0},{4,6},{6,4},{8,10},{10,8},{12,14},{14,12},{16,18},{18,... | collective-permute-start | bytes 983048 | tf_op jit(solution)/shard_map/ppermute | solution.py:21
  5.8 9.7 %collective-permute-start.1 = (f32[16,5120]{1,0:T(8,128)}, f32[16,5120]{1,0:T(8,128)}, u32[]{:S(2)}, u32[]{:S(2)}) collective-permute-start(f32[16,5120]{1,0:T(8,128)} %bitcast.2), channel_id=1, source_target_pairs={{0,2},{2,4},{4,6},{6,8},{8,10},{10,12},{12,14},{14,16},{16,18},{18... | collective-permute-start | bytes 983048 | tf_op jit(solution)/shard_map/ppermute | solution.py:15
  6.4 15.2 %collective-permute-start.5 = (f32[1,16,5120]{2,1,0:T(8,128)S(1)}, f32[1,16,5120]{2,1,0:T(8,128)S(1)}, u32[]{:S(2)}, u32[]{:S(2)}) collective-permute-start(f32[1,16,5120]{2,1,0:T(8,128)S(1)} %bitcast_convert_fusion.2), channel_id=1, source_target_pairs={{0,1},{1,0},{2,3},{3,2},{4,5},{5,4},{6,7},{7,6},{8,9},{9,8},{10,11... | collective-permute-start | bytes 983048 | tf_op jit(solution)/shard_map/ppermute | solution.py:15
  17.1 14.3 %collective-permute-start.3 = (f32[16,5120]{1,0:T(8,128)S(1)}, f32[16,5120]{1,0:T(8,128)S(1)}, u32[]{:S(2)}, u32[]{:S(2)}) collective-permute-start(f32[16,5120]{1,0:T(8,128)S(1)} %get-tuple-element.10), channel_id=1, source_target_pairs={{0,4},{2,6},{4,0},{6,2},{8,12},{10,14},{12,8},{14,10},{16,20},{18,... | collective-permute-start | bytes 983048 | tf_op jit(solution)/shard_map/ppermute | solution.py:21
  18.3 13.1 %collective-permute-start.4 = (f32[16,5120]{1,0:T(8,128)S(1)}, f32[16,5120]{1,0:T(8,128)S(1)}, u32[]{:S(2)}, u32[]{:S(2)}) collective-permute-start(f32[16,5120]{1,0:T(8,128)S(1)} %get-tuple-element.11), channel_id=1, source_target_pairs={{0,4},{2,6},{4,8},{6,10},{8,12},{10,14},{12,16},{14,18},{16,20},{1... | collective-permute-start | bytes 983048 | tf_op jit(solution)/shard_map/ppermute | solution.py:15
  19.3 15.7 %collective-permute-start.8 = (f32[1,16,5120]{2,1,0:T(8,128)S(1)}, f32[1,16,5120]{2,1,0:T(8,128)S(1)}, u32[]{:S(2)}, u32[]{:S(2)}) collective-permute-start(f32[1,16,5120]{2,1,0:T(8,128)S(1)} %bitcast_convert_fusion.1), channel_id=1, source_target_pairs={{0,1},{1,0},{2,3},{3,2},{4,5},{5,4},{6,7},{7,6},{8,9},{9,8},{10,11... | collective-permute-start | bytes 983048 | tf_op jit(solution)/shard_map/ppermute | solution.py:15
  31.9 9.5 %collective-permute-start.7 = (f32[16,5120]{1,0:T(8,128)S(1)}, f32[16,5120]{1,0:T(8,128)S(1)}, u32[]{:S(2)}, u32[]{:S(2)}) collective-permute-start(f32[16,5120]{1,0:T(8,128)S(1)} %get-tuple-element.9), channel_id=1, source_target_pairs={{0,8},{2,10},{4,12},{6,14},{8,16},{10,18},{12,20},{14,22},{16,24},... | collective-permute-start | bytes 983048 | tf_op jit(solution)/shard_map/ppermute | solution.py:15
  33.5 10.3 %collective-permute-start.11 = (f32[1,16,5120]{2,1,0:T(8,128)S(1)}, f32[1,16,5120]{2,1,0:T(8,128)S(1)}, u32[]{:S(2)}, u32[]{:S(2)}) collective-permute-start(f32[1,16,5120]{2,1,0:T(8,128)S(1)} %bitcast_convert_fusion), channel_id=1, source_target_pairs={{0,1},{1,0},{2,3},{3,2},{4,5},{5,4},{6,7},{7,6},{8,9},{9,8},{10,11... | collective-permute-start | bytes 983048 | tf_op jit(solution)/shard_map/ppermute | solution.py:15
  41.5 13.9 %collective-permute-start.10 = (f32[16,5120]{1,0:T(8,128)S(1)}, f32[16,5120]{1,0:T(8,128)S(1)}, u32[]{:S(2)}, u32[]{:S(2)}) collective-permute-start(f32[16,5120]{1,0:T(8,128)S(1)} %add_subtract_fusion), channel_id=1, source_target_pairs={{0,16},{2,18},{4,20},{6,22},{8,24},{10,26},{12,28},{14,30},{16,0},... | collective-permute-start | bytes 983048 | tf_op jit(solution)/shard_map/ppermute | solution.py:15
  42.2 15.1 %collective-permute-start.6 = (f32[16,5120]{1,0:T(8,128)S(1)}, f32[16,5120]{1,0:T(8,128)S(1)}, u32[]{:S(2)}, u32[]{:S(2)}) collective-permute-start(f32[16,5120]{1,0:T(8,128)S(1)} %get-tuple-element.8), channel_id=1, source_target_pairs={{0,8},{2,10},{4,12},{6,14},{8,0},{10,2},{12,4},{14,6},{16,24},{18,... | collective-permute-start | bytes 983048 | tf_op jit(solution)/shard_map/ppermute | solution.py:21
  57.5 16.7 %collective-permute-start.9 = (f32[16,5120]{1,0:T(8,128)S(1)}, f32[16,5120]{1,0:T(8,128)S(1)}, u32[]{:S(2)}, u32[]{:S(2)}) collective-permute-start(f32[16,5120]{1,0:T(8,128)S(1)} %divide_subtract_fusion), channel_id=1, source_target_pairs={{0,16},{2,18},{4,20},{6,22},{8,24},{10,26},{12,28},{14,30},{16,0},... | collective-permute-start | bytes 983048 | tf_op jit(solution)/shard_map/ppermute | solution.py:21

commit v2 on v1

--- a/solution.py
+++ b/solution.py
@@ -45,21 +45,28 @@
     inverse_count = 1.0 / lax.axis_size("fsdp")
     step_count = local_grads.shape[0]
     whole_span = step_count == span_bits and replicas == 2**span_bits
-    sums = [gradient_sum(local_grads[k : k + 1, 0, 0], rows)[0] for k in range(step_count)]
+    mixed = swapped if whole_span else shifted
+    local = local_grads[:, 0, 0]
+
+    remote_tracking = shifted(tracking, "replica", 1)
+    sums = [gradient_sum(local[k : k + 1], rows)[0] for k in range(step_count)]
+    remote_weights = mixed(weights, "replica", 1)
     for iteration in range(step_count):
         mean_grad = sums[iteration] * inverse_count
-        distance = 2 ** (iteration % span_bits)
-        remote_tracking = shifted(tracking, "replica", distance)
-        if whole_span:
-            remote_weights = swapped(weights, "replica", distance)
-        else:
-            remote_weights = shifted(weights, "replica", distance)
-        weights = 0.5 * (weights + remote_weights)
         tracking = 0.5 * (tracking + remote_tracking) + mean_grad - previous
         previous = mean_grad
+        tracking = lax.optimization_barrier(tracking)
+        if iteration + 1 < step_count:
+            remote_tracking = shifted(tracking, "replica", 2 ** ((iteration + 1) % span_bits))
+        if iteration > 0:
+            weights, _ = lax.optimization_barrier((weights, tracking))
+            remote_weights = mixed(weights, "replica", 2 ** (iteration % span_bits))
         moment_one = BETA_ONE * moment_one + (1.0 - BETA_ONE) * tracking
         moment_two = BETA_TWO * moment_two + (1.0 - BETA_TWO) * tracking * tracking
-        weights = weights - LEARNING_RATE * moment_one / (jnp.sqrt(moment_two) + EPSILON)
+        update = LEARNING_RATE * moment_one / (jnp.sqrt(moment_two) + EPSILON)
+        weights = 0.5 * (weights + remote_weights) - update
+        if iteration + 1 < step_count:
+            remote_tracking, weights = lax.optimization_barrier((remote_tracking, weights))
     change = (weights - initial) / LEARNING_RATE
     return (change[None], moment_one[None], moment_two[None])
 

time: 75.3 us -> 70.4 us (0.935)
  waiting for transfers between devices: 54.8 us -> 50.1 us
    ppermute x4, waiting for transfers between devices: 26.5 us -> 23.9 us  [swapped(): return lax.ppermute(value, axis, pairs)]
    ppermute x8, waiting for transfers between devices: 28.3 us -> 26.2 us  [shifted(): return lax.ppermute(value, axis, pairs)]
    broadcast_in_dim x3 -> x1, other arithmetic: 2.91 us -> 1.21 us  [per_device(): return (change[None], moment_one[None], moment_two[None])]
    sub x1 -> x4, other arithmetic: 0.15 us -> 1.66 us  [per_device(): tracking = 0.5 * (tracking + remote_tracking) + mean_grad - previous]
    ppermute x4, starting transfers between devices: 2.83 us -> 1.85 us  [swapped(): return lax.ppermute(value, axis, pairs)]
    ppermute x8, starting transfers between devices: 9.31 us -> 10.3 us  [shifted(): return lax.ppermute(value, axis, pairs)]
  transfers between devices with their start and end apart: 12 -> 12, of which waited for: 7 -> 8; matrix products, arithmetic and copies ran while one was open for 6% -> 5% of each run, Pallas kernels for 0% -> 0%
where the time goes in v2:
time: 70.4 us; the launch traced here: 70.1 us
  waiting for transfers between devices  50.1 us (71%)
  starting transfers between devices  12.1 us (17%)
  other arithmetic  5.63 us (8%)
  local copies, waits for them, and re-layouts  1.42 us (2%)
  between operations  0.76 us (1%)
    ppermute x8, waiting for transfers between devices, shifted(): return lax.ppermute(value, axis, pairs)  26.2 us
    ppermute x4, waiting for transfers between devices, swapped(): return lax.ppermute(value, axis, pairs)  23.9 us
    ppermute x8, starting transfers between devices, shifted(): return lax.ppermute(value, axis, pairs)  10.3 us
    sub x3, other arithmetic, per_device(): weights = 0.5 * (weights + remote_weights) - update  1.93 us
    ppermute x4, starting transfers between devices, swapped(): return lax.ppermute(value, axis, pairs)  1.85 us
    sub x4, other arithmetic, per_device(): tracking = 0.5 * (tracking + remote_tracking) + mean_grad - previous  1.66 us
  transfers between devices with their start and end apart: 12, of which 8 were waited for; matrix products, arithmetic and copies ran while one was open for 5% of the time, Pallas kernels for 0%

profile of v2, /device:TPU:0, one launch (start us, length us, event | category | flops | bytes accessed | tf_op | source)
XLA Modules:
  0.0 70.1 jit_solution(15112423178535346195)
XLA Ops:
  0.6 0.0 copy-start.2
  0.7 1.4 %fusion.17 = (bf16[1,1,1,32,5120]{4,3,2,1,0:T(8,128)(2,1)S(1)}, bf16[1,1,1,32,5120]{4,3,2,1,0:T(8,128)(2,1)S(1)}, bf16[1,1,1,32,5120]{4,3,2,1,0:T(8,128)(2,1)S(1)}, bf16[1,1,1,32,5120]{4,3,2,1,0:T(8,128)(2,1)S(1)}) fusion(bf16[4,1,1,32,5120]{4,3,2,1,0:T(8,128)(2,1)} %param.11), kind=kLoop, calls=%fused_computation.39 | loop fusion | bytes 2621440 | tf_op jit(solution)/shard_map/slice | solution.py:52
  2.1 0.0 copy-start
  2.1 0.0 copy-start.1
  2.1 0.8 %bitcast_convert_fusion.3 = f32[1,16,5120]{2,1,0:T(8,128)} fusion(bf16[1,1,1,32,5120]{4,3,2,1,0:T(8,128)(2,1)S(1)} %get-tuple-element.26, s32[]{:T(128)S(6)} %select_n.27), kind=kLoop, calls=%fused_computation.36 | loop fusion | flops 81920 | bytes 491524 | tf_op jit(solution)/shard_map/convert_element_type | solution.py:30
  2.9 2.9 %collective-permute-start.1 = (f32[1,16,5120]{2,1,0:T(8,128)}, f32[1,16,5120]{2,1,0:T(8,128)S(1)}, u32[]{:S(2)}, u32[]{:S(2)}) collective-permute-start(f32[1,16,5120]{2,1,0:T(8,128)} %bitcast_convert_fusion.3), channel_id=1, source_target_pairs={{0,1},{1,0},{2,3},{3,2},{4,5},{5,4},{6,7},{7,6},{8,9},{9,8},{10,11... | collective-permute-start | bytes 983048 | tf_op jit(solution)/shard_map/ppermute | solution.py:15
  5.8 0.0 collective-permute-start
  5.8 0.0 copy-done.2
  5.8 1.6 %collective-permute-start.3 = (f32[16,5120]{1,0:T(8,128)S(1)}, f32[16,5120]{1,0:T(8,128)}, u32[]{:S(2)}, u32[]{:S(2)}) collective-permute-start(f32[16,5120]{1,0:T(8,128)S(1)} %bitcast.84), channel_id=1, source_target_pairs={{0,2},{2,0},{4,6},{6,4},{8,10},{10,8},{12,14},{14,12},{16,18},{18,... | collective-permute-start | bytes 983048 | tf_op jit(solution)/shard_map/ppermute | solution.py:21
  7.5 0.6 collective-permute-start.4
  8.1 6.5 %collective-permute-done.1 = f32[1,16,5120]{2,1,0:T(8,128)S(1)} collective-permute-done((f32[1,16,5120]{2,1,0:T(8,128)}, f32[1,16,5120]{2,1,0:T(8,128)S(1)}, u32[]{:S(2)}, u32[]{:S(2)}) %collective-permute-start.1) | collective-permute-done | bytes 327712 | tf_op jit(solution)/shard_map/ppermute | solution.py:15
  14.5 0.8 %collective-permute-done = f32[16,5120]{1,0:T(8,128)} collective-permute-done((f32[16,5120]{1,0:T(8,128)}, f32[16,5120]{1,0:T(8,128)}, u32[]{:S(2)}, u32[]{:S(2)}) %collective-permute-start) | collective-permute-done | bytes 327712 | tf_op jit(solution)/shard_map/ppermute | solution.py:15
  15.3 1.2 %bitcast_subtract_fusion = f32[16,5120]{1,0:T(8,128)S(1)} fusion(f32[1,16,5120]{2,1,0:T(8,128)} %param.8, f32[16,5120]{1,0:T(8,128)} %collective-permute-done, f32[1,16,5120]{2,1,0:T(8,128)S(1)} %collective-permute-done.1, bf16[1,1,1,32,5120]{4,3,2,1,0:T(8,128)(2,1)S(1)} %get-tuple-element.26, s32[]{:T(128)S(6)} %select_n.25, f32[1,16,5120]{2,1,0:T(8,128)} %param.7), kind=kLoop, calls=%fused_computation.23 | loop fusion | flops 573440 | bytes 1802244 | tf_op jit(solution)/shard_map/sub | solution.py:56
  16.6 1.4 %collective-permute-start.2 = (f32[16,5120]{1,0:T(8,128)S(1)}, f32[16,5120]{1,0:T(8,128)S(1)}, u32[]{:S(2)}, u32[]{:S(2)}) collective-permute-start(f32[16,5120]{1,0:T(8,128)S(1)} %bitcast_subtract_fusion), channel_id=1, source_target_pairs={{0,4},{2,6},{4,8},{6,10},{8,12},{10,14},{12,16},{14,18},{16,20},{1... | collective-permute-start | bytes 983048 | tf_op jit(solution)/shard_map/ppermute | solution.py:15
  17.9 0.0 collective-permute-done.3
  17.9 0.0 copy-done
  17.9 0.0 copy-done.1
  17.9 1.2 %divide_subtract_fusion.2 = f32[16,5120]{1,0:T(8,128)S(1)} fusion(f32[16,5120]{1,0:T(8,128)} %collective-permute-done.3, f32[1,16,5120]{2,1,0:T(8,128)S(1)} %copy-done.2, f32[16,5120]{1,0:T(8,128)S(1)} %bitcast_subtract_fusion, f32[1,16,5120]{2,1,0:T(8,128)S(1)} %copy-done, f32[1,16,5120]{2,1,0:T(8,128)S(1)} %copy-done.1), kind=kLoop, calls=%fused_computation.32 | loop fusion | flops 1064960 | bytes 1966080 | tf_op jit(solution)/shard_map/sub | solution.py:67
  19.2 7.6 %collective-permute-done.2 = f32[16,5120]{1,0:T(8,128)S(1)} collective-permute-done((f32[16,5120]{1,0:T(8,128)S(1)}, f32[16,5120]{1,0:T(8,128)S(1)}, u32[]{:S(2)}, u32[]{:S(2)}) %collective-permute-start.2) | collective-permute-done | bytes 327712 | tf_op jit(solution)/shard_map/ppermute | solution.py:15
  26.8 0.0 collective-permute-done.4
  26.8 0.1 add_subtract_fusion.1
  26.9 0.1 collective-permute-start.6
  27.0 1.5 %collective-permute-start.7 = (f32[1,16,5120]{2,1,0:T(8,128)S(1)}, f32[1,16,5120]{2,1,0:T(8,128)S(1)}, u32[]{:S(2)}, u32[]{:S(2)}) collective-permute-start(f32[1,16,5120]{2,1,0:T(8,128)S(1)} %bitcast_convert_fusion.1), channel_id=1, source_target_pairs={{0,1},{1,0},{2,3},{3,2},{4,5},{5,4},{6,7},{7,6},{8,9},{9,8},{10,11... | collective-permute-start | bytes 983048 | tf_op jit(solution)/shard_map/ppermute | solution.py:15
  28.5 0.5 collective-permute-start.5
  29.0 5.1 %collective-permute-done.6 = f32[16,5120]{1,0:T(8,128)S(1)} collective-permute-done((f32[16,5120]{1,0:T(8,128)S(1)}, f32[16,5120]{1,0:T(8,128)S(1)}, u32[]{:S(2)}, u32[]{:S(2)}) %collective-permute-start.6) | collective-permute-done | bytes 327712 | tf_op jit(solution)/shard_map/ppermute | solution.py:21
  34.0 0.3 divide_subtract_fusion.1
  34.4 6.0 %collective-permute-done.5 = f32[16,5120]{1,0:T(8,128)S(1)} collective-permute-done((f32[16,5120]{1,0:T(8,128)S(1)}, f32[16,5120]{1,0:T(8,128)S(1)}, u32[]{:S(2)}, u32[]{:S(2)}) %collective-permute-start.5) | collective-permute-done | bytes 327712 | tf_op jit(solution)/shard_map/ppermute | solution.py:15
  40.3 0.0 collective-permute-done.7
  40.3 0.1 add_subtract_fusion
  40.5 0.1 collective-permute-start.9
  40.6 0.7 %collective-permute-start.10 = (f32[1,16,5120]{2,1,0:T(8,128)S(1)}, f32[1,16,5120]{2,1,0:T(8,128)S(1)}, u32[]{:S(2)}, u32[]{:S(2)}) collective-permute-start(f32[1,16,5120]{2,1,0:T(8,128)S(1)} %bitcast_convert_fusion), channel_id=1, source_target_pairs={{0,1},{1,0},{2,3},{3,2},{4,5},{5,4},{6,7},{7,6},{8,9},{9,8},{10,11... | collective-permute-start | bytes 983048 | tf_op jit(solution)/shard_map/ppermute | solution.py:15
  41.3 2.6 %collective-permute-start.8 = (f32[16,5120]{1,0:T(8,128)S(1)}, f32[16,5120]{1,0:T(8,128)S(1)}, u32[]{:S(2)}, u32[]{:S(2)}) collective-permute-start(f32[16,5120]{1,0:T(8,128)S(1)} %add_subtract_fusion), channel_id=1, source_target_pairs={{0,16},{2,18},{4,20},{6,22},{8,24},{10,26},{12,28},{14,30},{16,0},... | collective-permute-start | bytes 983048 | tf_op jit(solution)/shard_map/ppermute | solution.py:15
  44.0 7.4 %collective-permute-done.9 = f32[16,5120]{1,0:T(8,128)S(1)} collective-permute-done((f32[16,5120]{1,0:T(8,128)S(1)}, f32[16,5120]{1,0:T(8,128)S(1)}, u32[]{:S(2)}, u32[]{:S(2)}) %collective-permute-start.9) | collective-permute-done | bytes 327712 | tf_op jit(solution)/shard_map/ppermute | solution.py:21
  51.4 0.4 divide_subtract_fusion
  51.7 5.4 %collective-permute-done.8 = f32[16,5120]{1,0:T(8,128)S(1)} collective-permute-done((f32[16,5120]{1,0:T(8,128)S(1)}, f32[16,5120]{1,0:T(8,128)S(1)}, u32[]{:S(2)}, u32[]{:S(2)}) %collective-permute-start.8) | collective-permute-done | bytes 327712 | tf_op jit(solution)/shard_map/ppermute | solution.py:15
  57.2 0.0 collective-permute-done.10
  57.2 0.1 fusion.7
  57.3 0.1 collective-permute-start.11
  57.4 11.5 %collective-permute-done.11 = f32[16,5120]{1,0:T(8,128)S(1)} collective-permute-done((f32[16,5120]{1,0:T(8,128)S(1)}, f32[16,5120]{1,0:T(8,128)S(1)}, u32[]{:S(2)}, u32[]{:S(2)}) %collective-permute-start.11) | collective-permute-done | bytes 327712 | tf_op jit(solution)/shard_map/ppermute | solution.py:21
  68.9 1.2 %fusion.15 = (f32[1,16,5120]{2,1,0:T(8,128)}, f32[1,16,5120]{2,1,0:T(8,128)}, f32[1,16,5120]{2,1,0:T(8,128)}) fusion(f32[16,5120]{1,0:T(8,128)S(1)} %fusion.7, f32[16,5120]{1,0:T(8,128)S(1)} %get-tuple-element.23, f32[1,16,5120]{2,1,0:T(8,128)S(1)} %copy-done.2, f32[16,5120]{1,0:T(8,128)S(1)} %get-tuple-element.22, f32[16,5120]{1,0:T(8,128)S(1)} %get-tuple-element.20, ...), kind=kLoop, calls=%fused_computation.38 | loop fusion | flops 1228800 | bytes 2949120 | tf_op jit(solution)/shard_map/broadcast_in_dim | solution.py:71
  (3 shorter events, 0.1 us)
Async XLA Ops:
  0.6 5.2 %copy-start.2 = (f32[1,16,5120]{2,1,0:T(8,128)S(1)}, f32[1,16,5120]{2,1,0:T(8,128)}, u32[]{:S(2)}) copy-start(f32[1,16,5120]{2,1,0:T(8,128)} %param.6) | copy-start | bytes 983044
  2.1 15.9 %copy-start = (f32[1,16,5120]{2,1,0:T(8,128)S(1)}, f32[1,16,5120]{2,1,0:T(8,128)}, u32[]{:S(2)}) copy-start(f32[1,16,5120]{2,1,0:T(8,128)} %param.9) | copy-start | bytes 983044
  2.1 15.9 %copy-start.1 = (f32[1,16,5120]{2,1,0:T(8,128)S(1)}, f32[1,16,5120]{2,1,0:T(8,128)}, u32[]{:S(2)}) copy-start(f32[1,16,5120]{2,1,0:T(8,128)} %param.10) | copy-start | bytes 983044
  2.9 11.7 %collective-permute-start.1 = (f32[1,16,5120]{2,1,0:T(8,128)}, f32[1,16,5120]{2,1,0:T(8,128)S(1)}, u32[]{:S(2)}, u32[]{:S(2)}) collective-permute-start(f32[1,16,5120]{2,1,0:T(8,128)} %bitcast_convert_fusion.3), channel_id=1, source_target_pairs={{0,1},{1,0},{2,3},{3,2},{4,5},{5,4},{6,7},{7,6},{8,9},{9,8},{10,11... | collective-permute-start | bytes 983048 | tf_op jit(solution)/shard_map/ppermute | solution.py:15
  5.8 9.5 %collective-permute-start = (f32[16,5120]{1,0:T(8,128)}, f32[16,5120]{1,0:T(8,128)}, u32[]{:S(2)}, u32[]{:S(2)}) collective-permute-start(f32[16,5120]{1,0:T(8,128)} %bitcast), channel_id=1, source_target_pairs={{0,2},{2,4},{4,6},{6,8},{8,10},{10,12},{12,14},{14,16},{16,18},{18... | collective-permute-start | bytes 983048 | tf_op jit(solution)/shard_map/ppermute | solution.py:15
  5.8 12.1 %collective-permute-start.3 = (f32[16,5120]{1,0:T(8,128)S(1)}, f32[16,5120]{1,0:T(8,128)}, u32[]{:S(2)}, u32[]{:S(2)}) collective-permute-start(f32[16,5120]{1,0:T(8,128)S(1)} %bitcast.84), channel_id=1, source_target_pairs={{0,2},{2,0},{4,6},{6,4},{8,10},{10,8},{12,14},{14,12},{16,18},{18,... | collective-permute-start | bytes 983048 | tf_op jit(solution)/shard_map/ppermute | solution.py:21
  7.5 19.3 %collective-permute-start.4 = (f32[1,16,5120]{2,1,0:T(8,128)S(1)}, f32[1,16,5120]{2,1,0:T(8,128)S(1)}, u32[]{:S(2)}, u32[]{:S(2)}) collective-permute-start(f32[1,16,5120]{2,1,0:T(8,128)S(1)} %bitcast_convert_fusion.2), channel_id=1, source_target_pairs={{0,1},{1,0},{2,3},{3,2},{4,5},{5,4},{6,7},{7,6},{8,9},{9,8},{10,11... | collective-permute-start | bytes 983048 | tf_op jit(solution)/shard_map/ppermute | solution.py:15
  16.6 10.2 %collective-permute-start.2 = (f32[16,5120]{1,0:T(8,128)S(1)}, f32[16,5120]{1,0:T(8,128)S(1)}, u32[]{:S(2)}, u32[]{:S(2)}) collective-permute-start(f32[16,5120]{1,0:T(8,128)S(1)} %bitcast_subtract_fusion), channel_id=1, source_target_pairs={{0,4},{2,6},{4,8},{6,10},{8,12},{10,14},{12,16},{14,18},{16,20},{1... | collective-permute-start | bytes 983048 | tf_op jit(solution)/shard_map/ppermute | solution.py:15
  26.9 7.1 %collective-permute-start.6 = (f32[16,5120]{1,0:T(8,128)S(1)}, f32[16,5120]{1,0:T(8,128)S(1)}, u32[]{:S(2)}, u32[]{:S(2)}) collective-permute-start(f32[16,5120]{1,0:T(8,128)S(1)} %divide_subtract_fusion.2), channel_id=1, source_target_pairs={{0,4},{2,6},{4,0},{6,2},{8,12},{10,14},{12,8},{14,10},{16,20},{18,... | collective-permute-start | bytes 983048 | tf_op jit(solution)/shard_map/ppermute | solution.py:21
  27.0 13.3 %collective-permute-start.7 = (f32[1,16,5120]{2,1,0:T(8,128)S(1)}, f32[1,16,5120]{2,1,0:T(8,128)S(1)}, u32[]{:S(2)}, u32[]{:S(2)}) collective-permute-start(f32[1,16,5120]{2,1,0:T(8,128)S(1)} %bitcast_convert_fusion.1), channel_id=1, source_target_pairs={{0,1},{1,0},{2,3},{3,2},{4,5},{5,4},{6,7},{7,6},{8,9},{9,8},{10,11... | collective-permute-start | bytes 983048 | tf_op jit(solution)/shard_map/ppermute | solution.py:15
  28.5 11.8 %collective-permute-start.5 = (f32[16,5120]{1,0:T(8,128)S(1)}, f32[16,5120]{1,0:T(8,128)S(1)}, u32[]{:S(2)}, u32[]{:S(2)}) collective-permute-start(f32[16,5120]{1,0:T(8,128)S(1)} %add_subtract_fusion.1), channel_id=1, source_target_pairs={{0,8},{2,10},{4,12},{6,14},{8,16},{10,18},{12,20},{14,22},{16,24},... | collective-permute-start | bytes 983048 | tf_op jit(solution)/shard_map/ppermute | solution.py:15
  40.5 10.9 %collective-permute-start.9 = (f32[16,5120]{1,0:T(8,128)S(1)}, f32[16,5120]{1,0:T(8,128)S(1)}, u32[]{:S(2)}, u32[]{:S(2)}) collective-permute-start(f32[16,5120]{1,0:T(8,128)S(1)} %divide_subtract_fusion.1), channel_id=1, source_target_pairs={{0,8},{2,10},{4,12},{6,14},{8,0},{10,2},{12,4},{14,6},{16,24},{18,... | collective-permute-start | bytes 983048 | tf_op jit(solution)/shard_map/ppermute | solution.py:21
  40.6 16.6 %collective-permute-start.10 = (f32[1,16,5120]{2,1,0:T(8,128)S(1)}, f32[1,16,5120]{2,1,0:T(8,128)S(1)}, u32[]{:S(2)}, u32[]{:S(2)}) collective-permute-start(f32[1,16,5120]{2,1,0:T(8,128)S(1)} %bitcast_convert_fusion), channel_id=1, source_target_pairs={{0,1},{1,0},{2,3},{3,2},{4,5},{5,4},{6,7},{7,6},{8,9},{9,8},{10,11... | collective-permute-start | bytes 983048 | tf_op jit(solution)/shard_map/ppermute | solution.py:15
  41.3 15.8 %collective-permute-start.8 = (f32[16,5120]{1,0:T(8,128)S(1)}, f32[16,5120]{1,0:T(8,128)S(1)}, u32[]{:S(2)}, u32[]{:S(2)}) collective-permute-start(f32[16,5120]{1,0:T(8,128)S(1)} %add_subtract_fusion), channel_id=1, source_target_pairs={{0,16},{2,18},{4,20},{6,22},{8,24},{10,26},{12,28},{14,30},{16,0},... | collective-permute-start | bytes 983048 | tf_op jit(solution)/shard_map/ppermute | solution.py:15
  57.3 11.6 %collective-permute-start.11 = (f32[16,5120]{1,0:T(8,128)S(1)}, f32[16,5120]{1,0:T(8,128)S(1)}, u32[]{:S(2)}, u32[]{:S(2)}) collective-permute-start(f32[16,5120]{1,0:T(8,128)S(1)} %get-tuple-element.20), channel_id=1, source_target_pairs={{0,16},{2,18},{4,20},{6,22},{8,24},{10,26},{12,28},{14,30},{16,0},... | collective-permute-start | bytes 983048 | tf_op jit(solution)/shard_map/ppermute | solution.py:21

commit v3 on v1

v3 whole, which is shorter than its diff:
```python
import jax
import jax.numpy as jnp
from jax import lax
from jax.sharding import PartitionSpec as P

LEARNING_RATE = 0.001
BETA_ONE = 0.9
BETA_TWO = 0.999
EPSILON = 1e-08
PART = 8


def shifted(value, axis, steps):
    count = lax.axis_size(axis)
    pairs = [(source, (source + steps) % count) for source in range(count)]
    return lax.ppermute(value, axis, pairs)


def swapped(value, axis, distance):
    count = lax.axis_size(axis)
    pairs = [(source, source ^ distance) for source in range(count)]
    return lax.ppermute(value, axis, pairs)


def after(value, *others):
    return lax.optimization_barrier((value, *others))[0]


def per_device(params, tracker, last_grad, first_moment, second_moment, local_grads):
    initial = params[0]
    rows, columns = initial.shape
    replicas = lax.axis_size("replica")
    span_bits = replicas.bit_length() - 1
    fsdp = lax.axis_size("fsdp")
    place = lax.axis_index("fsdp")
    inverse_count = 1.0 / fsdp
    step_count = local_grads.shape[0]
    whole_span = step_count == span_bits and replicas == 2**span_bits
    mixed = swapped if whole_span else shifted
    size = PART if rows % PART == 0 else rows
    firsts = range(0, rows, size)
    parts = range(len(firsts))
    split = lambda whole: [whole[first : first + size] for first in firsts]

    def gradient_rows(step, keeper, first, count):
        begin = (step, 0, 0, keeper * rows + first, 0)
        return lax.dynamic_slice(local_grads, begin, (1, 1, 1, count, columns))[0, 0, 0].astype(jnp.float32)

    def received(step, first, count, *needed):
        pieces = []
        for distance in range(1, fsdp):
            outgoing = gradient_rows(step, (place + distance) % fsdp, first, count)
            if needed:
                outgoing = after(outgoing, *needed)
            pieces.append(shifted(outgoing, "fsdp", distance))
        return sum(pieces)

    remote_tracking = split(shifted(tracker[0], "replica", 1))
    remote_grads = [[received(0, first, size) for first in firsts]]
    remote_grads.append(split(received(1, 0, rows)))
    weights = initial
    remote_weights = mixed(weights, "replica", 1)
    tracking = split(tracker[0])
    previous = split(last_grad[0])
    moment_one = split(first_moment[0])
    moment_two = split(second_moment[0])
    order = ()
    for step in range(step_count):
        last = step + 1 == step_count
        for part in parts:
            own = gradient_rows(step, place, firsts[part], size)
            mean_grad = (own + remote_grads[step][part]) * inverse_count
            known = after(remote_tracking[part], *order)
            tracking[part] = 0.5 * (tracking[part] + known) + mean_grad - previous[part]
            previous[part] = mean_grad
            tracking[part] = lax.optimization_barrier(tracking[part])
            order = (tracking[part],)
        if not last:
            for part in parts:
                remote_tracking[part] = shifted(tracking[part], "replica", 2 ** ((step + 1) % span_bits))
        update = []
        settled = [after(tracking[part], tracking[-1]) for part in parts]
        for part in parts:
            moment_one[part] = BETA_ONE * moment_one[part] + (1.0 - BETA_ONE) * settled[part]
            moment_two[part] = BETA_TWO * moment_two[part] + (1.0 - BETA_TWO) * settled[part] * settled[part]
            update.append(LEARNING_RATE * moment_one[part] / (jnp.sqrt(moment_two[part]) + EPSILON))
        update = jnp.concatenate(update, 0)
        if step > 0:
            weights = after(weights, tracking[-1])
            remote_weights = mixed(weights, "replica", 2 ** (step % span_bits))
        if step + 2 < step_count:
            remote_grads.append(split(received(step + 2, 0, rows, tracking[-1])))
        if last:
            settled_weights = 0.5 * weights - update - initial
            settled_weights = lax.optimization_barrier(settled_weights)
            change = (settled_weights + 0.5 * remote_weights) / LEARNING_RATE
        else:
            update = lax.optimization_barrier(update)
            order = (update,)
            weights = 0.5 * (weights + remote_weights) - update
            if step == 0:
                weights = lax.optimization_barrier(weights)
                order = (weights,)
            else:
                remote_tracking[-1], weights = lax.optimization_barrier((remote_tracking[-1], weights))
    return (change[None], jnp.concatenate(moment_one, 0)[None], jnp.concatenate(moment_two, 0)[None])


def solution(mesh):
    in_specs = (
        P("replica", "fsdp", None),
        P("replica", "fsdp", None),
        P("replica", "fsdp", None),
        P("replica", "fsdp", None),
        P("replica", "fsdp", None),
        P(None, "replica", "fsdp", None, None),
    )
    out_specs = (P("replica", "fsdp", None), P("replica", "fsdp", None), P("replica", "fsdp", None))
    return jax.shard_map(
        per_device, mesh=mesh, in_specs=in_specs, out_specs=out_specs, check_vma=False
    )
```

time: 75.3 us -> 66.3 us (0.88)
  waiting for transfers between devices: 54.8 us -> 40.5 us
  starting transfers between devices: 12.1 us -> 15.5 us
  other arithmetic: 6.08 us -> 8.32 us
    ppermute x4, waiting for transfers between devices: 26.5 us -> 17.5 us  [swapped(): return lax.ppermute(value, axis, pairs)]
    ppermute x8 -> x12, waiting for transfers between devices: 28.3 us -> 22.9 us  [shifted(): return lax.ppermute(value, axis, pairs)]
    ppermute x8 -> x12, starting transfers between devices: 9.31 us -> 12.9 us  [shifted(): return lax.ppermute(value, axis, pairs)]
    convert_element_type x4 -> x2, other arithmetic: 0.82 us -> 3.76 us  [gradient_rows(): lax.dynamic_slice(local_grads, begin, (1, 1, 1, count, columns))[0, 0, 0]]
    slice x1, local copies, waits for them, and re-layouts: 1.44 us -> 0.02 us  [per_device(): split = lambda whole: [whole[first:first + size] for first in firsts]]
    broadcast_in_dim x3 -> x2, other arithmetic: 2.91 us -> 1.65 us  [the longest x1 0.88 us: per_device(): jnp.concatenate(moment_one, 0)[None]]
    div x0 -> x4, other arithmetic: none -> 1.11 us  [per_device(): LEARNING_RATE * moment_one[part] / (jnp.sqrt(moment_two[part]) + EPSILON)]
    unnamed x6 -> x16, local copies, waits for them, and re-layouts: 0.01 us -> 0.89 us
  transfers between devices with their start and end apart: 12 -> 16, of which waited for: 7 -> 7; matrix products, arithmetic and copies ran while one was open for 6% -> 9% of each run, Pallas kernels for 0% -> 0%
where the time goes in v3:
time: 66.3 us; the launch traced here: 66.1 us
  waiting for transfers between devices  40.5 us (61%)
  starting transfers between devices  15.5 us (23%)
  other arithmetic  8.32 us (13%)
  local copies, waits for them, and re-layouts  0.91 us (1%)
  between operations  0.9 us (1%)
    ppermute x12, waiting for transfers between devices, shifted(): return lax.ppermute(value, axis, pairs)  22.9 us
    ppermute x4, waiting for transfers between devices, swapped(): return lax.ppermute(value, axis, pairs)  17.5 us
    ppermute x12, starting transfers between devices, shifted(): return lax.ppermute(value, axis, pairs)  12.9 us
    convert_element_type x2, other arithmetic, gradient_rows(): lax.dynamic_slice(local_grads, begin, (1, 1, 1, count, columns))[0, 0, 0]  3.76 us
    ppermute x4, starting transfers between devices, swapped(): return lax.ppermute(value, axis, pairs)  2.55 us
    sub x8, other arithmetic, per_device(): tracking[part] = 0.5 * (tracking[part] + known) + mean_grad - previous[part]  1.48 us
  transfers between devices with their start and end apart: 16, of which 7 were waited for; matrix products, arithmetic and copies ran while one was open for 9% of the time, Pallas kernels for 0%

profile of v3, /device:TPU:0, one launch (start us, length us, event | category | flops | bytes accessed | tf_op | source)
XLA Modules:
  0.0 66.1 jit_solution(8793530061513870949)
XLA Ops:
  0.7 0.0 copy-start.1
  0.7 1.7 %bitcast_convert_fusion.3 = (f32[8,5120]{1,0:T(8,128)S(1)}, f32[8,5120]{1,0:T(8,128)}) fusion(bf16[4,1,1,32,5120]{4,3,2,1,0:T(8,128)(2,1)} %param.11, s32[]{:T(128)S(6)} %select_n.40, s32[]{:T(128)S(6)} %select_n.38), kind=kLoop, calls=%fused_computation.78 | loop fusion | flops 81920 | bytes 491528 | tf_op jit(solution)/shard_map/convert_element_type | solution.py:47
  2.4 2.9 %collective-permute-start.1 = (f32[8,5120]{1,0:T(8,128)}, f32[8,5120]{1,0:T(8,128)S(1)}, u32[]{:S(2)}, u32[]{:S(2)}) collective-permute-start(f32[8,5120]{1,0:T(8,128)} %get-tuple-element.65), channel_id=1, source_target_pairs={{0,1},{1,0},{2,3},{3,2},{4,5},{5,4},{6,7},{7,6},{8,9},{9,8},{10,11... | collective-permute-start | bytes 491528 | tf_op jit(solution)/shard_map/ppermute | solution.py:16
  5.3 0.0 collective-permute-start.2
  5.4 1.9 %collective-permute-start.5 = (f32[16,5120]{1,0:T(8,128)}, f32[16,5120]{1,0:T(8,128)S(1)}, u32[]{:S(2)}, u32[]{:S(2)}) collective-permute-start(f32[16,5120]{1,0:T(8,128)} %bitcast.111), channel_id=1, source_target_pairs={{0,2},{2,0},{4,6},{6,4},{8,10},{10,8},{12,14},{14,12},{16,18},{18,... | collective-permute-start | bytes 983048 | tf_op jit(solution)/shard_map/ppermute | solution.py:22
  7.2 2.0 %bitcast_convert_fusion.1 = (f32[16,5120]{1,0:T(8,128)}, f32[16,5120]{1,0:T(8,128)}, f32[16,5120]{1,0:T(8,128)}) fusion(bf16[4,1,1,32,5120]{4,3,2,1,0:T(8,128)(2,1)} %param.11, s32[]{:T(128)S(6)} %select_n.38), kind=kLoop, calls=%fused_computation.44 | loop fusion | flops 245760 | bytes 1474564 | tf_op jit(solution)/shard_map/convert_element_type | solution.py:47
  9.3 1.5 %collective-permute-start.6 = (f32[16,5120]{1,0:T(8,128)}, f32[16,5120]{1,0:T(8,128)S(1)}, u32[]{:S(2)}, u32[]{:S(2)}) collective-permute-start(f32[16,5120]{1,0:T(8,128)} %get-tuple-element.62), channel_id=1, source_target_pairs={{0,1},{1,0},{2,3},{3,2},{4,5},{5,4},{6,7},{7,6},{8,9},{9,8},{10,11... | collective-permute-start | bytes 983048 | tf_op jit(solution)/shard_map/ppermute | solution.py:16
  10.8 4.0 %collective-permute-done = f32[16,5120]{1,0:T(8,128)S(1)} collective-permute-done((f32[16,5120]{1,0:T(8,128)}, f32[16,5120]{1,0:T(8,128)S(1)}, u32[]{:S(2)}, u32[]{:S(2)}) %collective-permute-start) | collective-permute-done | bytes 327712 | tf_op jit(solution)/shard_map/ppermute | solution.py:16
  14.8 1.1 %bitcast_subtract_fusion.1 = f32[8,5120]{1,0:T(8,128)S(1)} fusion(f32[8,5120]{1,0:T(8,128)S(1)} %get-tuple-element.75, f32[1,16,5120]{2,1,0:T(8,128)} %param.8, f32[1,16,5120]{2,1,0:T(8,128)} %param.7, f32[8,5120]{1,0:T(8,128)S(1)} %collective-permute-done.1, bf16[4,1,1,32,5120]{4,3,2,1,0:T(8,128)(2,1)S(1)} %copy-done.1, s32[]{:T(128)S(6)} %select_n.36), kind=kLoop, calls=%fused_computation.53 | loop fusion | flops 286720 | bytes 901124 | tf_op jit(solution)/shard_map/sub | solution.py:74
  15.8 0.0 copy-start.2
  15.9 0.1 bitcast_subtract_fusion
  15.9 0.1 collective-permute-start.4
  16.0 1.2 %collective-permute-start.3 = (f32[8,5120]{1,0:T(8,128)S(1)}, f32[8,5120]{1,0:T(8,128)S(1)}, u32[]{:S(2)}, u32[]{:S(2)}) collective-permute-start(f32[8,5120]{1,0:T(8,128)S(1)} %bitcast_subtract_fusion), channel_id=1, source_target_pairs={{0,4},{2,6},{4,8},{6,10},{8,12},{10,14},{12,16},{14,18},{16,20},{1... | collective-permute-start | bytes 491528 | tf_op jit(solution)/shard_map/ppermute | solution.py:16
  17.2 0.2 add_divide_fusion.7
  17.5 0.0 copy-start.7
  17.5 0.0 collective-permute-done.5
  17.5 0.1 multiply_subtract_fusion.2
  17.6 0.9 %copy-done.7 = f32[16,5120]{1,0:T(8,128)S(1)} copy-done((f32[16,5120]{1,0:T(8,128)S(1)}, f32[16,5120]{1,0:T(8,128)}, u32[]{:S(2)}) %copy-start.7) | copy-done | bytes 327704
  18.4 2.0 %collective-permute-start.10 = (f32[16,5120]{1,0:T(8,128)S(1)}, f32[16,5120]{1,0:T(8,128)S(1)}, u32[]{:S(2)}, u32[]{:S(2)}) collective-permute-start(f32[16,5120]{1,0:T(8,128)S(1)} %copy-done.7), channel_id=1, source_target_pairs={{0,1},{1,0},{2,3},{3,2},{4,5},{5,4},{6,7},{7,6},{8,9},{9,8},{10,11... | collective-permute-start | bytes 983048 | tf_op jit(solution)/shard_map/ppermute | solution.py:16
  20.5 3.5 %collective-permute-done.4 = f32[8,5120]{1,0:T(8,128)S(1)} collective-permute-done((f32[8,5120]{1,0:T(8,128)S(1)}, f32[8,5120]{1,0:T(8,128)S(1)}, u32[]{:S(2)}, u32[]{:S(2)}) %collective-permute-start.4) | collective-permute-done | bytes 163872 | tf_op jit(solution)/shard_map/ppermute | solution.py:16
  24.0 0.1 add_subtract_fusion.3
  24.1 1.7 %collective-permute-done.3 = f32[8,5120]{1,0:T(8,128)S(1)} collective-permute-done((f32[8,5120]{1,0:T(8,128)S(1)}, f32[8,5120]{1,0:T(8,128)S(1)}, u32[]{:S(2)}, u32[]{:S(2)}) %collective-permute-start.3) | collective-permute-done | bytes 163872 | tf_op jit(solution)/shard_map/ppermute | solution.py:16
  25.8 0.1 add_subtract_fusion.2
  25.8 0.0 copy-start.6
  25.8 0.1 collective-permute-start.7
  25.9 1.2 %collective-permute-start.9 = (f32[8,5120]{1,0:T(8,128)S(1)}, f32[8,5120]{1,0:T(8,128)S(1)}, u32[]{:S(2)}, u32[]{:S(2)}) collective-permute-start(f32[8,5120]{1,0:T(8,128)S(1)} %add_subtract_fusion.3), channel_id=1, source_target_pairs={{0,8},{2,10},{4,12},{6,14},{8,16},{10,18},{12,20},{14,22},{16,24},... | collective-permute-start | bytes 491528 | tf_op jit(solution)/shard_map/ppermute | solution.py:16
  27.2 0.6 collective-permute-start.8
  27.8 0.3 add_divide_fusion.5
  28.1 0.8 %collective-permute-start.14 = (f32[16,5120]{1,0:T(8,128)S(1)}, f32[16,5120]{1,0:T(8,128)S(1)}, u32[]{:S(2)}, u32[]{:S(2)}) collective-permute-start(f32[16,5120]{1,0:T(8,128)S(1)} %copy-done.6), channel_id=1, source_target_pairs={{0,1},{1,0},{2,3},{3,2},{4,5},{5,4},{6,7},{7,6},{8,9},{9,8},{10,11... | collective-permute-start | bytes 983048 | tf_op jit(solution)/shard_map/ppermute | solution.py:16
  28.9 7.0 %collective-permute-done.9 = f32[8,5120]{1,0:T(8,128)S(1)} collective-permute-done((f32[8,5120]{1,0:T(8,128)S(1)}, f32[8,5120]{1,0:T(8,128)S(1)}, u32[]{:S(2)}, u32[]{:S(2)}) %collective-permute-start.9) | collective-permute-done | bytes 163872 | tf_op jit(solution)/shard_map/ppermute | solution.py:16
  35.8 0.0 collective-permute-done.10
  35.8 0.1 add_subtract_fusion.1
  35.9 0.1 collective-permute-start.13
  36.0 0.0 collective-permute-done.8
  36.0 0.1 multiply_subtract_fusion.1
  36.1 0.1 add_subtract_fusion
  36.1 3.0 %collective-permute-start.11 = (f32[8,5120]{1,0:T(8,128)S(1)}, f32[8,5120]{1,0:T(8,128)S(1)}, u32[]{:S(2)}, u32[]{:S(2)}) collective-permute-start(f32[8,5120]{1,0:T(8,128)S(1)} %add_subtract_fusion), channel_id=1, source_target_pairs={{0,16},{2,18},{4,20},{6,22},{8,24},{10,26},{12,28},{14,30},{16,0},... | collective-permute-start | bytes 491528 | tf_op jit(solution)/shard_map/ppermute | solution.py:16
  39.1 0.3 add_divide_fusion.3
  39.4 6.7 %collective-permute-done.13 = f32[8,5120]{1,0:T(8,128)S(1)} collective-permute-done((f32[8,5120]{1,0:T(8,128)S(1)}, f32[8,5120]{1,0:T(8,128)S(1)}, u32[]{:S(2)}, u32[]{:S(2)}) %collective-permute-start.13) | collective-permute-done | bytes 163872 | tf_op jit(solution)/shard_map/ppermute | solution.py:16
  46.2 0.1 fusion.14
  46.2 5.2 %collective-permute-done.12 = f32[16,5120]{1,0:T(8,128)S(1)} collective-permute-done((f32[16,5120]{1,0:T(8,128)S(1)}, f32[16,5120]{1,0:T(8,128)S(1)}, u32[]{:S(2)}, u32[]{:S(2)}) %collective-permute-start.12) | collective-permute-done | bytes 327712 | tf_op jit(solution)/shard_map/ppermute | solution.py:22
  51.4 0.1 multiply_subtract_fusion
  51.5 0.1 fusion.11
  51.5 0.1 collective-permute-start.15
  51.6 0.3 add_divide_fusion.1
  52.0 0.9 %maximum_bitcast_fusion = (f32[1,16,5120]{2,1,0:T(8,128)}, f32[1,16,5120]{2,1,0:T(8,128)}) fusion(f32[8,5120]{1,0:T(8,128)S(1)} %get-tuple-element.72, f32[8,5120]{1,0:T(8,128)S(1)} %get-tuple-element.52, f32[8,5120]{1,0:T(8,128)S(1)} %get-tuple-element.71, f32[8,5120]{1,0:T(8,128)S(1)} %get-tuple-element.53), kind=kLoop, calls=%fused_computation.5 | loop fusion | flops 163840 | bytes 1310720 | tf_op jit(solution)/shard_map/broadcast_in_dim | solution.py:106
  52.9 12.4 %collective-permute-done.15 = f32[16,5120]{1,0:T(8,128)S(1)} collective-permute-done((f32[16,5120]{1,0:T(8,128)S(1)}, f32[16,5120]{1,0:T(8,128)S(1)}, u32[]{:S(2)}, u32[]{:S(2)}) %collective-permute-start.15) | collective-permute-done | bytes 327712 | tf_op jit(solution)/shard_map/ppermute | solution.py:22
  65.3 0.8 %multiply_bitcast_fusion = f32[1,16,5120]{2,1,0:T(8,128)} fusion(f32[16,5120]{1,0:T(8,128)S(1)} %fusion, f32[16,5120]{1,0:T(8,128)S(1)} %collective-permute-done.15), kind=kLoop, calls=%fused_computation.7 | loop fusion | flops 245760 | bytes 983040 | tf_op jit(solution)/shard_map/broadcast_in_dim | solution.py:106
  (24 shorter events, 0.2 us)
Async XLA Ops:
  0.7 14.1 %copy-start.1 = (bf16[4,1,1,32,5120]{4,3,2,1,0:T(8,128)(2,1)S(1)}, bf16[4,1,1,32,5120]{4,3,2,1,0:T(8,128)(2,1)}, u32[]{:S(2)}) copy-start(bf16[4,1,1,32,5120]{4,3,2,1,0:T(8,128)(2,1)} %param.11) | copy-start | bytes 3932164
  2.4 12.4 %collective-permute-start.1 = (f32[8,5120]{1,0:T(8,128)}, f32[8,5120]{1,0:T(8,128)S(1)}, u32[]{:S(2)}, u32[]{:S(2)}) collective-permute-start(f32[8,5120]{1,0:T(8,128)} %get-tuple-element.65), channel_id=1, source_target_pairs={{0,1},{1,0},{2,3},{3,2},{4,5},{5,4},{6,7},{7,6},{8,9},{9,8},{10,11... | collective-permute-start | bytes 491528 | tf_op jit(solution)/shard_map/ppermute | solution.py:16
  5.3 9.4 %collective-permute-start = (f32[16,5120]{1,0:T(8,128)}, f32[16,5120]{1,0:T(8,128)S(1)}, u32[]{:S(2)}, u32[]{:S(2)}) collective-permute-start(f32[16,5120]{1,0:T(8,128)} %bitcast.112), channel_id=1, source_target_pairs={{0,2},{2,4},{4,6},{6,8},{8,10},{10,12},{12,14},{14,16},{16,18},{18... | collective-permute-start | bytes 983048 | tf_op jit(solution)/shard_map/ppermute | solution.py:16
  5.3 10.5 %collective-permute-start.2 = (f32[8,5120]{1,0:T(8,128)S(1)}, f32[8,5120]{1,0:T(8,128)S(1)}, u32[]{:S(2)}, u32[]{:S(2)}) collective-permute-start(f32[8,5120]{1,0:T(8,128)S(1)} %get-tuple-element.64), channel_id=1, source_target_pairs={{0,1},{1,0},{2,3},{3,2},{4,5},{5,4},{6,7},{7,6},{8,9},{9,8},{10,11... | collective-permute-start | bytes 491528 | tf_op jit(solution)/shard_map/ppermute | solution.py:16
  5.4 12.1 %collective-permute-start.5 = (f32[16,5120]{1,0:T(8,128)}, f32[16,5120]{1,0:T(8,128)S(1)}, u32[]{:S(2)}, u32[]{:S(2)}) collective-permute-start(f32[16,5120]{1,0:T(8,128)} %bitcast.111), channel_id=1, source_target_pairs={{0,2},{2,0},{4,6},{6,4},{8,10},{10,8},{12,14},{14,12},{16,18},{18,... | collective-permute-start | bytes 983048 | tf_op jit(solution)/shard_map/ppermute | solution.py:22
  9.3 8.0 %copy-start = (f32[1,16,5120]{2,1,0:T(8,128)S(1)}, f32[1,16,5120]{2,1,0:T(8,128)}, u32[]{:S(2)}) copy-start(f32[1,16,5120]{2,1,0:T(8,128)} %param.9) | copy-start | bytes 983044
  9.3 8.0 %copy-start.3 = (f32[1,16,5120]{2,1,0:T(8,128)S(1)}, f32[1,16,5120]{2,1,0:T(8,128)}, u32[]{:S(2)}) copy-start(f32[1,16,5120]{2,1,0:T(8,128)} %param.10) | copy-start | bytes 983044
  9.3 14.8 %collective-permute-start.6 = (f32[16,5120]{1,0:T(8,128)}, f32[16,5120]{1,0:T(8,128)S(1)}, u32[]{:S(2)}, u32[]{:S(2)}) collective-permute-start(f32[16,5120]{1,0:T(8,128)} %get-tuple-element.62), channel_id=1, source_target_pairs={{0,1},{1,0},{2,3},{3,2},{4,5},{5,4},{6,7},{7,6},{8,9},{9,8},{10,11... | collective-permute-start | bytes 983048 | tf_op jit(solution)/shard_map/ppermute | solution.py:16
  10.7 5.1 %copy-start.4 = (f32[1,16,5120]{2,1,0:T(8,128)S(1)}, f32[1,16,5120]{2,1,0:T(8,128)}, u32[]{:S(2)}) copy-start(f32[1,16,5120]{2,1,0:T(8,128)} %param.7) | copy-start | bytes 983044
  10.8 5.1 %copy-start.5 = (f32[1,16,5120]{2,1,0:T(8,128)S(1)}, f32[1,16,5120]{2,1,0:T(8,128)}, u32[]{:S(2)}) copy-start(f32[1,16,5120]{2,1,0:T(8,128)} %param.8) | copy-start | bytes 983044
  15.8 1.7 %copy-start.2 = (f32[1,16,5120]{2,1,0:T(8,128)S(1)}, f32[1,16,5120]{2,1,0:T(8,128)}, u32[]{:S(2)}) copy-start(f32[1,16,5120]{2,1,0:T(8,128)} %param.6) | copy-start | bytes 983044
  15.9 8.1 %collective-permute-start.4 = (f32[8,5120]{1,0:T(8,128)S(1)}, f32[8,5120]{1,0:T(8,128)S(1)}, u32[]{:S(2)}, u32[]{:S(2)}) collective-permute-start(f32[8,5120]{1,0:T(8,128)S(1)} %bitcast_subtract_fusion.1), channel_id=1, source_target_pairs={{0,4},{2,6},{4,8},{6,10},{8,12},{10,14},{12,16},{14,18},{16,20},{1... | collective-permute-start | bytes 491528 | tf_op jit(solution)/shard_map/ppermute | solution.py:16
  16.0 9.8 %collective-permute-start.3 = (f32[8,5120]{1,0:T(8,128)S(1)}, f32[8,5120]{1,0:T(8,128)S(1)}, u32[]{:S(2)}, u32[]{:S(2)}) collective-permute-start(f32[8,5120]{1,0:T(8,128)S(1)} %bitcast_subtract_fusion), channel_id=1, source_target_pairs={{0,4},{2,6},{4,8},{6,10},{8,12},{10,14},{12,16},{14,18},{16,20},{1... | collective-permute-start | bytes 491528 | tf_op jit(solution)/shard_map/ppermute | solution.py:16
  17.5 1.0 %copy-start.7 = (f32[16,5120]{1,0:T(8,128)S(1)}, f32[16,5120]{1,0:T(8,128)}, u32[]{:S(2)}) copy-start(f32[16,5120]{1,0:T(8,128)} %get-tuple-element.37) | copy-start | bytes 983044
  18.4 17.4 %collective-permute-start.10 = (f32[16,5120]{1,0:T(8,128)S(1)}, f32[16,5120]{1,0:T(8,128)S(1)}, u32[]{:S(2)}, u32[]{:S(2)}) collective-permute-start(f32[16,5120]{1,0:T(8,128)S(1)} %copy-done.7), channel_id=1, source_target_pairs={{0,1},{1,0},{2,3},{3,2},{4,5},{5,4},{6,7},{7,6},{8,9},{9,8},{10,11... | collective-permute-start | bytes 983048 | tf_op jit(solution)/shard_map/ppermute | solution.py:16
  25.8 2.3 %copy-start.6 = (f32[16,5120]{1,0:T(8,128)S(1)}, f32[16,5120]{1,0:T(8,128)}, u32[]{:S(2)}) copy-start(f32[16,5120]{1,0:T(8,128)} %get-tuple-element.46) | copy-start | bytes 983044
  25.8 10.2 %collective-permute-start.7 = (f32[8,5120]{1,0:T(8,128)S(1)}, f32[8,5120]{1,0:T(8,128)S(1)}, u32[]{:S(2)}, u32[]{:S(2)}) collective-permute-start(f32[8,5120]{1,0:T(8,128)S(1)} %add_subtract_fusion.2), channel_id=1, source_target_pairs={{0,8},{2,10},{4,12},{6,14},{8,16},{10,18},{12,20},{14,22},{16,24},... | collective-permute-start | bytes 491528 | tf_op jit(solution)/shard_map/ppermute | solution.py:16
  25.9 9.9 %collective-permute-start.9 = (f32[8,5120]{1,0:T(8,128)S(1)}, f32[8,5120]{1,0:T(8,128)S(1)}, u32[]{:S(2)}, u32[]{:S(2)}) collective-permute-start(f32[8,5120]{1,0:T(8,128)S(1)} %add_subtract_fusion.3), channel_id=1, source_target_pairs={{0,8},{2,10},{4,12},{6,14},{8,16},{10,18},{12,20},{14,22},{16,24},... | collective-permute-start | bytes 491528 | tf_op jit(solution)/shard_map/ppermute | solution.py:16
  27.2 8.8 %collective-permute-start.8 = (f32[16,5120]{1,0:T(8,128)S(1)}, f32[16,5120]{1,0:T(8,128)S(1)}, u32[]{:S(2)}, u32[]{:S(2)}) collective-permute-start(f32[16,5120]{1,0:T(8,128)S(1)} %multiply_subtract_fusion.2), channel_id=1, source_target_pairs={{0,4},{2,6},{4,0},{6,2},{8,12},{10,14},{12,8},{14,10},{16,20},{18,... | collective-permute-start | bytes 983048 | tf_op jit(solution)/shard_map/ppermute | solution.py:22
  28.1 18.1 %collective-permute-start.14 = (f32[16,5120]{1,0:T(8,128)S(1)}, f32[16,5120]{1,0:T(8,128)S(1)}, u32[]{:S(2)}, u32[]{:S(2)}) collective-permute-start(f32[16,5120]{1,0:T(8,128)S(1)} %copy-done.6), channel_id=1, source_target_pairs={{0,1},{1,0},{2,3},{3,2},{4,5},{5,4},{6,7},{7,6},{8,9},{9,8},{10,11... | collective-permute-start | bytes 983048 | tf_op jit(solution)/shard_map/ppermute | solution.py:16
  35.9 10.3 %collective-permute-start.13 = (f32[8,5120]{1,0:T(8,128)S(1)}, f32[8,5120]{1,0:T(8,128)S(1)}, u32[]{:S(2)}, u32[]{:S(2)}) collective-permute-start(f32[8,5120]{1,0:T(8,128)S(1)} %add_subtract_fusion.1), channel_id=1, source_target_pairs={{0,16},{2,18},{4,20},{6,22},{8,24},{10,26},{12,28},{14,30},{16,0},... | collective-permute-start | bytes 491528 | tf_op jit(solution)/shard_map/ppermute | solution.py:16
  36.1 15.3 %collective-permute-start.11 = (f32[8,5120]{1,0:T(8,128)S(1)}, f32[8,5120]{1,0:T(8,128)S(1)}, u32[]{:S(2)}, u32[]{:S(2)}) collective-permute-start(f32[8,5120]{1,0:T(8,128)S(1)} %add_subtract_fusion), channel_id=1, source_target_pairs={{0,16},{2,18},{4,20},{6,22},{8,24},{10,26},{12,28},{14,30},{16,0},... | collective-permute-start | bytes 491528 | tf_op jit(solution)/shard_map/ppermute | solution.py:16
  39.1 12.3 %collective-permute-start.12 = (f32[16,5120]{1,0:T(8,128)S(1)}, f32[16,5120]{1,0:T(8,128)S(1)}, u32[]{:S(2)}, u32[]{:S(2)}) collective-permute-start(f32[16,5120]{1,0:T(8,128)S(1)} %multiply_subtract_fusion.1), channel_id=1, source_target_pairs={{0,8},{2,10},{4,12},{6,14},{8,0},{10,2},{12,4},{14,6},{16,24},{18,... | collective-permute-start | bytes 983048 | tf_op jit(solution)/shard_map/ppermute | solution.py:22
  51.5 13.7 %collective-permute-start.15 = (f32[16,5120]{1,0:T(8,128)S(1)}, f32[16,5120]{1,0:T(8,128)S(1)}, u32[]{:S(2)}, u32[]{:S(2)}) collective-permute-start(f32[16,5120]{1,0:T(8,128)S(1)} %multiply_subtract_fusion), channel_id=1, source_target_pairs={{0,16},{2,18},{4,20},{6,22},{8,24},{10,26},{12,28},{14,30},{16,0},... | collective-permute-start | bytes 983048 | tf_op jit(solution)/shard_map/ppermute | solution.py:22

commit v4 on v3

v4 whole, which is shorter than its diff:
```python
import jax
import jax.numpy as jnp
from jax import lax
from jax.sharding import PartitionSpec as P

LEARNING_RATE = 0.001
BETA_ONE = 0.9
BETA_TWO = 0.999
EPSILON = 1e-08
PART = 8


def shifted(value, axis, steps):
    count = lax.axis_size(axis)
    pairs = [(source, (source + steps) % count) for source in range(count)]
    return lax.ppermute(value, axis, pairs)


def swapped(value, axis, distance):
    count = lax.axis_size(axis)
    pairs = [(source, source ^ distance) for source in range(count)]
    return lax.ppermute(value, axis, pairs)


def after(value, *others):
    return lax.optimization_barrier((value, *others))[0]


def per_device(params, tracker, last_grad, first_moment, second_moment, local_grads):
    initial = params[0]
    rows, columns = initial.shape
    replicas = lax.axis_size("replica")
    span_bits = replicas.bit_length() - 1
    fsdp = lax.axis_size("fsdp")
    place = lax.axis_index("fsdp")
    inverse_count = 1.0 / fsdp
    step_count = local_grads.shape[0]
    whole_span = step_count == span_bits and replicas == 2**span_bits
    mixed = swapped if whole_span else shifted
    size = PART if rows % PART == 0 else rows
    firsts = range(0, rows, size)
    parts = range(len(firsts))
    split = lambda whole: [whole[first : first + size] for first in firsts]

    def gradient_rows(step, keeper, first, count, *needed):
        source = after(local_grads, *needed) if needed else local_grads
        begin = (step, 0, 0, keeper * rows + first, 0)
        return lax.dynamic_slice(source, begin, (1, 1, 1, count, columns))[0, 0, 0].astype(jnp.float32)

    def received(step, first, count, *needed):
        pieces = []
        for distance in range(1, fsdp):
            outgoing = lax.optimization_barrier(gradient_rows(step, (place + distance) % fsdp, first, count, *needed))
            pieces.append(shifted(outgoing, "fsdp", distance))
        return sum(pieces) if pieces else jnp.zeros((count, columns), jnp.float32)

    remote_tracking = split(shifted(tracker[0], "replica", 1))
    remote_grads = [[received(0, first, size) for first in firsts]]
    remote_grads.append(split(received(1, 0, rows)))
    weights = initial
    remote_weights = mixed(weights, "replica", 1)
    tracking = split(tracker[0])
    previous = split(last_grad[0])
    moment_one = split(first_moment[0])
    moment_two = split(second_moment[0])
    begun = lax.optimization_barrier([0.5 * (tracking[part] + remote_tracking[part]) - previous[part] for part in parts])
    remote_grads[0] = [after(grads, *begun) for grads in remote_grads[0]]

    def moments(known):
        update = []
        for part in parts:
            moment_one[part] = BETA_ONE * moment_one[part] + (1.0 - BETA_ONE) * known[part]
            moment_two[part] = BETA_TWO * moment_two[part] + (1.0 - BETA_TWO) * known[part] * known[part]
            update.append(LEARNING_RATE * moment_one[part] / (jnp.sqrt(moment_two[part]) + EPSILON))
        return jnp.concatenate(update, 0)

    order = ()
    for step in range(step_count):
        last = step + 1 == step_count
        if last:
            weights = 0.5 * (weights + remote_weights) - moments(tracking)
            weights = lax.optimization_barrier(weights)
            remote_weights = mixed(weights, "replica", 2 ** (step % span_bits))
            order = (weights,)
        for part in parts:
            if 0 < step and part == len(parts) - 1 and not last:
                update = lax.optimization_barrier(moments([after(before[done], *order) for done in parts]))
                weights = 0.5 * (weights + after(remote_weights, *order)) - update
                weights = lax.optimization_barrier(weights)
                order = (weights, *order)
                if step + 2 == step_count:
                    remote_weights = mixed(weights, "replica", 2 ** (step % span_bits))
            own = gradient_rows(step, place, firsts[part], size)
            mean_grad = (own + remote_grads[step][part]) * inverse_count
            if step == 0:
                now = after(begun[part], *order) + mean_grad
            else:
                known = after(remote_tracking[part], *order)
                now = 0.5 * (tracking[part] + known) + mean_grad - previous[part]
            previous[part] = mean_grad
            if part == 0:
                before = list(tracking)
            tracking[part] = lax.optimization_barrier(now)
            order = (tracking[part],)
            if not last:
                remote_tracking[part] = shifted(tracking[part], "replica", 2 ** ((step + 1) % span_bits))
            if part == 0 and step + 2 < step_count:
                remote_grads.append(split(received(step + 2, 0, rows, tracking[part])))
        if 0 < step and not last and not (step + 2 == step_count):
            weights = after(weights, tracking[-1])
            remote_weights = mixed(weights, "replica", 2 ** (step % span_bits))
    update = moments(tracking)
    settled_weights = lax.optimization_barrier(0.5 * weights - update - initial)
    change = (settled_weights + 0.5 * remote_weights) / LEARNING_RATE
    return (change[None], jnp.concatenate(moment_one, 0)[None], jnp.concatenate(moment_two, 0)[None])


def solution(mesh):
    in_specs = (
        P("replica", "fsdp", None),
        P("replica", "fsdp", None),
        P("replica", "fsdp", None),
        P("replica", "fsdp", None),
        P("replica", "fsdp", None),
        P(None, "replica", "fsdp", None, None),
    )
    out_specs = (P("replica", "fsdp", None), P("replica", "fsdp", None), P("replica", "fsdp", None))
    return jax.shard_map(
        per_device, mesh=mesh, in_specs=in_specs, out_specs=out_specs, check_vma=False
    )
```

time: 66.3 us -> 61.7 us (0.931)
  waiting for transfers between devices: 40.5 us -> 37.9 us
  other arithmetic: 8.32 us -> 6.69 us
  local copies, waits for them, and re-layouts: 0.91 us -> 0.03 us
    ppermute x12, waiting for transfers between devices: 22.9 us -> 15 us  [shifted(): return lax.ppermute(value, axis, pairs)]
    ppermute x4, waiting for transfers between devices: 17.5 us -> 22.9 us  [swapped(): return lax.ppermute(value, axis, pairs)]
    convert_element_type x2 -> x4, other arithmetic: 3.76 us -> 2.04 us  [gradient_rows(): lax.dynamic_slice(source, begin, (1, 1, 1, count, columns))[0, 0, 0]]
    unnamed x16 -> x8, local copies, waits for them, and re-layouts: 0.89 us -> 0.03 us
    sub x12 -> x11, other arithmetic: 1.74 us -> 1.76 us  [the longest x1 1.2 us: per_device(): 0.5 * (tracking[part] + remote_tracking[part]) - previous[part]]
  transfers between devices with their start and end apart: 16 -> 16, of which waited for: 7 -> 8; matrix products, arithmetic and copies ran while one was open for 9% -> 8% of each run, Pallas kernels for 0% -> 0%
where the time goes in v4:
time: 61.7 us; the launch traced here: 61.4 us
  waiting for transfers between devices  37.9 us (61%)
  starting transfers between devices  15.9 us (26%)
  other arithmetic  6.69 us (11%)
  between operations  0.93 us (2%)
    ppermute x4, waiting for transfers between devices, swapped(): return lax.ppermute(value, axis, pairs)  22.9 us
    ppermute x12, waiting for transfers between devices, shifted(): return lax.ppermute(value, axis, pairs)  15 us
    ppermute x12, starting transfers between devices, shifted(): return lax.ppermute(value, axis, pairs)  13.1 us
    ppermute x4, starting transfers between devices, swapped(): return lax.ppermute(value, axis, pairs)  2.8 us
    convert_element_type x4, other arithmetic, gradient_rows(): lax.dynamic_slice(source, begin, (1, 1, 1, count, columns))[0, 0, 0]  2.04 us
  transfers between devices with their start and end apart: 16, of which 8 were waited for; matrix products, arithmetic and copies ran while one was open for 8% of the time, Pallas kernels for 0%

profile of v4, /device:TPU:0, one launch (start us, length us, event | category | flops | bytes accessed | tf_op | source)
XLA Modules:
  0.0 61.4 jit_solution(17697859404372610294)
XLA Ops:
  0.6 0.0 copy-start.1
  0.7 1.1 %bitcast_convert_fusion.3 = (f32[8,5120]{1,0:T(8,128)S(1)}, f32[8,5120]{1,0:T(8,128)S(1)}) fusion(bf16[4,1,1,32,5120]{4,3,2,1,0:T(8,128)(2,1)} %param.11, s32[]{:T(128)S(6)} %select_n.40, s32[]{:T(128)S(6)} %select_n.38), kind=kLoop, calls=%fused_computation.77 | loop fusion | flops 81920 | bytes 491528 | tf_op jit(solution)/shard_map/convert_element_type | solution.py:48
  1.7 3.0 %collective-permute-start.4 = (f32[8,5120]{1,0:T(8,128)S(1)}, f32[8,5120]{1,0:T(8,128)S(1)}, u32[]{:S(2)}, u32[]{:S(2)}) collective-permute-start(f32[8,5120]{1,0:T(8,128)S(1)} %get-tuple-element.53), channel_id=1, source_target_pairs={{0,1},{1,0},{2,3},{3,2},{4,5},{5,4},{6,7},{7,6},{8,9},{9,8},{10,11... | collective-permute-start | bytes 491528 | tf_op jit(solution)/shard_map/ppermute | solution.py:16
  4.7 0.0 collective-permute-start.1
  4.7 0.1 collective-permute-start.2
  4.9 0.9 %bitcast_convert_fusion.2 = f32[16,5120]{1,0:T(8,128)S(1)} fusion(bf16[4,1,1,32,5120]{4,3,2,1,0:T(8,128)(2,1)} %param.11, s32[]{:T(128)S(6)} %select_n.38), kind=kLoop, calls=%fused_computation.50 | loop fusion | flops 81920 | bytes 491524 | tf_op jit(solution)/shard_map/convert_element_type | solution.py:48
  5.8 1.9 %collective-permute-start.5 = (f32[16,5120]{1,0:T(8,128)S(1)}, f32[16,5120]{1,0:T(8,128)S(1)}, u32[]{:S(2)}, u32[]{:S(2)}) collective-permute-start(f32[16,5120]{1,0:T(8,128)S(1)} %bitcast_convert_fusion.2), channel_id=1, source_target_pairs={{0,1},{1,0},{2,3},{3,2},{4,5},{5,4},{6,7},{7,6},{8,9},{9,8},{10,11... | collective-permute-start | bytes 983048 | tf_op jit(solution)/shard_map/ppermute | solution.py:16
  7.8 1.1 %collective-permute-start = (f32[16,5120]{1,0:T(8,128)}, f32[16,5120]{1,0:T(8,128)S(1)}, u32[]{:S(2)}, u32[]{:S(2)}) collective-permute-start(f32[16,5120]{1,0:T(8,128)} %bitcast.99), channel_id=1, source_target_pairs={{0,2},{2,0},{4,6},{6,4},{8,10},{10,8},{12,14},{14,12},{16,18},{18,... | collective-permute-start | bytes 983048 | tf_op jit(solution)/shard_map/ppermute | solution.py:22
  8.8 5.3 %collective-permute-done.1 = f32[16,5120]{1,0:T(8,128)S(1)} collective-permute-done((f32[16,5120]{1,0:T(8,128)}, f32[16,5120]{1,0:T(8,128)S(1)}, u32[]{:S(2)}, u32[]{:S(2)}) %collective-permute-start.1) | collective-permute-done | bytes 327712 | tf_op jit(solution)/shard_map/ppermute | solution.py:16
  14.1 1.2 %fusion.20 = (f32[8,5120]{1,0:T(8,128)S(1)}, f32[8,5120]{1,0:T(8,128)S(1)}) fusion(f32[16,5120]{1,0:T(8,128)S(1)} %collective-permute-done.1, f32[1,16,5120]{2,1,0:T(8,128)} %param.8, f32[1,16,5120]{2,1,0:T(8,128)} %param.7), kind=kLoop, calls=%fused_computation.44 | loop fusion | flops 245760 | bytes 1310720 | tf_op jit(solution)/shard_map/sub | solution.py:66
  15.3 0.0 copy-start
  15.3 0.0 copy-start.3
  15.4 0.1 collective-permute-start.3
  15.5 0.0 collective-permute-done.4
  15.5 1.3 %collective-permute-start.6 = (f32[8,5120]{1,0:T(8,128)S(1)}, f32[8,5120]{1,0:T(8,128)S(1)}, u32[]{:S(2)}, u32[]{:S(2)}) collective-permute-start(f32[8,5120]{1,0:T(8,128)S(1)} %fusion.26), channel_id=1, source_target_pairs={{0,4},{2,6},{4,8},{6,10},{8,12},{10,14},{12,16},{14,18},{16,20},{1... | collective-permute-start | bytes 491528 | tf_op jit(solution)/shard_map/ppermute | solution.py:16
  16.9 0.0 copy-start.2
  16.9 1.8 %collective-permute-start.9 = (f32[16,5120]{1,0:T(8,128)S(1)}, f32[16,5120]{1,0:T(8,128)S(1)}, u32[]{:S(2)}, u32[]{:S(2)}) collective-permute-start(f32[16,5120]{1,0:T(8,128)S(1)} %bitcast_convert_fusion.1), channel_id=1, source_target_pairs={{0,1},{1,0},{2,3},{3,2},{4,5},{5,4},{6,7},{7,6},{8,9},{9,8},{10,11... | collective-permute-start | bytes 983048 | tf_op jit(solution)/shard_map/ppermute | solution.py:16
  18.6 4.8 %collective-permute-done.3 = f32[8,5120]{1,0:T(8,128)S(1)} collective-permute-done((f32[8,5120]{1,0:T(8,128)S(1)}, f32[8,5120]{1,0:T(8,128)S(1)}, u32[]{:S(2)}, u32[]{:S(2)}) %collective-permute-start.3) | collective-permute-done | bytes 163872 | tf_op jit(solution)/shard_map/ppermute | solution.py:16
  23.5 0.1 add_subtract_fusion.3
  23.6 0.1 collective-permute-start.8
  23.6 0.2 add_divide_fusion.7
  23.9 0.0 collective-permute-done
  23.9 0.1 multiply_subtract_fusion.1
  24.0 1.3 %collective-permute-done.6 = f32[8,5120]{1,0:T(8,128)S(1)} collective-permute-done((f32[8,5120]{1,0:T(8,128)S(1)}, f32[8,5120]{1,0:T(8,128)S(1)}, u32[]{:S(2)}, u32[]{:S(2)}) %collective-permute-start.6) | collective-permute-done | bytes 163872 | tf_op jit(solution)/shard_map/ppermute | solution.py:16
  25.3 0.1 add_subtract_fusion.2
  25.4 0.1 collective-permute-start.11
  25.4 0.1 collective-permute-start.7
  25.6 2.1 %collective-permute-start.13 = (f32[16,5120]{1,0:T(8,128)S(1)}, f32[16,5120]{1,0:T(8,128)S(1)}, u32[]{:S(2)}, u32[]{:S(2)}) collective-permute-start(f32[16,5120]{1,0:T(8,128)S(1)} %bitcast_convert_fusion), channel_id=1, source_target_pairs={{0,1},{1,0},{2,3},{3,2},{4,5},{5,4},{6,7},{7,6},{8,9},{9,8},{10,11... | collective-permute-start | bytes 983048 | tf_op jit(solution)/shard_map/ppermute | solution.py:16
  27.7 3.2 %collective-permute-done.8 = f32[8,5120]{1,0:T(8,128)S(1)} collective-permute-done((f32[8,5120]{1,0:T(8,128)S(1)}, f32[8,5120]{1,0:T(8,128)S(1)}, u32[]{:S(2)}, u32[]{:S(2)}) %collective-permute-start.8) | collective-permute-done | bytes 163872 | tf_op jit(solution)/shard_map/ppermute | solution.py:16
  30.9 0.1 add_subtract_fusion.1
  30.9 0.1 collective-permute-start.12
  31.0 0.3 add_divide_fusion.3
  31.3 0.1 add_divide_fusion.5
  31.5 1.1 %collective-permute-done.7 = f32[16,5120]{1,0:T(8,128)S(1)} collective-permute-done((f32[16,5120]{1,0:T(8,128)S(1)}, f32[16,5120]{1,0:T(8,128)S(1)}, u32[]{:S(2)}, u32[]{:S(2)}) %collective-permute-start.7) | collective-permute-done | bytes 327712 | tf_op jit(solution)/shard_map/ppermute | solution.py:22
  32.6 1.5 %collective-permute-start.10 = (f32[16,5120]{1,0:T(8,128)S(1)}, f32[16,5120]{1,0:T(8,128)S(1)}, u32[]{:S(2)}, u32[]{:S(2)}) collective-permute-start(f32[16,5120]{1,0:T(8,128)S(1)} %multiply_subtract_fusion), channel_id=1, source_target_pairs={{0,8},{2,10},{4,12},{6,14},{8,0},{10,2},{12,4},{14,6},{16,24},{18,... | collective-permute-start | bytes 983048 | tf_op jit(solution)/shard_map/ppermute | solution.py:22
  34.1 0.3 collective-permute-done.11
  34.4 0.1 add_subtract_fusion
  34.5 2.6 %collective-permute-start.14 = (f32[8,5120]{1,0:T(8,128)S(1)}, f32[8,5120]{1,0:T(8,128)S(1)}, u32[]{:S(2)}, u32[]{:S(2)}) collective-permute-start(f32[8,5120]{1,0:T(8,128)S(1)} %add_subtract_fusion), channel_id=1, source_target_pairs={{0,16},{2,18},{4,20},{6,22},{8,24},{10,26},{12,28},{14,30},{16,0},... | collective-permute-start | bytes 491528 | tf_op jit(solution)/shard_map/ppermute | solution.py:16
  37.1 0.1 add_divide_fusion.2
  37.3 9.9 %collective-permute-done.10 = f32[16,5120]{1,0:T(8,128)S(1)} collective-permute-done((f32[16,5120]{1,0:T(8,128)S(1)}, f32[16,5120]{1,0:T(8,128)S(1)}, u32[]{:S(2)}, u32[]{:S(2)}) %collective-permute-start.10) | collective-permute-done | bytes 327712 | tf_op jit(solution)/shard_map/ppermute | solution.py:22
  47.2 0.1 collective-permute-start.15
  47.3 0.0 collective-permute-done.12
  47.3 0.1 fusion.14
  47.4 0.1 fusion.11
  47.5 0.3 add_divide_fusion.1
  47.9 0.9 %maximum_bitcast_fusion = (f32[1,16,5120]{2,1,0:T(8,128)}, f32[1,16,5120]{2,1,0:T(8,128)}) fusion(f32[8,5120]{1,0:T(8,128)S(1)} %get-tuple-element.63, f32[8,5120]{1,0:T(8,128)S(1)} %get-tuple-element.44, f32[8,5120]{1,0:T(8,128)S(1)} %get-tuple-element.62, f32[8,5120]{1,0:T(8,128)S(1)} %get-tuple-element.45), kind=kLoop, calls=%fused_computation.5 | loop fusion | flops 163840 | bytes 1310720 | tf_op jit(solution)/shard_map/broadcast_in_dim | solution.py:115
  48.8 11.9 %collective-permute-done.15 = f32[16,5120]{1,0:T(8,128)S(1)} collective-permute-done((f32[16,5120]{1,0:T(8,128)S(1)}, f32[16,5120]{1,0:T(8,128)S(1)}, u32[]{:S(2)}, u32[]{:S(2)}) %collective-permute-start.15) | collective-permute-done | bytes 327712 | tf_op jit(solution)/shard_map/ppermute | solution.py:22
  60.7 0.8 %multiply_bitcast_fusion = f32[1,16,5120]{2,1,0:T(8,128)} fusion(f32[16,5120]{1,0:T(8,128)S(1)} %fusion, f32[16,5120]{1,0:T(8,128)S(1)} %collective-permute-done.15), kind=kLoop, calls=%fused_computation.7 | loop fusion | flops 245760 | bytes 983040 | tf_op jit(solution)/shard_map/broadcast_in_dim | solution.py:115
  (18 shorter events, 0.3 us)
Async XLA Ops:
  0.6 14.7 %copy-start.1 = (bf16[4,1,1,32,5120]{4,3,2,1,0:T(8,128)(2,1)S(1)}, bf16[4,1,1,32,5120]{4,3,2,1,0:T(8,128)(2,1)}, u32[]{:S(2)}) copy-start(bf16[4,1,1,32,5120]{4,3,2,1,0:T(8,128)(2,1)} %param.11) | copy-start | bytes 3932164
  1.7 13.8 %collective-permute-start.4 = (f32[8,5120]{1,0:T(8,128)S(1)}, f32[8,5120]{1,0:T(8,128)S(1)}, u32[]{:S(2)}, u32[]{:S(2)}) collective-permute-start(f32[8,5120]{1,0:T(8,128)S(1)} %get-tuple-element.53), channel_id=1, source_target_pairs={{0,1},{1,0},{2,3},{3,2},{4,5},{5,4},{6,7},{7,6},{8,9},{9,8},{10,11... | collective-permute-start | bytes 491528 | tf_op jit(solution)/shard_map/ppermute | solution.py:16
  4.7 9.4 %collective-permute-start.1 = (f32[16,5120]{1,0:T(8,128)}, f32[16,5120]{1,0:T(8,128)S(1)}, u32[]{:S(2)}, u32[]{:S(2)}) collective-permute-start(f32[16,5120]{1,0:T(8,128)} %bitcast.100), channel_id=1, source_target_pairs={{0,2},{2,4},{4,6},{6,8},{8,10},{10,12},{12,14},{14,16},{16,18},{18... | collective-permute-start | bytes 983048 | tf_op jit(solution)/shard_map/ppermute | solution.py:16
  4.7 10.6 %collective-permute-start.2 = (f32[8,5120]{1,0:T(8,128)S(1)}, f32[8,5120]{1,0:T(8,128)S(1)}, u32[]{:S(2)}, u32[]{:S(2)}) collective-permute-start(f32[8,5120]{1,0:T(8,128)S(1)} %get-tuple-element.54), channel_id=1, source_target_pairs={{0,1},{1,0},{2,3},{3,2},{4,5},{5,4},{6,7},{7,6},{8,9},{9,8},{10,11... | collective-permute-start | bytes 491528 | tf_op jit(solution)/shard_map/ppermute | solution.py:16
  5.8 17.7 %collective-permute-start.5 = (f32[16,5120]{1,0:T(8,128)S(1)}, f32[16,5120]{1,0:T(8,128)S(1)}, u32[]{:S(2)}, u32[]{:S(2)}) collective-permute-start(f32[16,5120]{1,0:T(8,128)S(1)} %bitcast_convert_fusion.2), channel_id=1, source_target_pairs={{0,1},{1,0},{2,3},{3,2},{4,5},{5,4},{6,7},{7,6},{8,9},{9,8},{10,11... | collective-permute-start | bytes 983048 | tf_op jit(solution)/shard_map/ppermute | solution.py:16
  7.8 16.1 %collective-permute-start = (f32[16,5120]{1,0:T(8,128)}, f32[16,5120]{1,0:T(8,128)S(1)}, u32[]{:S(2)}, u32[]{:S(2)}) collective-permute-start(f32[16,5120]{1,0:T(8,128)} %bitcast.99), channel_id=1, source_target_pairs={{0,2},{2,0},{4,6},{6,4},{8,10},{10,8},{12,14},{14,12},{16,18},{18,... | collective-permute-start | bytes 983048 | tf_op jit(solution)/shard_map/ppermute | solution.py:22
  15.3 8.3 %copy-start = (f32[1,16,5120]{2,1,0:T(8,128)S(1)}, f32[1,16,5120]{2,1,0:T(8,128)}, u32[]{:S(2)}) copy-start(f32[1,16,5120]{2,1,0:T(8,128)} %param.9) | copy-start | bytes 983044
  15.3 8.3 %copy-start.3 = (f32[1,16,5120]{2,1,0:T(8,128)S(1)}, f32[1,16,5120]{2,1,0:T(8,128)}, u32[]{:S(2)}) copy-start(f32[1,16,5120]{2,1,0:T(8,128)} %param.10) | copy-start | bytes 983044
  15.4 8.1 %collective-permute-start.3 = (f32[8,5120]{1,0:T(8,128)S(1)}, f32[8,5120]{1,0:T(8,128)S(1)}, u32[]{:S(2)}, u32[]{:S(2)}) collective-permute-start(f32[8,5120]{1,0:T(8,128)S(1)} %fusion.25), channel_id=1, source_target_pairs={{0,4},{2,6},{4,8},{6,10},{8,12},{10,14},{12,16},{14,18},{16,20},{1... | collective-permute-start | bytes 491528 | tf_op jit(solution)/shard_map/ppermute | solution.py:16
  15.5 9.8 %collective-permute-start.6 = (f32[8,5120]{1,0:T(8,128)S(1)}, f32[8,5120]{1,0:T(8,128)S(1)}, u32[]{:S(2)}, u32[]{:S(2)}) collective-permute-start(f32[8,5120]{1,0:T(8,128)S(1)} %fusion.26), channel_id=1, source_target_pairs={{0,4},{2,6},{4,8},{6,10},{8,12},{10,14},{12,16},{14,18},{16,20},{1... | collective-permute-start | bytes 491528 | tf_op jit(solution)/shard_map/ppermute | solution.py:16
  16.9 7.0 %copy-start.2 = (f32[1,16,5120]{2,1,0:T(8,128)S(1)}, f32[1,16,5120]{2,1,0:T(8,128)}, u32[]{:S(2)}) copy-start(f32[1,16,5120]{2,1,0:T(8,128)} %param.6) | copy-start | bytes 983044
  16.9 14.0 %collective-permute-start.9 = (f32[16,5120]{1,0:T(8,128)S(1)}, f32[16,5120]{1,0:T(8,128)S(1)}, u32[]{:S(2)}, u32[]{:S(2)}) collective-permute-start(f32[16,5120]{1,0:T(8,128)S(1)} %bitcast_convert_fusion.1), channel_id=1, source_target_pairs={{0,1},{1,0},{2,3},{3,2},{4,5},{5,4},{6,7},{7,6},{8,9},{9,8},{10,11... | collective-permute-start | bytes 983048 | tf_op jit(solution)/shard_map/ppermute | solution.py:16
  23.6 7.3 %collective-permute-start.8 = (f32[8,5120]{1,0:T(8,128)S(1)}, f32[8,5120]{1,0:T(8,128)S(1)}, u32[]{:S(2)}, u32[]{:S(2)}) collective-permute-start(f32[8,5120]{1,0:T(8,128)S(1)} %add_subtract_fusion.3), channel_id=1, source_target_pairs={{0,8},{2,10},{4,12},{6,14},{8,16},{10,18},{12,20},{14,22},{16,24},... | collective-permute-start | bytes 491528 | tf_op jit(solution)/shard_map/ppermute | solution.py:16
  25.4 9.1 %collective-permute-start.11 = (f32[8,5120]{1,0:T(8,128)S(1)}, f32[8,5120]{1,0:T(8,128)S(1)}, u32[]{:S(2)}, u32[]{:S(2)}) collective-permute-start(f32[8,5120]{1,0:T(8,128)S(1)} %add_subtract_fusion.2), channel_id=1, source_target_pairs={{0,8},{2,10},{4,12},{6,14},{8,16},{10,18},{12,20},{14,22},{16,24},... | collective-permute-start | bytes 491528 | tf_op jit(solution)/shard_map/ppermute | solution.py:16
  25.4 7.1 %collective-permute-start.7 = (f32[16,5120]{1,0:T(8,128)S(1)}, f32[16,5120]{1,0:T(8,128)S(1)}, u32[]{:S(2)}, u32[]{:S(2)}) collective-permute-start(f32[16,5120]{1,0:T(8,128)S(1)} %multiply_subtract_fusion.1), channel_id=1, source_target_pairs={{0,4},{2,6},{4,0},{6,2},{8,12},{10,14},{12,8},{14,10},{16,20},{18,... | collective-permute-start | bytes 983048 | tf_op jit(solution)/shard_map/ppermute | solution.py:22
  25.6 21.7 %collective-permute-start.13 = (f32[16,5120]{1,0:T(8,128)S(1)}, f32[16,5120]{1,0:T(8,128)S(1)}, u32[]{:S(2)}, u32[]{:S(2)}) collective-permute-start(f32[16,5120]{1,0:T(8,128)S(1)} %bitcast_convert_fusion), channel_id=1, source_target_pairs={{0,1},{1,0},{2,3},{3,2},{4,5},{5,4},{6,7},{7,6},{8,9},{9,8},{10,11... | collective-permute-start | bytes 983048 | tf_op jit(solution)/shard_map/ppermute | solution.py:16
  30.9 16.4 %collective-permute-start.12 = (f32[8,5120]{1,0:T(8,128)S(1)}, f32[8,5120]{1,0:T(8,128)S(1)}, u32[]{:S(2)}, u32[]{:S(2)}) collective-permute-start(f32[8,5120]{1,0:T(8,128)S(1)} %add_subtract_fusion.1), channel_id=1, source_target_pairs={{0,16},{2,18},{4,20},{6,22},{8,24},{10,26},{12,28},{14,30},{16,0},... | collective-permute-start | bytes 491528 | tf_op jit(solution)/shard_map/ppermute | solution.py:16
  32.6 14.6 %collective-permute-start.10 = (f32[16,5120]{1,0:T(8,128)S(1)}, f32[16,5120]{1,0:T(8,128)S(1)}, u32[]{:S(2)}, u32[]{:S(2)}) collective-permute-start(f32[16,5120]{1,0:T(8,128)S(1)} %multiply_subtract_fusion), channel_id=1, source_target_pairs={{0,8},{2,10},{4,12},{6,14},{8,0},{10,2},{12,4},{14,6},{16,24},{18,... | collective-permute-start | bytes 983048 | tf_op jit(solution)/shard_map/ppermute | solution.py:22
  34.5 12.9 %collective-permute-start.14 = (f32[8,5120]{1,0:T(8,128)S(1)}, f32[8,5120]{1,0:T(8,128)S(1)}, u32[]{:S(2)}, u32[]{:S(2)}) collective-permute-start(f32[8,5120]{1,0:T(8,128)S(1)} %add_subtract_fusion), channel_id=1, source_target_pairs={{0,16},{2,18},{4,20},{6,22},{8,24},{10,26},{12,28},{14,30},{16,0},... | collective-permute-start | bytes 491528 | tf_op jit(solution)/shard_map/ppermute | solution.py:16
  47.2 13.4 %collective-permute-start.15 = (f32[16,5120]{1,0:T(8,128)S(1)}, f32[16,5120]{1,0:T(8,128)S(1)}, u32[]{:S(2)}, u32[]{:S(2)}) collective-permute-start(f32[16,5120]{1,0:T(8,128)S(1)} %maximum_subtract_fusion), channel_id=1, source_target_pairs={{0,16},{2,18},{4,20},{6,22},{8,24},{10,26},{12,28},{14,30},{16,0},... | collective-permute-start | bytes 983048 | tf_op jit(solution)/shard_map/ppermute | solution.py:22

commit v5 on v4

--- a/solution.py
+++ b/solution.py
@@ -66,22 +66,23 @@
     begun = lax.optimization_barrier([0.5 * (tracking[part] + remote_tracking[part]) - previous[part] for part in parts])
     remote_grads[0] = [after(grads, *begun) for grads in remote_grads[0]]
 
+    def moment_part(part, known):
+        moment_one[part] = BETA_ONE * moment_one[part] + (1.0 - BETA_ONE) * known
+        moment_two[part] = BETA_TWO * moment_two[part] + (1.0 - BETA_TWO) * known * known
+        return LEARNING_RATE * moment_one[part] / (jnp.sqrt(moment_two[part]) + EPSILON)
+
     def moments(known):
-        update = []
-        for part in parts:
-            moment_one[part] = BETA_ONE * moment_one[part] + (1.0 - BETA_ONE) * known[part]
-            moment_two[part] = BETA_TWO * moment_two[part] + (1.0 - BETA_TWO) * known[part] * known[part]
-            update.append(LEARNING_RATE * moment_one[part] / (jnp.sqrt(moment_two[part]) + EPSILON))
-        return jnp.concatenate(update, 0)
+        return jnp.concatenate([moment_part(part, known[part]) for part in parts], 0)
 
     order = ()
     for step in range(step_count):
         last = step + 1 == step_count
         if last:
-            weights = 0.5 * (weights + remote_weights) - moments(tracking)
-            weights = lax.optimization_barrier(weights)
-            remote_weights = mixed(weights, "replica", 2 ** (step % span_bits))
-            order = (weights,)
+            for part in parts:
+                now = 0.5 * (pieces[part] + after(remote_pieces[part], *order)) - moment_part(part, tracking[part])
+                pieces[part] = lax.optimization_barrier(now)
+                remote_pieces[part] = mixed(pieces[part], "replica", 2 ** (step % span_bits))
+                order = (pieces[part],)
         for part in parts:
             if 0 < step and part == len(parts) - 1 and not last:
                 update = lax.optimization_barrier(moments([after(before[done], *order) for done in parts]))
@@ -89,7 +90,8 @@
                 weights = lax.optimization_barrier(weights)
                 order = (weights, *order)
                 if step + 2 == step_count:
-                    remote_weights = mixed(weights, "replica", 2 ** (step % span_bits))
+                    pieces = lax.optimization_barrier(split(weights))
+                    remote_pieces = [mixed(piece, "replica", 2 ** (step % span_bits)) for piece in pieces]
             own = gradient_rows(step, place, firsts[part], size)
             mean_grad = (own + remote_grads[step][part]) * inverse_count
             if step == 0:
@@ -109,9 +111,9 @@
         if 0 < step and not last and not (step + 2 == step_count):
             weights = after(weights, tracking[-1])
             remote_weights = mixed(weights, "replica", 2 ** (step % span_bits))
-    update = moments(tracking)
-    settled_weights = lax.optimization_barrier(0.5 * weights - update - initial)
-    change = (settled_weights + 0.5 * remote_weights) / LEARNING_RATE
+    begin = split(initial)
+    settled = lax.optimization_barrier([0.5 * pieces[part] - moment_part(part, tracking[part]) - begin[part] for part in parts])
+    change = jnp.concatenate([(settled[part] + 0.5 * remote_pieces[part]) / LEARNING_RATE for part in parts], 0)
     return (change[None], jnp.concatenate(moment_one, 0)[None], jnp.concatenate(moment_two, 0)[None])
 
 

time: 61.7 us -> 61.5 us (level)
    ppermute x4 -> x6, waiting for transfers between devices: 22.9 us -> 14.8 us  [swapped(): return lax.ppermute(value, axis, pairs)]
    ppermute x12, waiting for transfers between devices: 15 us -> 22.5 us  [shifted(): return lax.ppermute(value, axis, pairs)]
    ppermute x4 -> x6, starting transfers between devices: 2.8 us -> 4.44 us  [swapped(): return lax.ppermute(value, axis, pairs)]
    ppermute x12, starting transfers between devices: 13.1 us -> 11.8 us  [shifted(): return lax.ppermute(value, axis, pairs)]
  transfers between devices with their start and end apart: 16 -> 18, of which waited for: 8 -> 11; matrix products, arithmetic and copies ran while one was open for 8% -> 8% of each run, Pallas kernels for 0% -> 0%
where the time goes in v5:
time: 61.5 us; the launch traced here: 61.4 us
  waiting for transfers between devices  37.3 us (61%)
  starting transfers between devices  16.3 us (27%)
  other arithmetic  6.83 us (11%)
  between operations  0.88 us (1%)
    ppermute x12, waiting for transfers between devices, shifted(): return lax.ppermute(value, axis, pairs)  22.5 us
    ppermute x6, waiting for transfers between devices, swapped(): return lax.ppermute(value, axis, pairs)  14.8 us
    ppermute x12, starting transfers between devices, shifted(): return lax.ppermute(value, axis, pairs)  11.8 us
    ppermute x6, starting transfers between devices, swapped(): return lax.ppermute(value, axis, pairs)  4.44 us
    convert_element_type x4, other arithmetic, gradient_rows(): lax.dynamic_slice(source, begin, (1, 1, 1, count, columns))[0, 0, 0]  2.04 us
  transfers between devices with their start and end apart: 18, of which 11 were waited for; matrix products, arithmetic and copies ran while one was open for 8% of the time, Pallas kernels for 0%

profile of v5, /device:TPU:0, one launch (start us, length us, event | category | flops | bytes accessed | tf_op | source)
XLA Modules:
  0.0 61.4 jit_solution(10151351248887592321)
XLA Ops:
  0.6 0.0 copy-start.1
  0.7 1.1 %bitcast_convert_fusion.3 = (f32[8,5120]{1,0:T(8,128)S(1)}, f32[8,5120]{1,0:T(8,128)S(1)}) fusion(bf16[4,1,1,32,5120]{4,3,2,1,0:T(8,128)(2,1)} %param.11, s32[]{:T(128)S(6)} %select_n.40, s32[]{:T(128)S(6)} %select_n.38), kind=kLoop, calls=%fused_computation.76 | loop fusion | flops 81920 | bytes 491528 | tf_op jit(solution)/shard_map/convert_element_type | solution.py:48
  1.7 3.0 %collective-permute-start.4 = (f32[8,5120]{1,0:T(8,128)S(1)}, f32[8,5120]{1,0:T(8,128)S(1)}, u32[]{:S(2)}, u32[]{:S(2)}) collective-permute-start(f32[8,5120]{1,0:T(8,128)S(1)} %get-tuple-element.65), channel_id=1, source_target_pairs={{0,1},{1,0},{2,3},{3,2},{4,5},{5,4},{6,7},{7,6},{8,9},{9,8},{10,11... | collective-permute-start | bytes 491528 | tf_op jit(solution)/shard_map/ppermute | solution.py:16
  4.7 0.1 collective-permute-start.2
  4.9 0.9 %bitcast_convert_fusion.2 = f32[16,5120]{1,0:T(8,128)S(1)} fusion(bf16[4,1,1,32,5120]{4,3,2,1,0:T(8,128)(2,1)} %param.11, s32[]{:T(128)S(6)} %select_n.38), kind=kLoop, calls=%fused_computation.47 | loop fusion | flops 81920 | bytes 491524 | tf_op jit(solution)/shard_map/convert_element_type | solution.py:48
  5.8 1.9 %collective-permute-start.5 = (f32[16,5120]{1,0:T(8,128)S(1)}, f32[16,5120]{1,0:T(8,128)S(1)}, u32[]{:S(2)}, u32[]{:S(2)}) collective-permute-start(f32[16,5120]{1,0:T(8,128)S(1)} %bitcast_convert_fusion.2), channel_id=1, source_target_pairs={{0,1},{1,0},{2,3},{3,2},{4,5},{5,4},{6,7},{7,6},{8,9},{9,8},{10,11... | collective-permute-start | bytes 983048 | tf_op jit(solution)/shard_map/ppermute | solution.py:16
  7.8 1.1 %collective-permute-start = (f32[16,5120]{1,0:T(8,128)}, f32[16,5120]{1,0:T(8,128)S(1)}, u32[]{:S(2)}, u32[]{:S(2)}) collective-permute-start(f32[16,5120]{1,0:T(8,128)} %bitcast.102), channel_id=1, source_target_pairs={{0,2},{2,0},{4,6},{6,4},{8,10},{10,8},{12,14},{14,12},{16,18},{18,... | collective-permute-start | bytes 983048 | tf_op jit(solution)/shard_map/ppermute | solution.py:22
  8.8 5.3 %collective-permute-done.1 = f32[16,5120]{1,0:T(8,128)S(1)} collective-permute-done((f32[16,5120]{1,0:T(8,128)}, f32[16,5120]{1,0:T(8,128)S(1)}, u32[]{:S(2)}, u32[]{:S(2)}) %collective-permute-start.1) | collective-permute-done | bytes 327712 | tf_op jit(solution)/shard_map/ppermute | solution.py:16
  14.1 1.2 %fusion.19 = (f32[8,5120]{1,0:T(8,128)S(1)}, f32[8,5120]{1,0:T(8,128)S(1)}) fusion(f32[16,5120]{1,0:T(8,128)S(1)} %collective-permute-done.1, f32[1,16,5120]{2,1,0:T(8,128)} %param.8, f32[1,16,5120]{2,1,0:T(8,128)} %param.7), kind=kLoop, calls=%fused_computation.41 | loop fusion | flops 245760 | bytes 1310720 | tf_op jit(solution)/shard_map/sub | solution.py:66
  15.3 0.0 copy-start.3
  15.4 0.1 collective-permute-start.3
  15.5 1.3 %collective-permute-start.6 = (f32[8,5120]{1,0:T(8,128)S(1)}, f32[8,5120]{1,0:T(8,128)S(1)}, u32[]{:S(2)}, u32[]{:S(2)}) collective-permute-start(f32[8,5120]{1,0:T(8,128)S(1)} %fusion.25), channel_id=1, source_target_pairs={{0,4},{2,6},{4,8},{6,10},{8,12},{10,14},{12,16},{14,18},{16,20},{1... | collective-permute-start | bytes 491528 | tf_op jit(solution)/shard_map/ppermute | solution.py:16
  16.9 0.0 copy-start.2
  16.9 1.8 %collective-permute-start.9 = (f32[16,5120]{1,0:T(8,128)S(1)}, f32[16,5120]{1,0:T(8,128)S(1)}, u32[]{:S(2)}, u32[]{:S(2)}) collective-permute-start(f32[16,5120]{1,0:T(8,128)S(1)} %bitcast_convert_fusion.1), channel_id=1, source_target_pairs={{0,1},{1,0},{2,3},{3,2},{4,5},{5,4},{6,7},{7,6},{8,9},{9,8},{10,11... | collective-permute-start | bytes 983048 | tf_op jit(solution)/shard_map/ppermute | solution.py:16
  18.6 4.8 %collective-permute-done.3 = f32[8,5120]{1,0:T(8,128)S(1)} collective-permute-done((f32[8,5120]{1,0:T(8,128)S(1)}, f32[8,5120]{1,0:T(8,128)S(1)}, u32[]{:S(2)}, u32[]{:S(2)}) %collective-permute-start.3) | collective-permute-done | bytes 163872 | tf_op jit(solution)/shard_map/ppermute | solution.py:16
  23.5 0.1 add_subtract_fusion.3
  23.6 0.1 collective-permute-start.8
  23.7 0.2 add_divide_fusion.3
  23.9 0.1 multiply_subtract_fusion.1
  24.0 1.3 %collective-permute-done.6 = f32[8,5120]{1,0:T(8,128)S(1)} collective-permute-done((f32[8,5120]{1,0:T(8,128)S(1)}, f32[8,5120]{1,0:T(8,128)S(1)}, u32[]{:S(2)}, u32[]{:S(2)}) %collective-permute-start.6) | collective-permute-done | bytes 163872 | tf_op jit(solution)/shard_map/ppermute | solution.py:16
  25.3 0.1 add_subtract_fusion.2
  25.4 0.1 collective-permute-start.11
  25.4 0.2 collective-permute-start.7
  25.6 2.1 %collective-permute-start.14 = (f32[16,5120]{1,0:T(8,128)S(1)}, f32[16,5120]{1,0:T(8,128)S(1)}, u32[]{:S(2)}, u32[]{:S(2)}) collective-permute-start(f32[16,5120]{1,0:T(8,128)S(1)} %bitcast_convert_fusion), channel_id=1, source_target_pairs={{0,1},{1,0},{2,3},{3,2},{4,5},{5,4},{6,7},{7,6},{8,9},{9,8},{10,11... | collective-permute-start | bytes 983048 | tf_op jit(solution)/shard_map/ppermute | solution.py:16
  27.7 3.2 %collective-permute-done.8 = f32[8,5120]{1,0:T(8,128)S(1)} collective-permute-done((f32[8,5120]{1,0:T(8,128)S(1)}, f32[8,5120]{1,0:T(8,128)S(1)}, u32[]{:S(2)}, u32[]{:S(2)}) %collective-permute-start.8) | collective-permute-done | bytes 163872 | tf_op jit(solution)/shard_map/ppermute | solution.py:16
  30.9 0.1 add_subtract_fusion.1
  31.0 0.1 collective-permute-start.12
  31.0 0.3 add_divide_fusion.1
  31.4 1.2 %collective-permute-done.7 = f32[16,5120]{1,0:T(8,128)S(1)} collective-permute-done((f32[16,5120]{1,0:T(8,128)S(1)}, f32[16,5120]{1,0:T(8,128)S(1)}, u32[]{:S(2)}, u32[]{:S(2)}) %collective-permute-start.7) | collective-permute-done | bytes 327712 | tf_op jit(solution)/shard_map/ppermute | solution.py:22
  32.6 0.1 multiply_subtract_fusion
  32.7 1.8 %collective-permute-done.11 = f32[8,5120]{1,0:T(8,128)S(1)} collective-permute-done((f32[8,5120]{1,0:T(8,128)S(1)}, f32[8,5120]{1,0:T(8,128)S(1)}, u32[]{:S(2)}, u32[]{:S(2)}) %collective-permute-start.11) | collective-permute-done | bytes 163872 | tf_op jit(solution)/shard_map/ppermute | solution.py:16
  34.4 0.1 add_subtract_fusion
  34.5 2.1 %collective-permute-start.13 = (f32[8,5120]{1,0:T(8,128)S(1)}, f32[8,5120]{1,0:T(8,128)S(1)}, u32[]{:S(2)}, u32[]{:S(2)}) collective-permute-start(f32[8,5120]{1,0:T(8,128)S(1)} %get-tuple-element.48), channel_id=1, source_target_pairs={{0,8},{2,10},{4,12},{6,14},{8,0},{10,2},{12,4},{14,6},{16,24},{18,... | collective-permute-start | bytes 491528 | tf_op jit(solution)/shard_map/ppermute | solution.py:22
  36.6 1.3 %collective-permute-start.15 = (f32[8,5120]{1,0:T(8,128)S(1)}, f32[8,5120]{1,0:T(8,128)S(1)}, u32[]{:S(2)}, u32[]{:S(2)}) collective-permute-start(f32[8,5120]{1,0:T(8,128)S(1)} %add_subtract_fusion), channel_id=1, source_target_pairs={{0,16},{2,18},{4,20},{6,22},{8,24},{10,26},{12,28},{14,30},{16,0},... | collective-permute-start | bytes 491528 | tf_op jit(solution)/shard_map/ppermute | solution.py:16
  37.9 7.3 %collective-permute-done.10 = f32[8,5120]{1,0:T(8,128)S(1)} collective-permute-done((f32[8,5120]{1,0:T(8,128)S(1)}, f32[8,5120]{1,0:T(8,128)S(1)}, u32[]{:S(2)}, u32[]{:S(2)}) %collective-permute-start.10) | collective-permute-done | bytes 163872 | tf_op jit(solution)/shard_map/ppermute | solution.py:22
  45.2 0.2 divide_subtract_fusion.1
  45.4 0.1 collective-permute-start.16
  45.4 1.9 %collective-permute-done.13 = f32[8,5120]{1,0:T(8,128)S(1)} collective-permute-done((f32[8,5120]{1,0:T(8,128)S(1)}, f32[8,5120]{1,0:T(8,128)S(1)}, u32[]{:S(2)}, u32[]{:S(2)}) %collective-permute-start.13) | collective-permute-done | bytes 163872 | tf_op jit(solution)/shard_map/ppermute | solution.py:22
  47.4 0.2 divide_subtract_fusion
  47.5 1.0 %collective-permute-start.17 = (f32[8,5120]{1,0:T(8,128)S(1)}, f32[8,5120]{1,0:T(8,128)S(1)}, u32[]{:S(2)}, u32[]{:S(2)}) collective-permute-start(f32[8,5120]{1,0:T(8,128)S(1)} %divide_subtract_fusion), channel_id=1, source_target_pairs={{0,16},{2,18},{4,20},{6,22},{8,24},{10,26},{12,28},{14,30},{16,0},... | collective-permute-start | bytes 491528 | tf_op jit(solution)/shard_map/ppermute | solution.py:22
  48.6 0.1 fusion.13
  48.7 6.1 %collective-permute-done.15 = f32[8,5120]{1,0:T(8,128)S(1)} collective-permute-done((f32[8,5120]{1,0:T(8,128)S(1)}, f32[8,5120]{1,0:T(8,128)S(1)}, u32[]{:S(2)}, u32[]{:S(2)}) %collective-permute-start.15) | collective-permute-done | bytes 163872 | tf_op jit(solution)/shard_map/ppermute | solution.py:16
  54.8 0.1 fusion.10
  54.9 0.4 bitcast_subtract_fusion
  55.3 0.9 %maximum_bitcast_fusion.1 = (f32[1,16,5120]{2,1,0:T(8,128)}, f32[1,16,5120]{2,1,0:T(8,128)}) fusion(f32[8,5120]{1,0:T(8,128)S(1)} %get-tuple-element.56, f32[8,5120]{1,0:T(8,128)S(1)} %get-tuple-element.71, f32[8,5120]{1,0:T(8,128)S(1)} %get-tuple-element.57, f32[8,5120]{1,0:T(8,128)S(1)} %get-tuple-element.70), kind=kLoop, calls=%fused_computation.3 | loop fusion | flops 163840 | bytes 1310720 | tf_op jit(solution)/shard_map/broadcast_in_dim | solution.py:117
  56.1 2.2 %collective-permute-done.16 = f32[8,5120]{1,0:T(8,128)S(1)} collective-permute-done((f32[8,5120]{1,0:T(8,128)S(1)}, f32[8,5120]{1,0:T(8,128)S(1)}, u32[]{:S(2)}, u32[]{:S(2)}) %collective-permute-start.16) | collective-permute-done | bytes 163872 | tf_op jit(solution)/shard_map/ppermute | solution.py:22
  58.3 2.2 %collective-permute-done.17 = f32[8,5120]{1,0:T(8,128)S(1)} collective-permute-done((f32[8,5120]{1,0:T(8,128)S(1)}, f32[8,5120]{1,0:T(8,128)S(1)}, u32[]{:S(2)}, u32[]{:S(2)}) %collective-permute-start.17) | collective-permute-done | bytes 163872 | tf_op jit(solution)/shard_map/ppermute | solution.py:22
  60.6 0.7 %maximum_bitcast_fusion = f32[1,16,5120]{2,1,0:T(8,128)} fusion(f32[8,5120]{1,0:T(8,128)S(1)} %add_multiply_fusion, f32[8,5120]{1,0:T(8,128)S(1)} %add_multiply_fusion.1), kind=kLoop, calls=%fused_computation.2 | loop fusion | flops 81920 | bytes 655360 | tf_op jit(solution)/shard_map/broadcast_in_dim | solution.py:117
  (23 shorter events, 0.3 us)
Async XLA Ops:
  0.6 14.7 %copy-start.1 = (bf16[4,1,1,32,5120]{4,3,2,1,0:T(8,128)(2,1)S(1)}, bf16[4,1,1,32,5120]{4,3,2,1,0:T(8,128)(2,1)}, u32[]{:S(2)}) copy-start(bf16[4,1,1,32,5120]{4,3,2,1,0:T(8,128)(2,1)} %param.11) | copy-start | bytes 3932164
  1.7 13.8 %collective-permute-start.4 = (f32[8,5120]{1,0:T(8,128)S(1)}, f32[8,5120]{1,0:T(8,128)S(1)}, u32[]{:S(2)}, u32[]{:S(2)}) collective-permute-start(f32[8,5120]{1,0:T(8,128)S(1)} %get-tuple-element.65), channel_id=1, source_target_pairs={{0,1},{1,0},{2,3},{3,2},{4,5},{5,4},{6,7},{7,6},{8,9},{9,8},{10,11... | collective-permute-start | bytes 491528 | tf_op jit(solution)/shard_map/ppermute | solution.py:16
  4.7 9.4 %collective-permute-start.1 = (f32[16,5120]{1,0:T(8,128)}, f32[16,5120]{1,0:T(8,128)S(1)}, u32[]{:S(2)}, u32[]{:S(2)}) collective-permute-start(f32[16,5120]{1,0:T(8,128)} %bitcast.103), channel_id=1, source_target_pairs={{0,2},{2,4},{4,6},{6,8},{8,10},{10,12},{12,14},{14,16},{16,18},{18... | collective-permute-start | bytes 983048 | tf_op jit(solution)/shard_map/ppermute | solution.py:16
  4.7 10.6 %collective-permute-start.2 = (f32[8,5120]{1,0:T(8,128)S(1)}, f32[8,5120]{1,0:T(8,128)S(1)}, u32[]{:S(2)}, u32[]{:S(2)}) collective-permute-start(f32[8,5120]{1,0:T(8,128)S(1)} %get-tuple-element.66), channel_id=1, source_target_pairs={{0,1},{1,0},{2,3},{3,2},{4,5},{5,4},{6,7},{7,6},{8,9},{9,8},{10,11... | collective-permute-start | bytes 491528 | tf_op jit(solution)/shard_map/ppermute | solution.py:16
  5.8 17.7 %collective-permute-start.5 = (f32[16,5120]{1,0:T(8,128)S(1)}, f32[16,5120]{1,0:T(8,128)S(1)}, u32[]{:S(2)}, u32[]{:S(2)}) collective-permute-start(f32[16,5120]{1,0:T(8,128)S(1)} %bitcast_convert_fusion.2), channel_id=1, source_target_pairs={{0,1},{1,0},{2,3},{3,2},{4,5},{5,4},{6,7},{7,6},{8,9},{9,8},{10,11... | collective-permute-start | bytes 983048 | tf_op jit(solution)/shard_map/ppermute | solution.py:16
  7.8 16.1 %collective-permute-start = (f32[16,5120]{1,0:T(8,128)}, f32[16,5120]{1,0:T(8,128)S(1)}, u32[]{:S(2)}, u32[]{:S(2)}) collective-permute-start(f32[16,5120]{1,0:T(8,128)} %bitcast.102), channel_id=1, source_target_pairs={{0,2},{2,0},{4,6},{6,4},{8,10},{10,8},{12,14},{14,12},{16,18},{18,... | collective-permute-start | bytes 983048 | tf_op jit(solution)/shard_map/ppermute | solution.py:22
  15.3 8.3 %copy-start = (f32[1,16,5120]{2,1,0:T(8,128)S(1)}, f32[1,16,5120]{2,1,0:T(8,128)}, u32[]{:S(2)}) copy-start(f32[1,16,5120]{2,1,0:T(8,128)} %param.9) | copy-start | bytes 983044
  15.3 8.3 %copy-start.3 = (f32[1,16,5120]{2,1,0:T(8,128)S(1)}, f32[1,16,5120]{2,1,0:T(8,128)}, u32[]{:S(2)}) copy-start(f32[1,16,5120]{2,1,0:T(8,128)} %param.10) | copy-start | bytes 983044
  15.4 8.1 %collective-permute-start.3 = (f32[8,5120]{1,0:T(8,128)S(1)}, f32[8,5120]{1,0:T(8,128)S(1)}, u32[]{:S(2)}, u32[]{:S(2)}) collective-permute-start(f32[8,5120]{1,0:T(8,128)S(1)} %fusion.24), channel_id=1, source_target_pairs={{0,4},{2,6},{4,8},{6,10},{8,12},{10,14},{12,16},{14,18},{16,20},{1... | collective-permute-start | bytes 491528 | tf_op jit(solution)/shard_map/ppermute | solution.py:16
  15.5 9.7 %collective-permute-start.6 = (f32[8,5120]{1,0:T(8,128)S(1)}, f32[8,5120]{1,0:T(8,128)S(1)}, u32[]{:S(2)}, u32[]{:S(2)}) collective-permute-start(f32[8,5120]{1,0:T(8,128)S(1)} %fusion.25), channel_id=1, source_target_pairs={{0,4},{2,6},{4,8},{6,10},{8,12},{10,14},{12,16},{14,18},{16,20},{1... | collective-permute-start | bytes 491528 | tf_op jit(solution)/shard_map/ppermute | solution.py:16
  16.9 7.1 %copy-start.2 = (f32[1,16,5120]{2,1,0:T(8,128)S(1)}, f32[1,16,5120]{2,1,0:T(8,128)}, u32[]{:S(2)}) copy-start(f32[1,16,5120]{2,1,0:T(8,128)} %param.6) | copy-start | bytes 983044
  16.9 14.0 %collective-permute-start.9 = (f32[16,5120]{1,0:T(8,128)S(1)}, f32[16,5120]{1,0:T(8,128)S(1)}, u32[]{:S(2)}, u32[]{:S(2)}) collective-permute-start(f32[16,5120]{1,0:T(8,128)S(1)} %bitcast_convert_fusion.1), channel_id=1, source_target_pairs={{0,1},{1,0},{2,3},{3,2},{4,5},{5,4},{6,7},{7,6},{8,9},{9,8},{10,11... | collective-permute-start | bytes 983048 | tf_op jit(solution)/shard_map/ppermute | solution.py:16
  23.6 7.3 %collective-permute-start.8 = (f32[8,5120]{1,0:T(8,128)S(1)}, f32[8,5120]{1,0:T(8,128)S(1)}, u32[]{:S(2)}, u32[]{:S(2)}) collective-permute-start(f32[8,5120]{1,0:T(8,128)S(1)} %add_subtract_fusion.3), channel_id=1, source_target_pairs={{0,8},{2,10},{4,12},{6,14},{8,16},{10,18},{12,20},{14,22},{16,24},... | collective-permute-start | bytes 491528 | tf_op jit(solution)/shard_map/ppermute | solution.py:16
  25.4 9.1 %collective-permute-start.11 = (f32[8,5120]{1,0:T(8,128)S(1)}, f32[8,5120]{1,0:T(8,128)S(1)}, u32[]{:S(2)}, u32[]{:S(2)}) collective-permute-start(f32[8,5120]{1,0:T(8,128)S(1)} %add_subtract_fusion.2), channel_id=1, source_target_pairs={{0,8},{2,10},{4,12},{6,14},{8,16},{10,18},{12,20},{14,22},{16,24},... | collective-permute-start | bytes 491528 | tf_op jit(solution)/shard_map/ppermute | solution.py:16
  25.4 7.1 %collective-permute-start.7 = (f32[16,5120]{1,0:T(8,128)S(1)}, f32[16,5120]{1,0:T(8,128)S(1)}, u32[]{:S(2)}, u32[]{:S(2)}) collective-permute-start(f32[16,5120]{1,0:T(8,128)S(1)} %multiply_subtract_fusion.1), channel_id=1, source_target_pairs={{0,4},{2,6},{4,0},{6,2},{8,12},{10,14},{12,8},{14,10},{16,20},{18,... | collective-permute-start | bytes 983048 | tf_op jit(solution)/shard_map/ppermute | solution.py:22
  25.6 23.0 %collective-permute-start.14 = (f32[16,5120]{1,0:T(8,128)S(1)}, f32[16,5120]{1,0:T(8,128)S(1)}, u32[]{:S(2)}, u32[]{:S(2)}) collective-permute-start(f32[16,5120]{1,0:T(8,128)S(1)} %bitcast_convert_fusion), channel_id=1, source_target_pairs={{0,1},{1,0},{2,3},{3,2},{4,5},{5,4},{6,7},{7,6},{8,9},{9,8},{10,11... | collective-permute-start | bytes 983048 | tf_op jit(solution)/shard_map/ppermute | solution.py:16
  31.0 17.6 %collective-permute-start.12 = (f32[8,5120]{1,0:T(8,128)S(1)}, f32[8,5120]{1,0:T(8,128)S(1)}, u32[]{:S(2)}, u32[]{:S(2)}) collective-permute-start(f32[8,5120]{1,0:T(8,128)S(1)} %add_subtract_fusion.1), channel_id=1, source_target_pairs={{0,16},{2,18},{4,20},{6,22},{8,24},{10,26},{12,28},{14,30},{16,0},... | collective-permute-start | bytes 491528 | tf_op jit(solution)/shard_map/ppermute | solution.py:16
  34.4 10.8 %collective-permute-start.10 = (f32[8,5120]{1,0:T(8,128)S(1)}, f32[8,5120]{1,0:T(8,128)S(1)}, u32[]{:S(2)}, u32[]{:S(2)}) collective-permute-start(f32[8,5120]{1,0:T(8,128)S(1)} %get-tuple-element.45), channel_id=1, source_target_pairs={{0,8},{2,10},{4,12},{6,14},{8,0},{10,2},{12,4},{14,6},{16,24},{18,... | collective-permute-start | bytes 491528 | tf_op jit(solution)/shard_map/ppermute | solution.py:22
  34.5 12.9 %collective-permute-start.13 = (f32[8,5120]{1,0:T(8,128)S(1)}, f32[8,5120]{1,0:T(8,128)S(1)}, u32[]{:S(2)}, u32[]{:S(2)}) collective-permute-start(f32[8,5120]{1,0:T(8,128)S(1)} %get-tuple-element.48), channel_id=1, source_target_pairs={{0,8},{2,10},{4,12},{6,14},{8,0},{10,2},{12,4},{14,6},{16,24},{18,... | collective-permute-start | bytes 491528 | tf_op jit(solution)/shard_map/ppermute | solution.py:22
  36.6 18.2 %collective-permute-start.15 = (f32[8,5120]{1,0:T(8,128)S(1)}, f32[8,5120]{1,0:T(8,128)S(1)}, u32[]{:S(2)}, u32[]{:S(2)}) collective-permute-start(f32[8,5120]{1,0:T(8,128)S(1)} %add_subtract_fusion), channel_id=1, source_target_pairs={{0,16},{2,18},{4,20},{6,22},{8,24},{10,26},{12,28},{14,30},{16,0},... | collective-permute-start | bytes 491528 | tf_op jit(solution)/shard_map/ppermute | solution.py:16
  45.4 12.9 %collective-permute-start.16 = (f32[8,5120]{1,0:T(8,128)S(1)}, f32[8,5120]{1,0:T(8,128)S(1)}, u32[]{:S(2)}, u32[]{:S(2)}) collective-permute-start(f32[8,5120]{1,0:T(8,128)S(1)} %divide_subtract_fusion.1), channel_id=1, source_target_pairs={{0,16},{2,18},{4,20},{6,22},{8,24},{10,26},{12,28},{14,30},{16,0},... | collective-permute-start | bytes 491528 | tf_op jit(solution)/shard_map/ppermute | solution.py:22
  47.5 13.0 %collective-permute-start.17 = (f32[8,5120]{1,0:T(8,128)S(1)}, f32[8,5120]{1,0:T(8,128)S(1)}, u32[]{:S(2)}, u32[]{:S(2)}) collective-permute-start(f32[8,5120]{1,0:T(8,128)S(1)} %divide_subtract_fusion), channel_id=1, source_target_pairs={{0,16},{2,18},{4,20},{6,22},{8,24},{10,26},{12,28},{14,30},{16,0},... | collective-permute-start | bytes 491528 | tf_op jit(solution)/shard_map/ppermute | solution.py:22

commit v6 on v5

v6 whole, which is shorter than its diff:
```python
import jax
import jax.numpy as jnp
from jax import lax
from jax.sharding import PartitionSpec as P

LEARNING_RATE = 0.001
BETA_ONE = 0.9
BETA_TWO = 0.999
EPSILON = 1e-08
PART = 8


def shifted(value, axis, steps):
    count = lax.axis_size(axis)
    pairs = [(source, (source + steps) % count) for source in range(count)]
    return lax.ppermute(value, axis, pairs)


def swapped(value, axis, distance):
    count = lax.axis_size(axis)
    pairs = [(source, source ^ distance) for source in range(count)]
    return lax.ppermute(value, axis, pairs)


def after(value, *others):
    return lax.optimization_barrier((value, *others))[0]


def per_device(params, tracker, last_grad, first_moment, second_moment, local_grads):
    initial = params[0]
    rows, columns = initial.shape
    replicas = lax.axis_size("replica")
    span_bits = replicas.bit_length() - 1
    fsdp = lax.axis_size("fsdp")
    place = lax.axis_index("fsdp")
    inverse_count = 1.0 / fsdp
    step_count = local_grads.shape[0]
    whole_span = step_count == span_bits and replicas == 2**span_bits
    mixed = swapped if whole_span else shifted
    size = PART if rows % PART == 0 else rows
    firsts = range(0, rows, size)
    parts = range(len(firsts))
    split = lambda whole: [whole[first : first + size] for first in firsts]

    def gradient_rows(step, keeper, first, count, *needed):
        source = after(local_grads, *needed) if needed else local_grads
        begin = (step, 0, 0, keeper * rows + first, 0)
        return lax.dynamic_slice(source, begin, (1, 1, 1, count, columns))[0, 0, 0].astype(jnp.float32)

    def packed(pieces, *needed):
        return lax.optimization_barrier([
            [gradient_rows(step, (place + distance) % fsdp, first, count, *needed) for step, first, count in pieces]
            for distance in range(1, fsdp)
        ])

    def sent(packs, chosen, *needed):
        totals = [jnp.zeros((1, 1), jnp.float32)] * len(chosen)
        for distance, values in enumerate(packs, 1):
            values = [values[number] for number in chosen]
            if needed:
                values = lax.optimization_barrier((values, needed))[0]
            pieces = [shifted(value, "fsdp", distance) for value in values]
            totals = pieces if distance == 1 else [total + piece for total, piece in zip(totals, pieces)]
        return totals

    def moment_part(part, known):
        moment_one[part] = BETA_ONE * moment_one[part] + (1.0 - BETA_ONE) * known
        moment_two[part] = BETA_TWO * moment_two[part] + (1.0 - BETA_TWO) * known * known
        return LEARNING_RATE * moment_one[part] / (jnp.sqrt(moment_two[part]) + EPSILON)

    def distance_of(step):
        return 2 ** (step % span_bits)

    def swap_out(pieces, step):
        return [mixed(piece, "replica", distance_of(step)) for piece in pieces]

    remote_tracking = split(shifted(tracker[0], "replica", 1))
    tracking = split(tracker[0])
    previous = split(last_grad[0])
    moment_one = split(first_moment[0])
    moment_two = split(second_moment[0])
    begin = split(initial)
    other = parts[-1]
    remote_grads = [[None for _ in parts] for _ in range(step_count)]
    pack = packed([(0, first, size) for first in firsts[:1]])
    later = packed([(0, first, size) for first in firsts[1:]] + [(1, first, size) for first in firsts], *sum(pack, []))
    shift = other
    remote_grads[0] = sent(pack, [0]) + sent(later, range(shift))
    remote_grads[1] = sent(later, range(shift, shift + len(firsts)))
    weights = [initial]
    remote_weights = swap_out(weights, 0)
    ready = after(last_grad[0], *sum(later, []))
    whole = lax.optimization_barrier(0.5 * tracker[0] - ready)
    base = split(whole)
    begun = [base[part] + 0.5 * remote_tracking[part] for part in parts]
    order = ()
    for step in range(step_count):
        last = step + 1 == step_count
        if last:
            for part in parts:
                now = 0.5 * (pieces[part] + after(remote_pieces[part], *order)) - moment_part(part, tracking[part])
                pieces[part] = lax.optimization_barrier(now)
                remote_pieces[part] = mixed(pieces[part], "replica", distance_of(step))
                order = (pieces[part],)
        for part in parts:
            if 0 < step and part == other and not last:
                update = [moment_part(done, after(before[done], *order)) for done in parts]
                update = lax.optimization_barrier(update)
                if step == 1:
                    whole = lax.optimization_barrier(weights[0] - jnp.concatenate(update, 0))
                    weights = lax.optimization_barrier(split(whole)) if False else [whole]
                else:
                    pairs = zip(weights, remote_weights)
                    mean = [0.5 * (weight + after(remote, *order)) for weight, remote in pairs]
                    whole = mean[0] if len(mean) == 1 else jnp.concatenate(mean, 0)
                    if len(mean) == 1:
                        whole = lax.optimization_barrier(whole - jnp.concatenate(update, 0))
                        weights = [whole]
                    else:
                        weights = lax.optimization_barrier([value - taken for value, taken in zip(mean, update)])
                    order = (*weights, *order)
                if step + 2 == step_count:
                    pieces = weights if len(weights) > 1 else lax.optimization_barrier(split(weights[0]))
                    remote_pieces = swap_out(pieces, step)
                elif step == 1:
                    remote_weights = swap_out(weights, step)
                    order = (*weights, *order)
            own = gradient_rows(step, place, firsts[part], size)
            mean_grad = (own + remote_grads[step][part]) * inverse_count
            if step == 0:
                now = after(begun[part], *order) + mean_grad
            else:
                known = after(remote_tracking[part], *order)
                now = 0.5 * (tracking[part] + known) + mean_grad - previous[part]
            previous[part] = mean_grad
            if part == 0:
                before = list(tracking)
            tracking[part] = lax.optimization_barrier(now)
            order = (tracking[part],)
            if not last:
                remote_tracking[part] = shifted(tracking[part], "replica", distance_of(step + 1))
            if step == 0 and part == other:
                weights = lax.optimization_barrier([0.5 * (weights[0] + after(remote_weights[0], *order))])
                order = (*weights, *order)
            if (step, part) == (0, 0) and 2 < step_count:
                remote_grads[2] = split(sent(packed([(2, 0, rows)], tracking[part]), [0])[0])
            if part == 0:
                for number in range(3, step_count):
                    if step == number - 3 + 1:
                        remote_grads[number] = split(sent(packed([(number, 0, rows)], tracking[part]), [0])[0])
        if step == 1 and not last:
            pass
    settled = [0.5 * pieces[part] - moment_part(part, tracking[part]) - begin[part] for part in parts]
    settled = lax.optimization_barrier(settled)
    change = jnp.concatenate([(settled[part] + 0.5 * remote_pieces[part]) / LEARNING_RATE for part in parts], 0)
    return (change[None], jnp.concatenate(moment_one, 0)[None], jnp.concatenate(moment_two, 0)[None])


def solution(mesh):
    in_specs = (
        P("replica", "fsdp", None),
        P("replica", "fsdp", None),
        P("replica", "fsdp", None),
        P("replica", "fsdp", None),
        P("replica", "fsdp", None),
        P(None, "replica", "fsdp", None, None),
    )
    out_specs = (P("replica", "fsdp", None), P("replica", "fsdp", None), P("replica", "fsdp", None))
    return jax.shard_map(
        per_device, mesh=mesh, in_specs=in_specs, out_specs=out_specs, check_vma=False
    )
```

time: 61.5 us -> 60.9 us (level)
  waiting for transfers between devices: 37.3 us -> 34.8 us
  starting transfers between devices: 16.3 us -> 17.7 us
    ppermute x12 -> x13, waiting for transfers between devices: 22.5 us -> 12.4 us  [shifted(): return lax.ppermute(value, axis, pairs)]
    ppermute x6, waiting for transfers between devices: 14.8 us -> 22.4 us  [swapped(): return lax.ppermute(value, axis, pairs)]
    ppermute x12 -> x13, starting transfers between devices: 11.8 us -> 14 us  [shifted(): return lax.ppermute(value, axis, pairs)]
    ppermute x6, starting transfers between devices: 4.44 us -> 3.7 us  [swapped(): return lax.ppermute(value, axis, pairs)]
    convert_element_type x4, other arithmetic: 2.04 us -> 2.73 us  [gradient_rows(): lax.dynamic_slice(source, begin, (1, 1, 1, count, columns))[0, 0, 0]]
  transfers between devices with their start and end apart: 18 -> 19, of which waited for: 11 -> 11; matrix products, arithmetic and copies ran while one was open for 8% -> 11% of each run, Pallas kernels for 0% -> 0%
where the time goes in v6:
time: 60.9 us; the launch traced here: 60.8 us
  waiting for transfers between devices  34.8 us (57%)
  starting transfers between devices  17.7 us (29%)
  other arithmetic  7.4 us (12%)
  between operations  0.83 us (1%)
    ppermute x6, waiting for transfers between devices, swapped(): return lax.ppermute(value, axis, pairs)  22.4 us
    ppermute x13, starting transfers between devices, shifted(): return lax.ppermute(value, axis, pairs)  14 us
    ppermute x13, waiting for transfers between devices, shifted(): return lax.ppermute(value, axis, pairs)  12.4 us
    ppermute x6, starting transfers between devices, swapped(): return lax.ppermute(value, axis, pairs)  3.7 us
    convert_element_type x4, other arithmetic, gradient_rows(): lax.dynamic_slice(source, begin, (1, 1, 1, count, columns))[0, 0, 0]  2.73 us
  transfers between devices with their start and end apart: 19, of which 11 were waited for; matrix products, arithmetic and copies ran while one was open for 11% of the time, Pallas kernels for 0%

profile of v6, /device:TPU:0, one launch (start us, length us, event | category | flops | bytes accessed | tf_op | source)
XLA Modules:
  0.0 60.8 jit_solution(10933771950146814399)
XLA Ops:
  0.6 0.5 collective-permute-start.1
  1.1 0.9 %bitcast_convert_fusion.5 = f32[8,5120]{1,0:T(8,128)S(1)} fusion(bf16[4,1,1,32,5120]{4,3,2,1,0:T(8,128)(2,1)} %param.11, s32[]{:T(128)S(6)} %select_n.40), kind=kLoop, calls=%fused_computation.76 | loop fusion | flops 40960 | bytes 245764 | tf_op jit(solution)/shard_map/convert_element_type | solution.py:48
  2.0 2.6 %collective-permute-start.2 = (f32[8,5120]{1,0:T(8,128)S(1)}, f32[8,5120]{1,0:T(8,128)S(1)}, u32[]{:S(2)}, u32[]{:S(2)}) collective-permute-start(f32[8,5120]{1,0:T(8,128)S(1)} %bitcast_convert_fusion.5), channel_id=1, source_target_pairs={{0,1},{1,0},{2,3},{3,2},{4,5},{5,4},{6,7},{7,6},{8,9},{9,8},{10,11... | collective-permute-start | bytes 491528 | tf_op jit(solution)/shard_map/ppermute | solution.py:16
  4.6 1.8 %bitcast_convert_fusion.2 = (f32[8,5120]{1,0:T(8,128)S(1)}, f32[8,5120]{1,0:T(8,128)S(1)}, f32[8,5120]{1,0:T(8,128)}) fusion(bf16[4,1,1,32,5120]{4,3,2,1,0:T(8,128)(2,1)} %param.11, s32[]{:T(128)S(6)} %select_n.41, s32[]{:T(128)S(6)} %select_n.40), kind=kLoop, calls=%fused_computation.73 | loop fusion | flops 122880 | bytes 737288 | tf_op jit(solution)/shard_map/convert_element_type | solution.py:48
  6.4 0.0 collective-permute-start.3
  6.4 2.0 %collective-permute-start.5 = (f32[8,5120]{1,0:T(8,128)S(1)}, f32[8,5120]{1,0:T(8,128)S(1)}, u32[]{:S(2)}, u32[]{:S(2)}) collective-permute-start(f32[8,5120]{1,0:T(8,128)S(1)} %get-tuple-element.35), channel_id=1, source_target_pairs={{0,1},{1,0},{2,3},{3,2},{4,5},{5,4},{6,7},{7,6},{8,9},{9,8},{10,11... | collective-permute-start | bytes 491528 | tf_op jit(solution)/shard_map/ppermute | solution.py:16
  8.4 0.1 collective-permute-start.9
  8.5 1.1 %multiply_subtract_fusion = f32[16,5120]{1,0:T(8,128)S(1)} fusion(f32[16,5120]{1,0:T(8,128)} %bitcast.100, f32[1,16,5120]{2,1,0:T(8,128)} %param.7), kind=kLoop, calls=%fused_computation.6 | loop fusion | flops 163840 | bytes 983040 | tf_op jit(solution)/shard_map/sub | solution.py:93
  9.6 1.5 %collective-permute-done.1 = f32[16,5120]{1,0:T(8,128)S(1)} collective-permute-done((f32[16,5120]{1,0:T(8,128)}, f32[16,5120]{1,0:T(8,128)S(1)}, u32[]{:S(2)}, u32[]{:S(2)}) %collective-permute-start.1) | collective-permute-done | bytes 327712 | tf_op jit(solution)/shard_map/ppermute | solution.py:16
  11.2 1.1 %collective-permute-start.4 = (f32[8,5120]{1,0:T(8,128)S(1)}, f32[8,5120]{1,0:T(8,128)S(1)}, u32[]{:S(2)}, u32[]{:S(2)}) collective-permute-start(f32[8,5120]{1,0:T(8,128)S(1)} %fusion.22), channel_id=1, source_target_pairs={{0,4},{2,6},{4,8},{6,10},{8,12},{10,14},{12,16},{14,18},{16,20},{1... | collective-permute-start | bytes 491528 | tf_op jit(solution)/shard_map/ppermute | solution.py:16
  12.3 1.0 %collective-permute-done.3 = f32[8,5120]{1,0:T(8,128)S(1)} collective-permute-done((f32[8,5120]{1,0:T(8,128)}, f32[8,5120]{1,0:T(8,128)S(1)}, u32[]{:S(2)}, u32[]{:S(2)}) %collective-permute-start.3) | collective-permute-done | bytes 163872 | tf_op jit(solution)/shard_map/ppermute | solution.py:16
  13.4 0.0 copy-start
  13.4 1.6 %collective-permute-start.8 = (f32[8,5120]{1,0:T(8,128)S(1)}, f32[8,5120]{1,0:T(8,128)S(1)}, u32[]{:S(2)}, u32[]{:S(2)}) collective-permute-start(f32[8,5120]{1,0:T(8,128)S(1)} %fusion.23), channel_id=1, source_target_pairs={{0,4},{2,6},{4,8},{6,10},{8,12},{10,14},{12,16},{14,18},{16,20},{1... | collective-permute-start | bytes 491528 | tf_op jit(solution)/shard_map/ppermute | solution.py:16
  15.1 0.1 add_multiply_fusion
  15.2 1.3 %collective-permute-start.10 = (f32[16,5120]{1,0:T(8,128)S(1)}, f32[16,5120]{1,0:T(8,128)S(1)}, u32[]{:S(2)}, u32[]{:S(2)}) collective-permute-start(f32[16,5120]{1,0:T(8,128)S(1)} %bitcast_convert_fusion.1), channel_id=1, source_target_pairs={{0,1},{1,0},{2,3},{3,2},{4,5},{5,4},{6,7},{7,6},{8,9},{9,8},{10,11... | collective-permute-start | bytes 983048 | tf_op jit(solution)/shard_map/ppermute | solution.py:16
  16.4 4.5 %collective-permute-done.4 = f32[8,5120]{1,0:T(8,128)S(1)} collective-permute-done((f32[8,5120]{1,0:T(8,128)S(1)}, f32[8,5120]{1,0:T(8,128)S(1)}, u32[]{:S(2)}, u32[]{:S(2)}) %collective-permute-start.4) | collective-permute-done | bytes 163872 | tf_op jit(solution)/shard_map/ppermute | solution.py:16
  21.0 0.1 add_subtract_fusion.3
  21.0 0.1 collective-permute-start.7
  21.1 0.2 add_divide_fusion.2
  21.3 0.1 maximum_subtract_fusion
  21.4 0.1 collective-permute-start.6
  21.5 3.0 %collective-permute-done.8 = f32[8,5120]{1,0:T(8,128)S(1)} collective-permute-done((f32[8,5120]{1,0:T(8,128)S(1)}, f32[8,5120]{1,0:T(8,128)S(1)}, u32[]{:S(2)}, u32[]{:S(2)}) %collective-permute-start.8) | collective-permute-done | bytes 163872 | tf_op jit(solution)/shard_map/ppermute | solution.py:16
  24.5 0.1 add_subtract_fusion.2
  24.6 0.1 collective-permute-start.12
  24.7 2.0 %collective-permute-start.15 = (f32[16,5120]{1,0:T(8,128)S(1)}, f32[16,5120]{1,0:T(8,128)S(1)}, u32[]{:S(2)}, u32[]{:S(2)}) collective-permute-start(f32[16,5120]{1,0:T(8,128)S(1)} %bitcast_convert_fusion), channel_id=1, source_target_pairs={{0,1},{1,0},{2,3},{3,2},{4,5},{5,4},{6,7},{7,6},{8,9},{9,8},{10,11... | collective-permute-start | bytes 983048 | tf_op jit(solution)/shard_map/ppermute | solution.py:16
  26.7 1.7 %collective-permute-done.7 = f32[8,5120]{1,0:T(8,128)S(1)} collective-permute-done((f32[8,5120]{1,0:T(8,128)S(1)}, f32[8,5120]{1,0:T(8,128)S(1)}, u32[]{:S(2)}, u32[]{:S(2)}) %collective-permute-start.7) | collective-permute-done | bytes 163872 | tf_op jit(solution)/shard_map/ppermute | solution.py:16
  28.3 0.1 add_subtract_fusion.1
  28.4 1.8 %collective-permute-start.13 = (f32[8,5120]{1,0:T(8,128)S(1)}, f32[8,5120]{1,0:T(8,128)S(1)}, u32[]{:S(2)}, u32[]{:S(2)}) collective-permute-start(f32[8,5120]{1,0:T(8,128)S(1)} %add_subtract_fusion.1), channel_id=1, source_target_pairs={{0,16},{2,18},{4,20},{6,22},{8,24},{10,26},{12,28},{14,30},{16,0},... | collective-permute-start | bytes 491528 | tf_op jit(solution)/shard_map/ppermute | solution.py:16
  30.2 0.3 add_divide_fusion
  30.5 0.6 %collective-permute-done.6 = f32[16,5120]{1,0:T(8,128)S(1)} collective-permute-done((f32[16,5120]{1,0:T(8,128)S(1)}, f32[16,5120]{1,0:T(8,128)S(1)}, u32[]{:S(2)}, u32[]{:S(2)}) %collective-permute-start.6) | collective-permute-done | bytes 327712 | tf_op jit(solution)/shard_map/ppermute | solution.py:22
  31.2 0.7 %collective-permute-done.12 = f32[8,5120]{1,0:T(8,128)S(1)} collective-permute-done((f32[8,5120]{1,0:T(8,128)S(1)}, f32[8,5120]{1,0:T(8,128)S(1)}, u32[]{:S(2)}, u32[]{:S(2)}) %collective-permute-start.12) | collective-permute-done | bytes 163872 | tf_op jit(solution)/shard_map/ppermute | solution.py:16
  31.9 0.4 collective-permute-start.11
  32.2 0.1 add_subtract_fusion
  32.3 1.7 %collective-permute-start.14 = (f32[8,5120]{1,0:T(8,128)S(1)}, f32[8,5120]{1,0:T(8,128)S(1)}, u32[]{:S(2)}, u32[]{:S(2)}) collective-permute-start(f32[8,5120]{1,0:T(8,128)S(1)} %get-tuple-element.56), channel_id=1, source_target_pairs={{0,8},{2,10},{4,12},{6,14},{8,0},{10,2},{12,4},{14,6},{16,24},{18,... | collective-permute-start | bytes 491528 | tf_op jit(solution)/shard_map/ppermute | solution.py:22
  34.0 0.9 %collective-permute-start.16 = (f32[8,5120]{1,0:T(8,128)S(1)}, f32[8,5120]{1,0:T(8,128)S(1)}, u32[]{:S(2)}, u32[]{:S(2)}) collective-permute-start(f32[8,5120]{1,0:T(8,128)S(1)} %add_subtract_fusion), channel_id=1, source_target_pairs={{0,16},{2,18},{4,20},{6,22},{8,24},{10,26},{12,28},{14,30},{16,0},... | collective-permute-start | bytes 491528 | tf_op jit(solution)/shard_map/ppermute | solution.py:16
  34.9 11.1 %collective-permute-done.11 = f32[8,5120]{1,0:T(8,128)S(1)} collective-permute-done((f32[8,5120]{1,0:T(8,128)S(1)}, f32[8,5120]{1,0:T(8,128)S(1)}, u32[]{:S(2)}, u32[]{:S(2)}) %collective-permute-start.11) | collective-permute-done | bytes 163872 | tf_op jit(solution)/shard_map/ppermute | solution.py:22
  46.0 0.2 divide_subtract_fusion.1
  46.1 0.1 collective-permute-start.17
  46.2 1.5 %collective-permute-done.14 = f32[8,5120]{1,0:T(8,128)S(1)} collective-permute-done((f32[8,5120]{1,0:T(8,128)S(1)}, f32[8,5120]{1,0:T(8,128)S(1)}, u32[]{:S(2)}, u32[]{:S(2)}) %collective-permute-start.14) | collective-permute-done | bytes 163872 | tf_op jit(solution)/shard_map/ppermute | solution.py:22
  47.7 0.2 divide_subtract_fusion
  47.9 1.5 %collective-permute-start.18 = (f32[8,5120]{1,0:T(8,128)S(1)}, f32[8,5120]{1,0:T(8,128)S(1)}, u32[]{:S(2)}, u32[]{:S(2)}) collective-permute-start(f32[8,5120]{1,0:T(8,128)S(1)} %divide_subtract_fusion), channel_id=1, source_target_pairs={{0,16},{2,18},{4,20},{6,22},{8,24},{10,26},{12,28},{14,30},{16,0},... | collective-permute-start | bytes 491528 | tf_op jit(solution)/shard_map/ppermute | solution.py:22
  49.4 0.1 fusion.13
  49.5 0.1 fusion.10
  49.5 0.4 bitcast_subtract_fusion
  49.9 0.9 %maximum_bitcast_fusion.1 = (f32[1,16,5120]{2,1,0:T(8,128)}, f32[1,16,5120]{2,1,0:T(8,128)}) fusion(f32[8,5120]{1,0:T(8,128)S(1)} %get-tuple-element.64, f32[8,5120]{1,0:T(8,128)S(1)} %get-tuple-element.78, f32[8,5120]{1,0:T(8,128)S(1)} %get-tuple-element.65, f32[8,5120]{1,0:T(8,128)S(1)} %get-tuple-element.77), kind=kLoop, calls=%fused_computation.3 | loop fusion | flops 163840 | bytes 1310720 | tf_op jit(solution)/shard_map/broadcast_in_dim | solution.py:156
  50.8 6.8 %collective-permute-done.17 = f32[8,5120]{1,0:T(8,128)S(1)} collective-permute-done((f32[8,5120]{1,0:T(8,128)S(1)}, f32[8,5120]{1,0:T(8,128)S(1)}, u32[]{:S(2)}, u32[]{:S(2)}) %collective-permute-start.17) | collective-permute-done | bytes 163872 | tf_op jit(solution)/shard_map/ppermute | solution.py:22
  57.7 2.3 %collective-permute-done.18 = f32[8,5120]{1,0:T(8,128)S(1)} collective-permute-done((f32[8,5120]{1,0:T(8,128)S(1)}, f32[8,5120]{1,0:T(8,128)S(1)}, u32[]{:S(2)}, u32[]{:S(2)}) %collective-permute-start.18) | collective-permute-done | bytes 163872 | tf_op jit(solution)/shard_map/ppermute | solution.py:22
  60.0 0.7 %maximum_bitcast_fusion = f32[1,16,5120]{2,1,0:T(8,128)} fusion(f32[8,5120]{1,0:T(8,128)S(1)} %add_multiply_fusion.1, f32[8,5120]{1,0:T(8,128)S(1)} %add_multiply_fusion.2), kind=kLoop, calls=%fused_computation.2 | loop fusion | flops 81920 | bytes 655360 | tf_op jit(solution)/shard_map/broadcast_in_dim | solution.py:156
  (25 shorter events, 0.3 us)
Async XLA Ops:
  0.6 10.5 %copy-start.2 = (f32[1,16,5120]{2,1,0:T(8,128)S(1)}, f32[1,16,5120]{2,1,0:T(8,128)}, u32[]{:S(2)}) copy-start(f32[1,16,5120]{2,1,0:T(8,128)} %param.6) | copy-start | bytes 983044
  0.6 10.5 %collective-permute-start.1 = (f32[16,5120]{1,0:T(8,128)}, f32[16,5120]{1,0:T(8,128)S(1)}, u32[]{:S(2)}, u32[]{:S(2)}) collective-permute-start(f32[16,5120]{1,0:T(8,128)} %bitcast.101), channel_id=1, source_target_pairs={{0,2},{2,4},{4,6},{6,8},{8,10},{10,12},{12,14},{14,16},{16,18},{18... | collective-permute-start | bytes 983048 | tf_op jit(solution)/shard_map/ppermute | solution.py:16
  2.0 9.1 %collective-permute-start.2 = (f32[8,5120]{1,0:T(8,128)S(1)}, f32[8,5120]{1,0:T(8,128)S(1)}, u32[]{:S(2)}, u32[]{:S(2)}) collective-permute-start(f32[8,5120]{1,0:T(8,128)S(1)} %bitcast_convert_fusion.5), channel_id=1, source_target_pairs={{0,1},{1,0},{2,3},{3,2},{4,5},{5,4},{6,7},{7,6},{8,9},{9,8},{10,11... | collective-permute-start | bytes 491528 | tf_op jit(solution)/shard_map/ppermute | solution.py:16
  4.6 6.5 %copy-start.1 = (bf16[4,1,1,32,5120]{4,3,2,1,0:T(8,128)(2,1)S(1)}, bf16[4,1,1,32,5120]{4,3,2,1,0:T(8,128)(2,1)}, u32[]{:S(2)}) copy-start(bf16[4,1,1,32,5120]{4,3,2,1,0:T(8,128)(2,1)} %param.11) | copy-start | bytes 3932164
  6.4 6.9 %collective-permute-start.3 = (f32[8,5120]{1,0:T(8,128)}, f32[8,5120]{1,0:T(8,128)S(1)}, u32[]{:S(2)}, u32[]{:S(2)}) collective-permute-start(f32[8,5120]{1,0:T(8,128)} %get-tuple-element.34), channel_id=1, source_target_pairs={{0,1},{1,0},{2,3},{3,2},{4,5},{5,4},{6,7},{7,6},{8,9},{9,8},{10,11... | collective-permute-start | bytes 491528 | tf_op jit(solution)/shard_map/ppermute | solution.py:16
  6.4 14.5 %collective-permute-start.5 = (f32[8,5120]{1,0:T(8,128)S(1)}, f32[8,5120]{1,0:T(8,128)S(1)}, u32[]{:S(2)}, u32[]{:S(2)}) collective-permute-start(f32[8,5120]{1,0:T(8,128)S(1)} %get-tuple-element.35), channel_id=1, source_target_pairs={{0,1},{1,0},{2,3},{3,2},{4,5},{5,4},{6,7},{7,6},{8,9},{9,8},{10,11... | collective-permute-start | bytes 491528 | tf_op jit(solution)/shard_map/ppermute | solution.py:16
  8.4 16.0 %collective-permute-start.9 = (f32[8,5120]{1,0:T(8,128)S(1)}, f32[8,5120]{1,0:T(8,128)S(1)}, u32[]{:S(2)}, u32[]{:S(2)}) collective-permute-start(f32[8,5120]{1,0:T(8,128)S(1)} %get-tuple-element.36), channel_id=1, source_target_pairs={{0,1},{1,0},{2,3},{3,2},{4,5},{5,4},{6,7},{7,6},{8,9},{9,8},{10,11... | collective-permute-start | bytes 491528 | tf_op jit(solution)/shard_map/ppermute | solution.py:16
  11.1 3.9 %collective-permute-start = (f32[16,5120]{1,0:T(8,128)S(1)}, f32[16,5120]{1,0:T(8,128)S(1)}, u32[]{:S(2)}, u32[]{:S(2)}) collective-permute-start(f32[16,5120]{1,0:T(8,128)S(1)} %bitcast.99), channel_id=1, source_target_pairs={{0,2},{2,0},{4,6},{6,4},{8,10},{10,8},{12,14},{14,12},{16,18},{18,... | collective-permute-start | bytes 983048 | tf_op jit(solution)/shard_map/ppermute | solution.py:22
  11.2 9.7 %collective-permute-start.4 = (f32[8,5120]{1,0:T(8,128)S(1)}, f32[8,5120]{1,0:T(8,128)S(1)}, u32[]{:S(2)}, u32[]{:S(2)}) collective-permute-start(f32[8,5120]{1,0:T(8,128)S(1)} %fusion.22), channel_id=1, source_target_pairs={{0,4},{2,6},{4,8},{6,10},{8,12},{10,14},{12,16},{14,18},{16,20},{1... | collective-permute-start | bytes 491528 | tf_op jit(solution)/shard_map/ppermute | solution.py:16
  13.4 7.7 %copy-start = (f32[1,16,5120]{2,1,0:T(8,128)S(1)}, f32[1,16,5120]{2,1,0:T(8,128)}, u32[]{:S(2)}) copy-start(f32[1,16,5120]{2,1,0:T(8,128)} %param.9) | copy-start | bytes 983044
  13.4 7.7 %copy-start.3 = (f32[1,16,5120]{2,1,0:T(8,128)S(1)}, f32[1,16,5120]{2,1,0:T(8,128)}, u32[]{:S(2)}) copy-start(f32[1,16,5120]{2,1,0:T(8,128)} %param.10) | copy-start | bytes 983044
  13.4 11.1 %collective-permute-start.8 = (f32[8,5120]{1,0:T(8,128)S(1)}, f32[8,5120]{1,0:T(8,128)S(1)}, u32[]{:S(2)}, u32[]{:S(2)}) collective-permute-start(f32[8,5120]{1,0:T(8,128)S(1)} %fusion.23), channel_id=1, source_target_pairs={{0,4},{2,6},{4,8},{6,10},{8,12},{10,14},{12,16},{14,18},{16,20},{1... | collective-permute-start | bytes 491528 | tf_op jit(solution)/shard_map/ppermute | solution.py:16
  15.2 13.2 %collective-permute-start.10 = (f32[16,5120]{1,0:T(8,128)S(1)}, f32[16,5120]{1,0:T(8,128)S(1)}, u32[]{:S(2)}, u32[]{:S(2)}) collective-permute-start(f32[16,5120]{1,0:T(8,128)S(1)} %bitcast_convert_fusion.1), channel_id=1, source_target_pairs={{0,1},{1,0},{2,3},{3,2},{4,5},{5,4},{6,7},{7,6},{8,9},{9,8},{10,11... | collective-permute-start | bytes 983048 | tf_op jit(solution)/shard_map/ppermute | solution.py:16
  21.0 7.3 %collective-permute-start.7 = (f32[8,5120]{1,0:T(8,128)S(1)}, f32[8,5120]{1,0:T(8,128)S(1)}, u32[]{:S(2)}, u32[]{:S(2)}) collective-permute-start(f32[8,5120]{1,0:T(8,128)S(1)} %add_subtract_fusion.3), channel_id=1, source_target_pairs={{0,8},{2,10},{4,12},{6,14},{8,16},{10,18},{12,20},{14,22},{16,24},... | collective-permute-start | bytes 491528 | tf_op jit(solution)/shard_map/ppermute | solution.py:16
  21.4 9.7 %collective-permute-start.6 = (f32[16,5120]{1,0:T(8,128)S(1)}, f32[16,5120]{1,0:T(8,128)S(1)}, u32[]{:S(2)}, u32[]{:S(2)}) collective-permute-start(f32[16,5120]{1,0:T(8,128)S(1)} %maximum_subtract_fusion), channel_id=1, source_target_pairs={{0,4},{2,6},{4,0},{6,2},{8,12},{10,14},{12,8},{14,10},{16,20},{18,... | collective-permute-start | bytes 983048 | tf_op jit(solution)/shard_map/ppermute | solution.py:22
  24.6 7.3 %collective-permute-start.12 = (f32[8,5120]{1,0:T(8,128)S(1)}, f32[8,5120]{1,0:T(8,128)S(1)}, u32[]{:S(2)}, u32[]{:S(2)}) collective-permute-start(f32[8,5120]{1,0:T(8,128)S(1)} %add_subtract_fusion.2), channel_id=1, source_target_pairs={{0,8},{2,10},{4,12},{6,14},{8,16},{10,18},{12,20},{14,22},{16,24},... | collective-permute-start | bytes 491528 | tf_op jit(solution)/shard_map/ppermute | solution.py:16
  24.7 24.7 %collective-permute-start.15 = (f32[16,5120]{1,0:T(8,128)S(1)}, f32[16,5120]{1,0:T(8,128)S(1)}, u32[]{:S(2)}, u32[]{:S(2)}) collective-permute-start(f32[16,5120]{1,0:T(8,128)S(1)} %bitcast_convert_fusion), channel_id=1, source_target_pairs={{0,1},{1,0},{2,3},{3,2},{4,5},{5,4},{6,7},{7,6},{8,9},{9,8},{10,11... | collective-permute-start | bytes 983048 | tf_op jit(solution)/shard_map/ppermute | solution.py:16
  28.4 21.0 %collective-permute-start.13 = (f32[8,5120]{1,0:T(8,128)S(1)}, f32[8,5120]{1,0:T(8,128)S(1)}, u32[]{:S(2)}, u32[]{:S(2)}) collective-permute-start(f32[8,5120]{1,0:T(8,128)S(1)} %add_subtract_fusion.1), channel_id=1, source_target_pairs={{0,16},{2,18},{4,20},{6,22},{8,24},{10,26},{12,28},{14,30},{16,0},... | collective-permute-start | bytes 491528 | tf_op jit(solution)/shard_map/ppermute | solution.py:16
  31.9 14.1 %collective-permute-start.11 = (f32[8,5120]{1,0:T(8,128)S(1)}, f32[8,5120]{1,0:T(8,128)S(1)}, u32[]{:S(2)}, u32[]{:S(2)}) collective-permute-start(f32[8,5120]{1,0:T(8,128)S(1)} %get-tuple-element.53), channel_id=1, source_target_pairs={{0,8},{2,10},{4,12},{6,14},{8,0},{10,2},{12,4},{14,6},{16,24},{18,... | collective-permute-start | bytes 491528 | tf_op jit(solution)/shard_map/ppermute | solution.py:22
  32.3 15.4 %collective-permute-start.14 = (f32[8,5120]{1,0:T(8,128)S(1)}, f32[8,5120]{1,0:T(8,128)S(1)}, u32[]{:S(2)}, u32[]{:S(2)}) collective-permute-start(f32[8,5120]{1,0:T(8,128)S(1)} %get-tuple-element.56), channel_id=1, source_target_pairs={{0,8},{2,10},{4,12},{6,14},{8,0},{10,2},{12,4},{14,6},{16,24},{18,... | collective-permute-start | bytes 491528 | tf_op jit(solution)/shard_map/ppermute | solution.py:22
  34.0 15.4 %collective-permute-start.16 = (f32[8,5120]{1,0:T(8,128)S(1)}, f32[8,5120]{1,0:T(8,128)S(1)}, u32[]{:S(2)}, u32[]{:S(2)}) collective-permute-start(f32[8,5120]{1,0:T(8,128)S(1)} %add_subtract_fusion), channel_id=1, source_target_pairs={{0,16},{2,18},{4,20},{6,22},{8,24},{10,26},{12,28},{14,30},{16,0},... | collective-permute-start | bytes 491528 | tf_op jit(solution)/shard_map/ppermute | solution.py:16
  46.1 11.5 %collective-permute-start.17 = (f32[8,5120]{1,0:T(8,128)S(1)}, f32[8,5120]{1,0:T(8,128)S(1)}, u32[]{:S(2)}, u32[]{:S(2)}) collective-permute-start(f32[8,5120]{1,0:T(8,128)S(1)} %divide_subtract_fusion.1), channel_id=1, source_target_pairs={{0,16},{2,18},{4,20},{6,22},{8,24},{10,26},{12,28},{14,30},{16,0},... | collective-permute-start | bytes 491528 | tf_op jit(solution)/shard_map/ppermute | solution.py:22
  47.9 12.1 %collective-permute-start.18 = (f32[8,5120]{1,0:T(8,128)S(1)}, f32[8,5120]{1,0:T(8,128)S(1)}, u32[]{:S(2)}, u32[]{:S(2)}) collective-permute-start(f32[8,5120]{1,0:T(8,128)S(1)} %divide_subtract_fusion), channel_id=1, source_target_pairs={{0,16},{2,18},{4,20},{6,22},{8,24},{10,26},{12,28},{14,30},{16,0},... | collective-permute-start | bytes 491528 | tf_op jit(solution)/shard_map/ppermute | solution.py:22

commit v7 on v6

--- a/solution.py
+++ b/solution.py
@@ -86,7 +86,7 @@
     later = packed([(0, first, size) for first in firsts[1:]] + [(1, first, size) for first in firsts], *sum(pack, []))
     shift = other
     remote_grads[0] = sent(pack, [0]) + sent(later, range(shift))
-    remote_grads[1] = sent(later, range(shift, shift + len(firsts)))
+    remote_grads[1] = sent(later, [shift])
     weights = [initial]
     remote_weights = swap_out(weights, 0)
     ready = after(last_grad[0], *sum(later, []))
@@ -139,14 +139,16 @@
             order = (tracking[part],)
             if not last:
                 remote_tracking[part] = shifted(tracking[part], "replica", distance_of(step + 1))
-            if step == 0 and part == other:
+            if step == 0 and part == 0:
                 weights = lax.optimization_barrier([0.5 * (weights[0] + after(remote_weights[0], *order))])
                 order = (*weights, *order)
-            if (step, part) == (0, 0) and 2 < step_count:
+            if step == 0 and part == other:
+                remote_grads[1] += sent(later, range(shift + 1, shift + len(firsts)), tracking[part])
+            if (step, part) == (0, other) and 2 < step_count:
                 remote_grads[2] = split(sent(packed([(2, 0, rows)], tracking[part]), [0])[0])
             if part == 0:
                 for number in range(3, step_count):
-                    if step == number - 3 + 1:
+                    if step == number - 3 + 2:
                         remote_grads[number] = split(sent(packed([(number, 0, rows)], tracking[part]), [0])[0])
         if step == 1 and not last:
             pass

time: 60.9 us -> 60.1 us (0.987)
  waiting for transfers between devices: 34.8 us -> 28.7 us
  starting transfers between devices: 17.7 us -> 23 us
    ppermute x13, waiting for transfers between devices: 12.4 us -> 9.11 us  [shifted(): return lax.ppermute(value, axis, pairs)]
    ppermute x6, waiting for transfers between devices: 22.4 us -> 19.6 us  [swapped(): return lax.ppermute(value, axis, pairs)]
    ppermute x6, starting transfers between devices: 3.7 us -> 6.48 us  [swapped(): return lax.ppermute(value, axis, pairs)]
    ppermute x13, starting transfers between devices: 14 us -> 16.5 us  [shifted(): return lax.ppermute(value, axis, pairs)]
  transfers between devices with their start and end apart: 19 -> 19, of which waited for: 11 -> 9; matrix products, arithmetic and copies ran while one was open for 11% -> 11% of each run, Pallas kernels for 0% -> 0%
where the time goes in v7:
time: 60.1 us; the launch traced here: 59.9 us
  waiting for transfers between devices  28.7 us (48%)
  starting transfers between devices  23 us (38%)
  other arithmetic  7.43 us (12%)
  between operations  0.8 us (1%)
    ppermute x6, waiting for transfers between devices, swapped(): return lax.ppermute(value, axis, pairs)  19.6 us
    ppermute x13, starting transfers between devices, shifted(): return lax.ppermute(value, axis, pairs)  16.5 us
    ppermute x13, waiting for transfers between devices, shifted(): return lax.ppermute(value, axis, pairs)  9.11 us
    ppermute x6, starting transfers between devices, swapped(): return lax.ppermute(value, axis, pairs)  6.48 us
    convert_element_type x4, other arithmetic, gradient_rows(): lax.dynamic_slice(source, begin, (1, 1, 1, count, columns))[0, 0, 0]  2.78 us
  transfers between devices with their start and end apart: 19, of which 9 were waited for; matrix products, arithmetic and copies ran while one was open for 11% of the time, Pallas kernels for 0%

profile of v7, /device:TPU:0, one launch (start us, length us, event | category | flops | bytes accessed | tf_op | source)
XLA Modules:
  0.0 59.9 jit_solution(17179042138465538670)
XLA Ops:
  0.6 0.5 collective-permute-start.1
  1.1 0.9 %bitcast_convert_fusion.5 = f32[8,5120]{1,0:T(8,128)S(1)} fusion(bf16[4,1,1,32,5120]{4,3,2,1,0:T(8,128)(2,1)} %param.11, s32[]{:T(128)S(6)} %select_n.40), kind=kLoop, calls=%fused_computation.76 | loop fusion | flops 40960 | bytes 245764 | tf_op jit(solution)/shard_map/convert_element_type | solution.py:48
  2.0 2.6 %collective-permute-start.2 = (f32[8,5120]{1,0:T(8,128)S(1)}, f32[8,5120]{1,0:T(8,128)S(1)}, u32[]{:S(2)}, u32[]{:S(2)}) collective-permute-start(f32[8,5120]{1,0:T(8,128)S(1)} %bitcast_convert_fusion.5), channel_id=1, source_target_pairs={{0,1},{1,0},{2,3},{3,2},{4,5},{5,4},{6,7},{7,6},{8,9},{9,8},{10,11... | collective-permute-start | bytes 491528 | tf_op jit(solution)/shard_map/ppermute | solution.py:16
  4.6 1.3 %collective-permute-start = (f32[16,5120]{1,0:T(8,128)}, f32[16,5120]{1,0:T(8,128)S(1)}, u32[]{:S(2)}, u32[]{:S(2)}) collective-permute-start(f32[16,5120]{1,0:T(8,128)} %bitcast.99), channel_id=1, source_target_pairs={{0,2},{2,0},{4,6},{6,4},{8,10},{10,8},{12,14},{14,12},{16,18},{18,... | collective-permute-start | bytes 983048 | tf_op jit(solution)/shard_map/ppermute | solution.py:22
  5.9 1.8 %bitcast_convert_fusion.2 = (f32[8,5120]{1,0:T(8,128)S(1)}, f32[8,5120]{1,0:T(8,128)}, f32[8,5120]{1,0:T(8,128)}) fusion(bf16[4,1,1,32,5120]{4,3,2,1,0:T(8,128)(2,1)} %param.11, s32[]{:T(128)S(6)} %select_n.41, s32[]{:T(128)S(6)} %select_n.40), kind=kLoop, calls=%fused_computation.73 | loop fusion | flops 122880 | bytes 737288 | tf_op jit(solution)/shard_map/convert_element_type | solution.py:48
  7.8 0.5 collective-permute-start.4
  8.3 1.5 %collective-permute-start.5 = (f32[8,5120]{1,0:T(8,128)}, f32[8,5120]{1,0:T(8,128)S(1)}, u32[]{:S(2)}, u32[]{:S(2)}) collective-permute-start(f32[8,5120]{1,0:T(8,128)} %get-tuple-element.36), channel_id=1, source_target_pairs={{0,1},{1,0},{2,3},{3,2},{4,5},{5,4},{6,7},{7,6},{8,9},{9,8},{10,11... | collective-permute-start | bytes 491528 | tf_op jit(solution)/shard_map/ppermute | solution.py:16
  9.8 1.1 %multiply_subtract_fusion = f32[16,5120]{1,0:T(8,128)S(1)} fusion(f32[16,5120]{1,0:T(8,128)} %bitcast.100, f32[1,16,5120]{2,1,0:T(8,128)} %param.7), kind=kLoop, calls=%fused_computation.6 | loop fusion | flops 163840 | bytes 983040 | tf_op jit(solution)/shard_map/sub | solution.py:93
  10.9 0.2 collective-permute-done.1
  11.1 0.0 collective-permute-done.2
  11.2 0.0 copy-start
  11.2 0.0 copy-start.3
  11.2 1.4 %collective-permute-start.3 = (f32[8,5120]{1,0:T(8,128)S(1)}, f32[8,5120]{1,0:T(8,128)S(1)}, u32[]{:S(2)}, u32[]{:S(2)}) collective-permute-start(f32[8,5120]{1,0:T(8,128)S(1)} %fusion.22), channel_id=1, source_target_pairs={{0,4},{2,6},{4,8},{6,10},{8,12},{10,14},{12,16},{14,18},{16,20},{1... | collective-permute-start | bytes 491528 | tf_op jit(solution)/shard_map/ppermute | solution.py:16
  12.7 2.4 %collective-permute-done.4 = f32[8,5120]{1,0:T(8,128)S(1)} collective-permute-done((f32[8,5120]{1,0:T(8,128)}, f32[8,5120]{1,0:T(8,128)S(1)}, u32[]{:S(2)}, u32[]{:S(2)}) %collective-permute-start.4) | collective-permute-done | bytes 163872 | tf_op jit(solution)/shard_map/ppermute | solution.py:16
  15.1 1.6 %collective-permute-start.8 = (f32[8,5120]{1,0:T(8,128)S(1)}, f32[8,5120]{1,0:T(8,128)S(1)}, u32[]{:S(2)}, u32[]{:S(2)}) collective-permute-start(f32[8,5120]{1,0:T(8,128)S(1)} %fusion.23), channel_id=1, source_target_pairs={{0,4},{2,6},{4,8},{6,10},{8,12},{10,14},{12,16},{14,18},{16,20},{1... | collective-permute-start | bytes 491528 | tf_op jit(solution)/shard_map/ppermute | solution.py:16
  16.7 0.6 %collective-permute-start.9 = (f32[8,5120]{1,0:T(8,128)S(1)}, f32[8,5120]{1,0:T(8,128)S(1)}, u32[]{:S(2)}, u32[]{:S(2)}) collective-permute-start(f32[8,5120]{1,0:T(8,128)S(1)} %get-tuple-element.47), channel_id=1, source_target_pairs={{0,1},{1,0},{2,3},{3,2},{4,5},{5,4},{6,7},{7,6},{8,9},{9,8},{10,11... | collective-permute-start | bytes 491528 | tf_op jit(solution)/shard_map/ppermute | solution.py:16
  17.3 1.5 %collective-permute-start.10 = (f32[16,5120]{1,0:T(8,128)S(1)}, f32[16,5120]{1,0:T(8,128)S(1)}, u32[]{:S(2)}, u32[]{:S(2)}) collective-permute-start(f32[16,5120]{1,0:T(8,128)S(1)} %bitcast_convert_fusion.1), channel_id=1, source_target_pairs={{0,1},{1,0},{2,3},{3,2},{4,5},{5,4},{6,7},{7,6},{8,9},{9,8},{10,11... | collective-permute-start | bytes 983048 | tf_op jit(solution)/shard_map/ppermute | solution.py:16
  18.8 1.3 %collective-permute-done.3 = f32[8,5120]{1,0:T(8,128)S(1)} collective-permute-done((f32[8,5120]{1,0:T(8,128)S(1)}, f32[8,5120]{1,0:T(8,128)S(1)}, u32[]{:S(2)}, u32[]{:S(2)}) %collective-permute-start.3) | collective-permute-done | bytes 163872 | tf_op jit(solution)/shard_map/ppermute | solution.py:16
  20.1 0.1 add_subtract_fusion.3
  20.2 0.3 collective-permute-start.7
  20.5 0.2 add_divide_fusion.2
  20.7 0.1 maximum_subtract_fusion
  20.8 1.6 %collective-permute-start.6 = (f32[16,5120]{1,0:T(8,128)S(1)}, f32[16,5120]{1,0:T(8,128)S(1)}, u32[]{:S(2)}, u32[]{:S(2)}) collective-permute-start(f32[16,5120]{1,0:T(8,128)S(1)} %maximum_subtract_fusion), channel_id=1, source_target_pairs={{0,4},{2,6},{4,0},{6,2},{8,12},{10,14},{12,8},{14,10},{16,20},{18,... | collective-permute-start | bytes 983048 | tf_op jit(solution)/shard_map/ppermute | solution.py:22
  22.3 1.8 %collective-permute-done.8 = f32[8,5120]{1,0:T(8,128)S(1)} collective-permute-done((f32[8,5120]{1,0:T(8,128)S(1)}, f32[8,5120]{1,0:T(8,128)S(1)}, u32[]{:S(2)}, u32[]{:S(2)}) %collective-permute-start.8) | collective-permute-done | bytes 163872 | tf_op jit(solution)/shard_map/ppermute | solution.py:16
  24.1 0.1 add_subtract_fusion.2
  24.2 1.3 %collective-permute-start.12 = (f32[8,5120]{1,0:T(8,128)S(1)}, f32[8,5120]{1,0:T(8,128)S(1)}, u32[]{:S(2)}, u32[]{:S(2)}) collective-permute-start(f32[8,5120]{1,0:T(8,128)S(1)} %add_subtract_fusion.2), channel_id=1, source_target_pairs={{0,8},{2,10},{4,12},{6,14},{8,16},{10,18},{12,20},{14,22},{16,24},... | collective-permute-start | bytes 491528 | tf_op jit(solution)/shard_map/ppermute | solution.py:16
  25.5 3.5 %collective-permute-done.7 = f32[8,5120]{1,0:T(8,128)S(1)} collective-permute-done((f32[8,5120]{1,0:T(8,128)S(1)}, f32[8,5120]{1,0:T(8,128)S(1)}, u32[]{:S(2)}, u32[]{:S(2)}) %collective-permute-start.7) | collective-permute-done | bytes 163872 | tf_op jit(solution)/shard_map/ppermute | solution.py:16
  29.0 0.1 add_subtract_fusion.1
  29.0 1.8 %collective-permute-start.13 = (f32[8,5120]{1,0:T(8,128)S(1)}, f32[8,5120]{1,0:T(8,128)S(1)}, u32[]{:S(2)}, u32[]{:S(2)}) collective-permute-start(f32[8,5120]{1,0:T(8,128)S(1)} %add_subtract_fusion.1), channel_id=1, source_target_pairs={{0,16},{2,18},{4,20},{6,22},{8,24},{10,26},{12,28},{14,30},{16,0},... | collective-permute-start | bytes 491528 | tf_op jit(solution)/shard_map/ppermute | solution.py:16
  30.9 0.3 add_divide_fusion
  31.2 1.3 %collective-permute-start.15 = (f32[16,5120]{1,0:T(8,128)S(1)}, f32[16,5120]{1,0:T(8,128)S(1)}, u32[]{:S(2)}, u32[]{:S(2)}) collective-permute-start(f32[16,5120]{1,0:T(8,128)S(1)} %bitcast_convert_fusion), channel_id=1, source_target_pairs={{0,1},{1,0},{2,3},{3,2},{4,5},{5,4},{6,7},{7,6},{8,9},{9,8},{10,11... | collective-permute-start | bytes 983048 | tf_op jit(solution)/shard_map/ppermute | solution.py:16
  32.6 1.6 %collective-permute-start.11 = (f32[8,5120]{1,0:T(8,128)S(1)}, f32[8,5120]{1,0:T(8,128)S(1)}, u32[]{:S(2)}, u32[]{:S(2)}) collective-permute-start(f32[8,5120]{1,0:T(8,128)S(1)} %get-tuple-element.55), channel_id=1, source_target_pairs={{0,8},{2,10},{4,12},{6,14},{8,0},{10,2},{12,4},{14,6},{16,24},{18,... | collective-permute-start | bytes 491528 | tf_op jit(solution)/shard_map/ppermute | solution.py:22
  34.1 0.1 add_subtract_fusion
  34.2 0.6 collective-permute-start.14
  34.8 1.6 %collective-permute-start.16 = (f32[8,5120]{1,0:T(8,128)S(1)}, f32[8,5120]{1,0:T(8,128)S(1)}, u32[]{:S(2)}, u32[]{:S(2)}) collective-permute-start(f32[8,5120]{1,0:T(8,128)S(1)} %add_subtract_fusion), channel_id=1, source_target_pairs={{0,16},{2,18},{4,20},{6,22},{8,24},{10,26},{12,28},{14,30},{16,0},... | collective-permute-start | bytes 491528 | tf_op jit(solution)/shard_map/ppermute | solution.py:16
  36.4 8.8 %collective-permute-done.11 = f32[8,5120]{1,0:T(8,128)S(1)} collective-permute-done((f32[8,5120]{1,0:T(8,128)S(1)}, f32[8,5120]{1,0:T(8,128)S(1)}, u32[]{:S(2)}, u32[]{:S(2)}) %collective-permute-start.11) | collective-permute-done | bytes 163872 | tf_op jit(solution)/shard_map/ppermute | solution.py:22
  45.2 0.2 divide_subtract_fusion.1
  45.3 0.1 collective-permute-start.17
  45.4 1.7 %collective-permute-done.14 = f32[8,5120]{1,0:T(8,128)S(1)} collective-permute-done((f32[8,5120]{1,0:T(8,128)S(1)}, f32[8,5120]{1,0:T(8,128)S(1)}, u32[]{:S(2)}, u32[]{:S(2)}) %collective-permute-start.14) | collective-permute-done | bytes 163872 | tf_op jit(solution)/shard_map/ppermute | solution.py:22
  47.1 0.2 divide_subtract_fusion
  47.2 1.4 %collective-permute-start.18 = (f32[8,5120]{1,0:T(8,128)S(1)}, f32[8,5120]{1,0:T(8,128)S(1)}, u32[]{:S(2)}, u32[]{:S(2)}) collective-permute-start(f32[8,5120]{1,0:T(8,128)S(1)} %divide_subtract_fusion), channel_id=1, source_target_pairs={{0,16},{2,18},{4,20},{6,22},{8,24},{10,26},{12,28},{14,30},{16,0},... | collective-permute-start | bytes 491528 | tf_op jit(solution)/shard_map/ppermute | solution.py:22
  48.6 0.1 fusion.13
  48.7 0.1 fusion.10
  48.8 0.4 bitcast_subtract_fusion
  49.2 0.9 %maximum_bitcast_fusion.1 = (f32[1,16,5120]{2,1,0:T(8,128)}, f32[1,16,5120]{2,1,0:T(8,128)}) fusion(f32[8,5120]{1,0:T(8,128)S(1)} %get-tuple-element.66, f32[8,5120]{1,0:T(8,128)S(1)} %get-tuple-element.80, f32[8,5120]{1,0:T(8,128)S(1)} %get-tuple-element.67, f32[8,5120]{1,0:T(8,128)S(1)} %get-tuple-element.79), kind=kLoop, calls=%fused_computation.3 | loop fusion | flops 163840 | bytes 1310720 | tf_op jit(solution)/shard_map/broadcast_in_dim | solution.py:158
  50.0 7.4 %collective-permute-done.17 = f32[8,5120]{1,0:T(8,128)S(1)} collective-permute-done((f32[8,5120]{1,0:T(8,128)S(1)}, f32[8,5120]{1,0:T(8,128)S(1)}, u32[]{:S(2)}, u32[]{:S(2)}) %collective-permute-start.17) | collective-permute-done | bytes 163872 | tf_op jit(solution)/shard_map/ppermute | solution.py:22
  57.4 1.7 %collective-permute-done.18 = f32[8,5120]{1,0:T(8,128)S(1)} collective-permute-done((f32[8,5120]{1,0:T(8,128)S(1)}, f32[8,5120]{1,0:T(8,128)S(1)}, u32[]{:S(2)}, u32[]{:S(2)}) %collective-permute-start.18) | collective-permute-done | bytes 163872 | tf_op jit(solution)/shard_map/ppermute | solution.py:22
  59.2 0.7 %maximum_bitcast_fusion = f32[1,16,5120]{2,1,0:T(8,128)} fusion(f32[8,5120]{1,0:T(8,128)S(1)} %add_multiply_fusion.1, f32[8,5120]{1,0:T(8,128)S(1)} %add_multiply_fusion.2), kind=kLoop, calls=%fused_computation.2 | loop fusion | flops 81920 | bytes 655360 | tf_op jit(solution)/shard_map/broadcast_in_dim | solution.py:158
  (25 shorter events, 0.3 us)
Async XLA Ops:
  0.6 10.5 %collective-permute-start.1 = (f32[16,5120]{1,0:T(8,128)}, f32[16,5120]{1,0:T(8,128)S(1)}, u32[]{:S(2)}, u32[]{:S(2)}) collective-permute-start(f32[16,5120]{1,0:T(8,128)} %bitcast.101), channel_id=1, source_target_pairs={{0,2},{2,4},{4,6},{6,8},{8,10},{10,12},{12,14},{14,16},{16,18},{18... | collective-permute-start | bytes 983048 | tf_op jit(solution)/shard_map/ppermute | solution.py:16
  2.0 9.1 %collective-permute-start.2 = (f32[8,5120]{1,0:T(8,128)S(1)}, f32[8,5120]{1,0:T(8,128)S(1)}, u32[]{:S(2)}, u32[]{:S(2)}) collective-permute-start(f32[8,5120]{1,0:T(8,128)S(1)} %bitcast_convert_fusion.5), channel_id=1, source_target_pairs={{0,1},{1,0},{2,3},{3,2},{4,5},{5,4},{6,7},{7,6},{8,9},{9,8},{10,11... | collective-permute-start | bytes 491528 | tf_op jit(solution)/shard_map/ppermute | solution.py:16
  4.6 8.0 %collective-permute-start = (f32[16,5120]{1,0:T(8,128)}, f32[16,5120]{1,0:T(8,128)S(1)}, u32[]{:S(2)}, u32[]{:S(2)}) collective-permute-start(f32[16,5120]{1,0:T(8,128)} %bitcast.99), channel_id=1, source_target_pairs={{0,2},{2,0},{4,6},{6,4},{8,10},{10,8},{12,14},{14,12},{16,18},{18,... | collective-permute-start | bytes 983048 | tf_op jit(solution)/shard_map/ppermute | solution.py:22
  5.9 5.2 %copy-start.1 = (bf16[4,1,1,32,5120]{4,3,2,1,0:T(8,128)(2,1)S(1)}, bf16[4,1,1,32,5120]{4,3,2,1,0:T(8,128)(2,1)}, u32[]{:S(2)}) copy-start(bf16[4,1,1,32,5120]{4,3,2,1,0:T(8,128)(2,1)} %param.11) | copy-start | bytes 3932164
  7.8 4.9 %copy-start.2 = (f32[1,16,5120]{2,1,0:T(8,128)S(1)}, f32[1,16,5120]{2,1,0:T(8,128)}, u32[]{:S(2)}) copy-start(f32[1,16,5120]{2,1,0:T(8,128)} %param.6) | copy-start | bytes 983044
  7.8 7.3 %collective-permute-start.4 = (f32[8,5120]{1,0:T(8,128)}, f32[8,5120]{1,0:T(8,128)S(1)}, u32[]{:S(2)}, u32[]{:S(2)}) collective-permute-start(f32[8,5120]{1,0:T(8,128)} %get-tuple-element.35), channel_id=1, source_target_pairs={{0,1},{1,0},{2,3},{3,2},{4,5},{5,4},{6,7},{7,6},{8,9},{9,8},{10,11... | collective-permute-start | bytes 491528 | tf_op jit(solution)/shard_map/ppermute | solution.py:16
  8.3 11.8 %collective-permute-start.5 = (f32[8,5120]{1,0:T(8,128)}, f32[8,5120]{1,0:T(8,128)S(1)}, u32[]{:S(2)}, u32[]{:S(2)}) collective-permute-start(f32[8,5120]{1,0:T(8,128)} %get-tuple-element.36), channel_id=1, source_target_pairs={{0,1},{1,0},{2,3},{3,2},{4,5},{5,4},{6,7},{7,6},{8,9},{9,8},{10,11... | collective-permute-start | bytes 491528 | tf_op jit(solution)/shard_map/ppermute | solution.py:16
  11.2 9.3 %copy-start = (f32[1,16,5120]{2,1,0:T(8,128)S(1)}, f32[1,16,5120]{2,1,0:T(8,128)}, u32[]{:S(2)}) copy-start(f32[1,16,5120]{2,1,0:T(8,128)} %param.9) | copy-start | bytes 983044
  11.2 9.3 %copy-start.3 = (f32[1,16,5120]{2,1,0:T(8,128)S(1)}, f32[1,16,5120]{2,1,0:T(8,128)}, u32[]{:S(2)}) copy-start(f32[1,16,5120]{2,1,0:T(8,128)} %param.10) | copy-start | bytes 983044
  11.2 8.8 %collective-permute-start.3 = (f32[8,5120]{1,0:T(8,128)S(1)}, f32[8,5120]{1,0:T(8,128)S(1)}, u32[]{:S(2)}, u32[]{:S(2)}) collective-permute-start(f32[8,5120]{1,0:T(8,128)S(1)} %fusion.22), channel_id=1, source_target_pairs={{0,4},{2,6},{4,8},{6,10},{8,12},{10,14},{12,16},{14,18},{16,20},{1... | collective-permute-start | bytes 491528 | tf_op jit(solution)/shard_map/ppermute | solution.py:16
  15.1 9.0 %collective-permute-start.8 = (f32[8,5120]{1,0:T(8,128)S(1)}, f32[8,5120]{1,0:T(8,128)S(1)}, u32[]{:S(2)}, u32[]{:S(2)}) collective-permute-start(f32[8,5120]{1,0:T(8,128)S(1)} %fusion.23), channel_id=1, source_target_pairs={{0,4},{2,6},{4,8},{6,10},{8,12},{10,14},{12,16},{14,18},{16,20},{1... | collective-permute-start | bytes 491528 | tf_op jit(solution)/shard_map/ppermute | solution.py:16
  16.7 7.4 %collective-permute-start.9 = (f32[8,5120]{1,0:T(8,128)S(1)}, f32[8,5120]{1,0:T(8,128)S(1)}, u32[]{:S(2)}, u32[]{:S(2)}) collective-permute-start(f32[8,5120]{1,0:T(8,128)S(1)} %get-tuple-element.47), channel_id=1, source_target_pairs={{0,1},{1,0},{2,3},{3,2},{4,5},{5,4},{6,7},{7,6},{8,9},{9,8},{10,11... | collective-permute-start | bytes 491528 | tf_op jit(solution)/shard_map/ppermute | solution.py:16
  17.3 11.7 %collective-permute-start.10 = (f32[16,5120]{1,0:T(8,128)S(1)}, f32[16,5120]{1,0:T(8,128)S(1)}, u32[]{:S(2)}, u32[]{:S(2)}) collective-permute-start(f32[16,5120]{1,0:T(8,128)S(1)} %bitcast_convert_fusion.1), channel_id=1, source_target_pairs={{0,1},{1,0},{2,3},{3,2},{4,5},{5,4},{6,7},{7,6},{8,9},{9,8},{10,11... | collective-permute-start | bytes 983048 | tf_op jit(solution)/shard_map/ppermute | solution.py:16
  20.2 8.8 %collective-permute-start.7 = (f32[8,5120]{1,0:T(8,128)S(1)}, f32[8,5120]{1,0:T(8,128)S(1)}, u32[]{:S(2)}, u32[]{:S(2)}) collective-permute-start(f32[8,5120]{1,0:T(8,128)S(1)} %add_subtract_fusion.3), channel_id=1, source_target_pairs={{0,8},{2,10},{4,12},{6,14},{8,16},{10,18},{12,20},{14,22},{16,24},... | collective-permute-start | bytes 491528 | tf_op jit(solution)/shard_map/ppermute | solution.py:16
  20.8 11.7 %collective-permute-start.6 = (f32[16,5120]{1,0:T(8,128)S(1)}, f32[16,5120]{1,0:T(8,128)S(1)}, u32[]{:S(2)}, u32[]{:S(2)}) collective-permute-start(f32[16,5120]{1,0:T(8,128)S(1)} %maximum_subtract_fusion), channel_id=1, source_target_pairs={{0,4},{2,6},{4,0},{6,2},{8,12},{10,14},{12,8},{14,10},{16,20},{18,... | collective-permute-start | bytes 983048 | tf_op jit(solution)/shard_map/ppermute | solution.py:22
  24.2 8.4 %collective-permute-start.12 = (f32[8,5120]{1,0:T(8,128)S(1)}, f32[8,5120]{1,0:T(8,128)S(1)}, u32[]{:S(2)}, u32[]{:S(2)}) collective-permute-start(f32[8,5120]{1,0:T(8,128)S(1)} %add_subtract_fusion.2), channel_id=1, source_target_pairs={{0,8},{2,10},{4,12},{6,14},{8,16},{10,18},{12,20},{14,22},{16,24},... | collective-permute-start | bytes 491528 | tf_op jit(solution)/shard_map/ppermute | solution.py:16
  29.0 19.6 %collective-permute-start.13 = (f32[8,5120]{1,0:T(8,128)S(1)}, f32[8,5120]{1,0:T(8,128)S(1)}, u32[]{:S(2)}, u32[]{:S(2)}) collective-permute-start(f32[8,5120]{1,0:T(8,128)S(1)} %add_subtract_fusion.1), channel_id=1, source_target_pairs={{0,16},{2,18},{4,20},{6,22},{8,24},{10,26},{12,28},{14,30},{16,0},... | collective-permute-start | bytes 491528 | tf_op jit(solution)/shard_map/ppermute | solution.py:16
  31.2 17.4 %collective-permute-start.15 = (f32[16,5120]{1,0:T(8,128)S(1)}, f32[16,5120]{1,0:T(8,128)S(1)}, u32[]{:S(2)}, u32[]{:S(2)}) collective-permute-start(f32[16,5120]{1,0:T(8,128)S(1)} %bitcast_convert_fusion), channel_id=1, source_target_pairs={{0,1},{1,0},{2,3},{3,2},{4,5},{5,4},{6,7},{7,6},{8,9},{9,8},{10,11... | collective-permute-start | bytes 983048 | tf_op jit(solution)/shard_map/ppermute | solution.py:16
  32.6 12.6 %collective-permute-start.11 = (f32[8,5120]{1,0:T(8,128)S(1)}, f32[8,5120]{1,0:T(8,128)S(1)}, u32[]{:S(2)}, u32[]{:S(2)}) collective-permute-start(f32[8,5120]{1,0:T(8,128)S(1)} %get-tuple-element.55), channel_id=1, source_target_pairs={{0,8},{2,10},{4,12},{6,14},{8,0},{10,2},{12,4},{14,6},{16,24},{18,... | collective-permute-start | bytes 491528 | tf_op jit(solution)/shard_map/ppermute | solution.py:22
  34.2 12.9 %collective-permute-start.14 = (f32[8,5120]{1,0:T(8,128)S(1)}, f32[8,5120]{1,0:T(8,128)S(1)}, u32[]{:S(2)}, u32[]{:S(2)}) collective-permute-start(f32[8,5120]{1,0:T(8,128)S(1)} %get-tuple-element.58), channel_id=1, source_target_pairs={{0,8},{2,10},{4,12},{6,14},{8,0},{10,2},{12,4},{14,6},{16,24},{18,... | collective-permute-start | bytes 491528 | tf_op jit(solution)/shard_map/ppermute | solution.py:22
  34.8 13.9 %collective-permute-start.16 = (f32[8,5120]{1,0:T(8,128)S(1)}, f32[8,5120]{1,0:T(8,128)S(1)}, u32[]{:S(2)}, u32[]{:S(2)}) collective-permute-start(f32[8,5120]{1,0:T(8,128)S(1)} %add_subtract_fusion), channel_id=1, source_target_pairs={{0,16},{2,18},{4,20},{6,22},{8,24},{10,26},{12,28},{14,30},{16,0},... | collective-permute-start | bytes 491528 | tf_op jit(solution)/shard_map/ppermute | solution.py:16
  45.3 12.1 %collective-permute-start.17 = (f32[8,5120]{1,0:T(8,128)S(1)}, f32[8,5120]{1,0:T(8,128)S(1)}, u32[]{:S(2)}, u32[]{:S(2)}) collective-permute-start(f32[8,5120]{1,0:T(8,128)S(1)} %divide_subtract_fusion.1), channel_id=1, source_target_pairs={{0,16},{2,18},{4,20},{6,22},{8,24},{10,26},{12,28},{14,30},{16,0},... | collective-permute-start | bytes 491528 | tf_op jit(solution)/shard_map/ppermute | solution.py:22
  47.2 11.9 %collective-permute-start.18 = (f32[8,5120]{1,0:T(8,128)S(1)}, f32[8,5120]{1,0:T(8,128)S(1)}, u32[]{:S(2)}, u32[]{:S(2)}) collective-permute-start(f32[8,5120]{1,0:T(8,128)S(1)} %divide_subtract_fusion), channel_id=1, source_target_pairs={{0,16},{2,18},{4,20},{6,22},{8,24},{10,26},{12,28},{14,30},{16,0},... | collective-permute-start | bytes 491528 | tf_op jit(solution)/shard_map/ppermute | solution.py:22

commit v8 on v7

--- a/solution.py
+++ b/solution.py
@@ -98,10 +98,11 @@
         last = step + 1 == step_count
         if last:
             for part in parts:
-                now = 0.5 * (pieces[part] + after(remote_pieces[part], *order)) - moment_part(part, tracking[part])
+                taken = lax.optimization_barrier(moment_part(part, tracking[part]))
+                now = 0.5 * (pieces[part] + after(remote_pieces[part], *order)) - taken
                 pieces[part] = lax.optimization_barrier(now)
                 remote_pieces[part] = mixed(pieces[part], "replica", distance_of(step))
-                order = (pieces[part],)
+                order = (pieces[part], *order)
         for part in parts:
             if 0 < step and part == other and not last:
                 update = [moment_part(done, after(before[done], *order)) for done in parts]

time: 60.1 us -> 60.2 us (level)
  no operation moved by 1% of the time
where the time goes in v8:
time: 60.2 us; the launch traced here: 60 us
  waiting for transfers between devices  28.9 us (48%)
  starting transfers between devices  22.8 us (38%)
  other arithmetic  7.46 us (12%)
  between operations  0.8 us (1%)
    ppermute x6, waiting for transfers between devices, swapped(): return lax.ppermute(value, axis, pairs)  19.8 us
    ppermute x13, starting transfers between devices, shifted(): return lax.ppermute(value, axis, pairs)  16.5 us
    ppermute x13, waiting for transfers between devices, shifted(): return lax.ppermute(value, axis, pairs)  9.11 us
    ppermute x6, starting transfers between devices, swapped(): return lax.ppermute(value, axis, pairs)  6.26 us
    convert_element_type x4, other arithmetic, gradient_rows(): lax.dynamic_slice(source, begin, (1, 1, 1, count, columns))[0, 0, 0]  2.78 us
  transfers between devices with their start and end apart: 19, of which 9 were waited for; matrix products, arithmetic and copies ran while one was open for 11% of the time, Pallas kernels for 0%

profile of v8, /device:TPU:0, one launch (start us, length us, event | category | flops | bytes accessed | tf_op | source)
XLA Modules:
  0.0 60.0 jit_solution(8697778469237930943)
XLA Ops:
  0.6 0.5 collective-permute-start.1
  1.1 0.9 %bitcast_convert_fusion.5 = f32[8,5120]{1,0:T(8,128)S(1)} fusion(bf16[4,1,1,32,5120]{4,3,2,1,0:T(8,128)(2,1)} %param.11, s32[]{:T(128)S(6)} %select_n.40), kind=kLoop, calls=%fused_computation.78 | loop fusion | flops 40960 | bytes 245764 | tf_op jit(solution)/shard_map/convert_element_type | solution.py:48
  2.0 2.6 %collective-permute-start.2 = (f32[8,5120]{1,0:T(8,128)S(1)}, f32[8,5120]{1,0:T(8,128)S(1)}, u32[]{:S(2)}, u32[]{:S(2)}) collective-permute-start(f32[8,5120]{1,0:T(8,128)S(1)} %bitcast_convert_fusion.5), channel_id=1, source_target_pairs={{0,1},{1,0},{2,3},{3,2},{4,5},{5,4},{6,7},{7,6},{8,9},{9,8},{10,11... | collective-permute-start | bytes 491528 | tf_op jit(solution)/shard_map/ppermute | solution.py:16
  4.6 1.3 %collective-permute-start = (f32[16,5120]{1,0:T(8,128)}, f32[16,5120]{1,0:T(8,128)S(1)}, u32[]{:S(2)}, u32[]{:S(2)}) collective-permute-start(f32[16,5120]{1,0:T(8,128)} %bitcast.99), channel_id=1, source_target_pairs={{0,2},{2,0},{4,6},{6,4},{8,10},{10,8},{12,14},{14,12},{16,18},{18,... | collective-permute-start | bytes 983048 | tf_op jit(solution)/shard_map/ppermute | solution.py:22
  5.9 1.8 %bitcast_convert_fusion.2 = (f32[8,5120]{1,0:T(8,128)S(1)}, f32[8,5120]{1,0:T(8,128)}, f32[8,5120]{1,0:T(8,128)}) fusion(bf16[4,1,1,32,5120]{4,3,2,1,0:T(8,128)(2,1)} %param.11, s32[]{:T(128)S(6)} %select_n.41, s32[]{:T(128)S(6)} %select_n.40), kind=kLoop, calls=%fused_computation.75 | loop fusion | flops 122880 | bytes 737288 | tf_op jit(solution)/shard_map/convert_element_type | solution.py:48
  7.8 0.5 collective-permute-start.4
  8.3 1.5 %collective-permute-start.5 = (f32[8,5120]{1,0:T(8,128)}, f32[8,5120]{1,0:T(8,128)S(1)}, u32[]{:S(2)}, u32[]{:S(2)}) collective-permute-start(f32[8,5120]{1,0:T(8,128)} %get-tuple-element.36), channel_id=1, source_target_pairs={{0,1},{1,0},{2,3},{3,2},{4,5},{5,4},{6,7},{7,6},{8,9},{9,8},{10,11... | collective-permute-start | bytes 491528 | tf_op jit(solution)/shard_map/ppermute | solution.py:16
  9.8 1.1 %multiply_subtract_fusion = f32[16,5120]{1,0:T(8,128)S(1)} fusion(f32[16,5120]{1,0:T(8,128)} %bitcast.100, f32[1,16,5120]{2,1,0:T(8,128)} %param.7), kind=kLoop, calls=%fused_computation.6 | loop fusion | flops 163840 | bytes 983040 | tf_op jit(solution)/shard_map/sub | solution.py:93
  10.9 0.2 collective-permute-done.1
  11.2 0.0 copy-start
  11.2 0.0 copy-start.3
  11.2 1.4 %collective-permute-start.3 = (f32[8,5120]{1,0:T(8,128)S(1)}, f32[8,5120]{1,0:T(8,128)S(1)}, u32[]{:S(2)}, u32[]{:S(2)}) collective-permute-start(f32[8,5120]{1,0:T(8,128)S(1)} %fusion.22), channel_id=1, source_target_pairs={{0,4},{2,6},{4,8},{6,10},{8,12},{10,14},{12,16},{14,18},{16,20},{1... | collective-permute-start | bytes 491528 | tf_op jit(solution)/shard_map/ppermute | solution.py:16
  12.6 0.0 collective-permute-done
  12.7 2.4 %collective-permute-done.4 = f32[8,5120]{1,0:T(8,128)S(1)} collective-permute-done((f32[8,5120]{1,0:T(8,128)}, f32[8,5120]{1,0:T(8,128)S(1)}, u32[]{:S(2)}, u32[]{:S(2)}) %collective-permute-start.4) | collective-permute-done | bytes 163872 | tf_op jit(solution)/shard_map/ppermute | solution.py:16
  15.1 1.6 %collective-permute-start.8 = (f32[8,5120]{1,0:T(8,128)S(1)}, f32[8,5120]{1,0:T(8,128)S(1)}, u32[]{:S(2)}, u32[]{:S(2)}) collective-permute-start(f32[8,5120]{1,0:T(8,128)S(1)} %fusion.23), channel_id=1, source_target_pairs={{0,4},{2,6},{4,8},{6,10},{8,12},{10,14},{12,16},{14,18},{16,20},{1... | collective-permute-start | bytes 491528 | tf_op jit(solution)/shard_map/ppermute | solution.py:16
  16.7 0.6 %collective-permute-start.9 = (f32[8,5120]{1,0:T(8,128)S(1)}, f32[8,5120]{1,0:T(8,128)S(1)}, u32[]{:S(2)}, u32[]{:S(2)}) collective-permute-start(f32[8,5120]{1,0:T(8,128)S(1)} %get-tuple-element.47), channel_id=1, source_target_pairs={{0,1},{1,0},{2,3},{3,2},{4,5},{5,4},{6,7},{7,6},{8,9},{9,8},{10,11... | collective-permute-start | bytes 491528 | tf_op jit(solution)/shard_map/ppermute | solution.py:16
  17.3 1.5 %collective-permute-start.10 = (f32[16,5120]{1,0:T(8,128)S(1)}, f32[16,5120]{1,0:T(8,128)S(1)}, u32[]{:S(2)}, u32[]{:S(2)}) collective-permute-start(f32[16,5120]{1,0:T(8,128)S(1)} %bitcast_convert_fusion.1), channel_id=1, source_target_pairs={{0,1},{1,0},{2,3},{3,2},{4,5},{5,4},{6,7},{7,6},{8,9},{9,8},{10,11... | collective-permute-start | bytes 983048 | tf_op jit(solution)/shard_map/ppermute | solution.py:16
  18.8 1.3 %collective-permute-done.3 = f32[8,5120]{1,0:T(8,128)S(1)} collective-permute-done((f32[8,5120]{1,0:T(8,128)S(1)}, f32[8,5120]{1,0:T(8,128)S(1)}, u32[]{:S(2)}, u32[]{:S(2)}) %collective-permute-start.3) | collective-permute-done | bytes 163872 | tf_op jit(solution)/shard_map/ppermute | solution.py:16
  20.1 0.1 add_subtract_fusion.3
  20.2 0.3 collective-permute-start.7
  20.5 0.2 add_divide_fusion.4
  20.7 0.1 maximum_subtract_fusion
  20.8 1.6 %collective-permute-start.6 = (f32[16,5120]{1,0:T(8,128)S(1)}, f32[16,5120]{1,0:T(8,128)S(1)}, u32[]{:S(2)}, u32[]{:S(2)}) collective-permute-start(f32[16,5120]{1,0:T(8,128)S(1)} %maximum_subtract_fusion), channel_id=1, source_target_pairs={{0,4},{2,6},{4,0},{6,2},{8,12},{10,14},{12,8},{14,10},{16,20},{18,... | collective-permute-start | bytes 983048 | tf_op jit(solution)/shard_map/ppermute | solution.py:22
  22.3 1.8 %collective-permute-done.8 = f32[8,5120]{1,0:T(8,128)S(1)} collective-permute-done((f32[8,5120]{1,0:T(8,128)S(1)}, f32[8,5120]{1,0:T(8,128)S(1)}, u32[]{:S(2)}, u32[]{:S(2)}) %collective-permute-start.8) | collective-permute-done | bytes 163872 | tf_op jit(solution)/shard_map/ppermute | solution.py:16
  24.1 0.1 add_subtract_fusion.2
  24.2 1.3 %collective-permute-start.12 = (f32[8,5120]{1,0:T(8,128)S(1)}, f32[8,5120]{1,0:T(8,128)S(1)}, u32[]{:S(2)}, u32[]{:S(2)}) collective-permute-start(f32[8,5120]{1,0:T(8,128)S(1)} %add_subtract_fusion.2), channel_id=1, source_target_pairs={{0,8},{2,10},{4,12},{6,14},{8,16},{10,18},{12,20},{14,22},{16,24},... | collective-permute-start | bytes 491528 | tf_op jit(solution)/shard_map/ppermute | solution.py:16
  25.5 3.5 %collective-permute-done.7 = f32[8,5120]{1,0:T(8,128)S(1)} collective-permute-done((f32[8,5120]{1,0:T(8,128)S(1)}, f32[8,5120]{1,0:T(8,128)S(1)}, u32[]{:S(2)}, u32[]{:S(2)}) %collective-permute-start.7) | collective-permute-done | bytes 163872 | tf_op jit(solution)/shard_map/ppermute | solution.py:16
  29.0 0.1 add_subtract_fusion.1
  29.0 1.8 %collective-permute-start.13 = (f32[8,5120]{1,0:T(8,128)S(1)}, f32[8,5120]{1,0:T(8,128)S(1)}, u32[]{:S(2)}, u32[]{:S(2)}) collective-permute-start(f32[8,5120]{1,0:T(8,128)S(1)} %add_subtract_fusion.1), channel_id=1, source_target_pairs={{0,16},{2,18},{4,20},{6,22},{8,24},{10,26},{12,28},{14,30},{16,0},... | collective-permute-start | bytes 491528 | tf_op jit(solution)/shard_map/ppermute | solution.py:16
  30.9 0.3 add_divide_fusion.2
  31.2 0.1 add_divide_fusion.3
  31.3 1.3 %collective-permute-start.15 = (f32[16,5120]{1,0:T(8,128)S(1)}, f32[16,5120]{1,0:T(8,128)S(1)}, u32[]{:S(2)}, u32[]{:S(2)}) collective-permute-start(f32[16,5120]{1,0:T(8,128)S(1)} %bitcast_convert_fusion), channel_id=1, source_target_pairs={{0,1},{1,0},{2,3},{3,2},{4,5},{5,4},{6,7},{7,6},{8,9},{9,8},{10,11... | collective-permute-start | bytes 983048 | tf_op jit(solution)/shard_map/ppermute | solution.py:16
  32.7 1.6 %collective-permute-start.11 = (f32[8,5120]{1,0:T(8,128)S(1)}, f32[8,5120]{1,0:T(8,128)S(1)}, u32[]{:S(2)}, u32[]{:S(2)}) collective-permute-start(f32[8,5120]{1,0:T(8,128)S(1)} %get-tuple-element.55), channel_id=1, source_target_pairs={{0,8},{2,10},{4,12},{6,14},{8,0},{10,2},{12,4},{14,6},{16,24},{18,... | collective-permute-start | bytes 491528 | tf_op jit(solution)/shard_map/ppermute | solution.py:22
  34.3 0.1 add_subtract_fusion
  34.3 0.6 collective-permute-start.14
  34.9 1.6 %collective-permute-start.16 = (f32[8,5120]{1,0:T(8,128)S(1)}, f32[8,5120]{1,0:T(8,128)S(1)}, u32[]{:S(2)}, u32[]{:S(2)}) collective-permute-start(f32[8,5120]{1,0:T(8,128)S(1)} %add_subtract_fusion), channel_id=1, source_target_pairs={{0,16},{2,18},{4,20},{6,22},{8,24},{10,26},{12,28},{14,30},{16,0},... | collective-permute-start | bytes 491528 | tf_op jit(solution)/shard_map/ppermute | solution.py:16
  36.5 0.1 add_divide_fusion
  36.7 8.6 %collective-permute-done.11 = f32[8,5120]{1,0:T(8,128)S(1)} collective-permute-done((f32[8,5120]{1,0:T(8,128)S(1)}, f32[8,5120]{1,0:T(8,128)S(1)}, u32[]{:S(2)}, u32[]{:S(2)}) %collective-permute-start.11) | collective-permute-done | bytes 163872 | tf_op jit(solution)/shard_map/ppermute | solution.py:22
  45.3 0.1 collective-permute-start.17
  45.4 1.8 %collective-permute-done.14 = f32[8,5120]{1,0:T(8,128)S(1)} collective-permute-done((f32[8,5120]{1,0:T(8,128)S(1)}, f32[8,5120]{1,0:T(8,128)S(1)}, u32[]{:S(2)}, u32[]{:S(2)}) %collective-permute-start.14) | collective-permute-done | bytes 163872 | tf_op jit(solution)/shard_map/ppermute | solution.py:22
  47.2 1.1 %collective-permute-start.18 = (f32[8,5120]{1,0:T(8,128)S(1)}, f32[8,5120]{1,0:T(8,128)S(1)}, u32[]{:S(2)}, u32[]{:S(2)}) collective-permute-start(f32[8,5120]{1,0:T(8,128)S(1)} %multiply_subtract_fusion.1), channel_id=1, source_target_pairs={{0,16},{2,18},{4,20},{6,22},{8,24},{10,26},{12,28},{14,30},{16,0},... | collective-permute-start | bytes 491528 | tf_op jit(solution)/shard_map/ppermute | solution.py:22
  48.4 0.1 fusion.13
  48.5 0.1 fusion.10
  48.6 0.4 bitcast_subtract_fusion
  48.9 0.9 %maximum_bitcast_fusion.1 = (f32[1,16,5120]{2,1,0:T(8,128)}, f32[1,16,5120]{2,1,0:T(8,128)}) fusion(f32[8,5120]{1,0:T(8,128)S(1)} %get-tuple-element.66, f32[8,5120]{1,0:T(8,128)S(1)} %get-tuple-element.80, f32[8,5120]{1,0:T(8,128)S(1)} %get-tuple-element.67, f32[8,5120]{1,0:T(8,128)S(1)} %get-tuple-element.79), kind=kLoop, calls=%fused_computation.3 | loop fusion | flops 163840 | bytes 1310720 | tf_op jit(solution)/shard_map/broadcast_in_dim | solution.py:159
  49.8 7.6 %collective-permute-done.17 = f32[8,5120]{1,0:T(8,128)S(1)} collective-permute-done((f32[8,5120]{1,0:T(8,128)S(1)}, f32[8,5120]{1,0:T(8,128)S(1)}, u32[]{:S(2)}, u32[]{:S(2)}) %collective-permute-start.17) | collective-permute-done | bytes 163872 | tf_op jit(solution)/shard_map/ppermute | solution.py:22
  57.5 1.7 %collective-permute-done.18 = f32[8,5120]{1,0:T(8,128)S(1)} collective-permute-done((f32[8,5120]{1,0:T(8,128)S(1)}, f32[8,5120]{1,0:T(8,128)S(1)}, u32[]{:S(2)}, u32[]{:S(2)}) %collective-permute-start.18) | collective-permute-done | bytes 163872 | tf_op jit(solution)/shard_map/ppermute | solution.py:22
  59.2 0.7 %maximum_bitcast_fusion = f32[1,16,5120]{2,1,0:T(8,128)} fusion(f32[8,5120]{1,0:T(8,128)S(1)} %add_multiply_fusion.1, f32[8,5120]{1,0:T(8,128)S(1)} %add_multiply_fusion.2), kind=kLoop, calls=%fused_computation.2 | loop fusion | flops 81920 | bytes 655360 | tf_op jit(solution)/shard_map/broadcast_in_dim | solution.py:159
  (27 shorter events, 0.4 us)
Async XLA Ops:
  0.6 10.5 %collective-permute-start.1 = (f32[16,5120]{1,0:T(8,128)}, f32[16,5120]{1,0:T(8,128)S(1)}, u32[]{:S(2)}, u32[]{:S(2)}) collective-permute-start(f32[16,5120]{1,0:T(8,128)} %bitcast.101), channel_id=1, source_target_pairs={{0,2},{2,4},{4,6},{6,8},{8,10},{10,12},{12,14},{14,16},{16,18},{18... | collective-permute-start | bytes 983048 | tf_op jit(solution)/shard_map/ppermute | solution.py:16
  2.0 9.1 %collective-permute-start.2 = (f32[8,5120]{1,0:T(8,128)S(1)}, f32[8,5120]{1,0:T(8,128)S(1)}, u32[]{:S(2)}, u32[]{:S(2)}) collective-permute-start(f32[8,5120]{1,0:T(8,128)S(1)} %bitcast_convert_fusion.5), channel_id=1, source_target_pairs={{0,1},{1,0},{2,3},{3,2},{4,5},{5,4},{6,7},{7,6},{8,9},{9,8},{10,11... | collective-permute-start | bytes 491528 | tf_op jit(solution)/shard_map/ppermute | solution.py:16
  4.6 8.0 %collective-permute-start = (f32[16,5120]{1,0:T(8,128)}, f32[16,5120]{1,0:T(8,128)S(1)}, u32[]{:S(2)}, u32[]{:S(2)}) collective-permute-start(f32[16,5120]{1,0:T(8,128)} %bitcast.99), channel_id=1, source_target_pairs={{0,2},{2,0},{4,6},{6,4},{8,10},{10,8},{12,14},{14,12},{16,18},{18,... | collective-permute-start | bytes 983048 | tf_op jit(solution)/shard_map/ppermute | solution.py:22
  5.9 5.2 %copy-start.1 = (bf16[4,1,1,32,5120]{4,3,2,1,0:T(8,128)(2,1)S(1)}, bf16[4,1,1,32,5120]{4,3,2,1,0:T(8,128)(2,1)}, u32[]{:S(2)}) copy-start(bf16[4,1,1,32,5120]{4,3,2,1,0:T(8,128)(2,1)} %param.11) | copy-start | bytes 3932164
  7.8 4.9 %copy-start.2 = (f32[1,16,5120]{2,1,0:T(8,128)S(1)}, f32[1,16,5120]{2,1,0:T(8,128)}, u32[]{:S(2)}) copy-start(f32[1,16,5120]{2,1,0:T(8,128)} %param.6) | copy-start | bytes 983044
  7.8 7.3 %collective-permute-start.4 = (f32[8,5120]{1,0:T(8,128)}, f32[8,5120]{1,0:T(8,128)S(1)}, u32[]{:S(2)}, u32[]{:S(2)}) collective-permute-start(f32[8,5120]{1,0:T(8,128)} %get-tuple-element.35), channel_id=1, source_target_pairs={{0,1},{1,0},{2,3},{3,2},{4,5},{5,4},{6,7},{7,6},{8,9},{9,8},{10,11... | collective-permute-start | bytes 491528 | tf_op jit(solution)/shard_map/ppermute | solution.py:16
  8.3 11.8 %collective-permute-start.5 = (f32[8,5120]{1,0:T(8,128)}, f32[8,5120]{1,0:T(8,128)S(1)}, u32[]{:S(2)}, u32[]{:S(2)}) collective-permute-start(f32[8,5120]{1,0:T(8,128)} %get-tuple-element.36), channel_id=1, source_target_pairs={{0,1},{1,0},{2,3},{3,2},{4,5},{5,4},{6,7},{7,6},{8,9},{9,8},{10,11... | collective-permute-start | bytes 491528 | tf_op jit(solution)/shard_map/ppermute | solution.py:16
  11.2 9.3 %copy-start = (f32[1,16,5120]{2,1,0:T(8,128)S(1)}, f32[1,16,5120]{2,1,0:T(8,128)}, u32[]{:S(2)}) copy-start(f32[1,16,5120]{2,1,0:T(8,128)} %param.9) | copy-start | bytes 983044
  11.2 9.3 %copy-start.3 = (f32[1,16,5120]{2,1,0:T(8,128)S(1)}, f32[1,16,5120]{2,1,0:T(8,128)}, u32[]{:S(2)}) copy-start(f32[1,16,5120]{2,1,0:T(8,128)} %param.10) | copy-start | bytes 983044
  11.2 8.8 %collective-permute-start.3 = (f32[8,5120]{1,0:T(8,128)S(1)}, f32[8,5120]{1,0:T(8,128)S(1)}, u32[]{:S(2)}, u32[]{:S(2)}) collective-permute-start(f32[8,5120]{1,0:T(8,128)S(1)} %fusion.22), channel_id=1, source_target_pairs={{0,4},{2,6},{4,8},{6,10},{8,12},{10,14},{12,16},{14,18},{16,20},{1... | collective-permute-start | bytes 491528 | tf_op jit(solution)/shard_map/ppermute | solution.py:16
  15.1 9.0 %collective-permute-start.8 = (f32[8,5120]{1,0:T(8,128)S(1)}, f32[8,5120]{1,0:T(8,128)S(1)}, u32[]{:S(2)}, u32[]{:S(2)}) collective-permute-start(f32[8,5120]{1,0:T(8,128)S(1)} %fusion.23), channel_id=1, source_target_pairs={{0,4},{2,6},{4,8},{6,10},{8,12},{10,14},{12,16},{14,18},{16,20},{1... | collective-permute-start | bytes 491528 | tf_op jit(solution)/shard_map/ppermute | solution.py:16
  16.7 7.4 %collective-permute-start.9 = (f32[8,5120]{1,0:T(8,128)S(1)}, f32[8,5120]{1,0:T(8,128)S(1)}, u32[]{:S(2)}, u32[]{:S(2)}) collective-permute-start(f32[8,5120]{1,0:T(8,128)S(1)} %get-tuple-element.47), channel_id=1, source_target_pairs={{0,1},{1,0},{2,3},{3,2},{4,5},{5,4},{6,7},{7,6},{8,9},{9,8},{10,11... | collective-permute-start | bytes 491528 | tf_op jit(solution)/shard_map/ppermute | solution.py:16
  17.3 11.7 %collective-permute-start.10 = (f32[16,5120]{1,0:T(8,128)S(1)}, f32[16,5120]{1,0:T(8,128)S(1)}, u32[]{:S(2)}, u32[]{:S(2)}) collective-permute-start(f32[16,5120]{1,0:T(8,128)S(1)} %bitcast_convert_fusion.1), channel_id=1, source_target_pairs={{0,1},{1,0},{2,3},{3,2},{4,5},{5,4},{6,7},{7,6},{8,9},{9,8},{10,11... | collective-permute-start | bytes 983048 | tf_op jit(solution)/shard_map/ppermute | solution.py:16
  20.2 8.8 %collective-permute-start.7 = (f32[8,5120]{1,0:T(8,128)S(1)}, f32[8,5120]{1,0:T(8,128)S(1)}, u32[]{:S(2)}, u32[]{:S(2)}) collective-permute-start(f32[8,5120]{1,0:T(8,128)S(1)} %add_subtract_fusion.3), channel_id=1, source_target_pairs={{0,8},{2,10},{4,12},{6,14},{8,16},{10,18},{12,20},{14,22},{16,24},... | collective-permute-start | bytes 491528 | tf_op jit(solution)/shard_map/ppermute | solution.py:16
  20.8 11.8 %collective-permute-start.6 = (f32[16,5120]{1,0:T(8,128)S(1)}, f32[16,5120]{1,0:T(8,128)S(1)}, u32[]{:S(2)}, u32[]{:S(2)}) collective-permute-start(f32[16,5120]{1,0:T(8,128)S(1)} %maximum_subtract_fusion), channel_id=1, source_target_pairs={{0,4},{2,6},{4,0},{6,2},{8,12},{10,14},{12,8},{14,10},{16,20},{18,... | collective-permute-start | bytes 983048 | tf_op jit(solution)/shard_map/ppermute | solution.py:22
  24.2 10.1 %collective-permute-start.12 = (f32[8,5120]{1,0:T(8,128)S(1)}, f32[8,5120]{1,0:T(8,128)S(1)}, u32[]{:S(2)}, u32[]{:S(2)}) collective-permute-start(f32[8,5120]{1,0:T(8,128)S(1)} %add_subtract_fusion.2), channel_id=1, source_target_pairs={{0,8},{2,10},{4,12},{6,14},{8,16},{10,18},{12,20},{14,22},{16,24},... | collective-permute-start | bytes 491528 | tf_op jit(solution)/shard_map/ppermute | solution.py:16
  29.0 19.3 %collective-permute-start.13 = (f32[8,5120]{1,0:T(8,128)S(1)}, f32[8,5120]{1,0:T(8,128)S(1)}, u32[]{:S(2)}, u32[]{:S(2)}) collective-permute-start(f32[8,5120]{1,0:T(8,128)S(1)} %add_subtract_fusion.1), channel_id=1, source_target_pairs={{0,16},{2,18},{4,20},{6,22},{8,24},{10,26},{12,28},{14,30},{16,0},... | collective-permute-start | bytes 491528 | tf_op jit(solution)/shard_map/ppermute | solution.py:16
  31.3 17.1 %collective-permute-start.15 = (f32[16,5120]{1,0:T(8,128)S(1)}, f32[16,5120]{1,0:T(8,128)S(1)}, u32[]{:S(2)}, u32[]{:S(2)}) collective-permute-start(f32[16,5120]{1,0:T(8,128)S(1)} %bitcast_convert_fusion), channel_id=1, source_target_pairs={{0,1},{1,0},{2,3},{3,2},{4,5},{5,4},{6,7},{7,6},{8,9},{9,8},{10,11... | collective-permute-start | bytes 983048 | tf_op jit(solution)/shard_map/ppermute | solution.py:16
  32.7 12.6 %collective-permute-start.11 = (f32[8,5120]{1,0:T(8,128)S(1)}, f32[8,5120]{1,0:T(8,128)S(1)}, u32[]{:S(2)}, u32[]{:S(2)}) collective-permute-start(f32[8,5120]{1,0:T(8,128)S(1)} %get-tuple-element.55), channel_id=1, source_target_pairs={{0,8},{2,10},{4,12},{6,14},{8,0},{10,2},{12,4},{14,6},{16,24},{18,... | collective-permute-start | bytes 491528 | tf_op jit(solution)/shard_map/ppermute | solution.py:22
  34.3 12.9 %collective-permute-start.14 = (f32[8,5120]{1,0:T(8,128)S(1)}, f32[8,5120]{1,0:T(8,128)S(1)}, u32[]{:S(2)}, u32[]{:S(2)}) collective-permute-start(f32[8,5120]{1,0:T(8,128)S(1)} %get-tuple-element.58), channel_id=1, source_target_pairs={{0,8},{2,10},{4,12},{6,14},{8,0},{10,2},{12,4},{14,6},{16,24},{18,... | collective-permute-start | bytes 491528 | tf_op jit(solution)/shard_map/ppermute | solution.py:22
  34.9 13.5 %collective-permute-start.16 = (f32[8,5120]{1,0:T(8,128)S(1)}, f32[8,5120]{1,0:T(8,128)S(1)}, u32[]{:S(2)}, u32[]{:S(2)}) collective-permute-start(f32[8,5120]{1,0:T(8,128)S(1)} %add_subtract_fusion), channel_id=1, source_target_pairs={{0,16},{2,18},{4,20},{6,22},{8,24},{10,26},{12,28},{14,30},{16,0},... | collective-permute-start | bytes 491528 | tf_op jit(solution)/shard_map/ppermute | solution.py:16
  45.3 12.1 %collective-permute-start.17 = (f32[8,5120]{1,0:T(8,128)S(1)}, f32[8,5120]{1,0:T(8,128)S(1)}, u32[]{:S(2)}, u32[]{:S(2)}) collective-permute-start(f32[8,5120]{1,0:T(8,128)S(1)} %multiply_subtract_fusion.2), channel_id=1, source_target_pairs={{0,16},{2,18},{4,20},{6,22},{8,24},{10,26},{12,28},{14,30},{16,0},... | collective-permute-start | bytes 491528 | tf_op jit(solution)/shard_map/ppermute | solution.py:22
  47.2 11.9 %collective-permute-start.18 = (f32[8,5120]{1,0:T(8,128)S(1)}, f32[8,5120]{1,0:T(8,128)S(1)}, u32[]{:S(2)}, u32[]{:S(2)}) collective-permute-start(f32[8,5120]{1,0:T(8,128)S(1)} %multiply_subtract_fusion.1), channel_id=1, source_target_pairs={{0,16},{2,18},{4,20},{6,22},{8,24},{10,26},{12,28},{14,30},{16,0},... | collective-permute-start | bytes 491528 | tf_op jit(solution)/shard_map/ppermute | solution.py:22

commit v9 on v7

--- a/solution.py
+++ b/solution.py
@@ -144,7 +144,7 @@
                 order = (*weights, *order)
             if step == 0 and part == other:
                 remote_grads[1] += sent(later, range(shift + 1, shift + len(firsts)), tracking[part])
-            if (step, part) == (0, other) and 2 < step_count:
+            if (step, part) == (0, 0) and 2 < step_count:
                 remote_grads[2] = split(sent(packed([(2, 0, rows)], tracking[part]), [0])[0])
             if part == 0:
                 for number in range(3, step_count):

time: 60.1 us -> 60.1 us (level)
  no operation moved by 1% of the time
where the time goes in v9:
time: 60.1 us; the launch traced here: 59.9 us
  waiting for transfers between devices  28.7 us (48%)
  starting transfers between devices  23 us (38%)
  other arithmetic  7.43 us (12%)
  between operations  0.8 us (1%)
    ppermute x6, waiting for transfers between devices, swapped(): return lax.ppermute(value, axis, pairs)  19.6 us
    ppermute x13, starting transfers between devices, shifted(): return lax.ppermute(value, axis, pairs)  16.5 us
    ppermute x13, waiting for transfers between devices, shifted(): return lax.ppermute(value, axis, pairs)  9.11 us
    ppermute x6, starting transfers between devices, swapped(): return lax.ppermute(value, axis, pairs)  6.48 us
    convert_element_type x4, other arithmetic, gradient_rows(): lax.dynamic_slice(source, begin, (1, 1, 1, count, columns))[0, 0, 0]  2.78 us
  transfers between devices with their start and end apart: 19, of which 9 were waited for; matrix products, arithmetic and copies ran while one was open for 11% of the time, Pallas kernels for 0%

profile of v9, /device:TPU:0, one launch (start us, length us, event | category | flops | bytes accessed | tf_op | source)
XLA Modules:
  0.0 59.9 jit_solution(17179042138465538670)
XLA Ops:
  0.6 0.5 collective-permute-start.1
  1.1 0.9 %bitcast_convert_fusion.5 = f32[8,5120]{1,0:T(8,128)S(1)} fusion(bf16[4,1,1,32,5120]{4,3,2,1,0:T(8,128)(2,1)} %param.11, s32[]{:T(128)S(6)} %select_n.40), kind=kLoop, calls=%fused_computation.76 | loop fusion | flops 40960 | bytes 245764 | tf_op jit(solution)/shard_map/convert_element_type | solution.py:48
  2.0 2.6 %collective-permute-start.2 = (f32[8,5120]{1,0:T(8,128)S(1)}, f32[8,5120]{1,0:T(8,128)S(1)}, u32[]{:S(2)}, u32[]{:S(2)}) collective-permute-start(f32[8,5120]{1,0:T(8,128)S(1)} %bitcast_convert_fusion.5), channel_id=1, source_target_pairs={{0,1},{1,0},{2,3},{3,2},{4,5},{5,4},{6,7},{7,6},{8,9},{9,8},{10,11... | collective-permute-start | bytes 491528 | tf_op jit(solution)/shard_map/ppermute | solution.py:16
  4.6 1.3 %collective-permute-start = (f32[16,5120]{1,0:T(8,128)}, f32[16,5120]{1,0:T(8,128)S(1)}, u32[]{:S(2)}, u32[]{:S(2)}) collective-permute-start(f32[16,5120]{1,0:T(8,128)} %bitcast.99), channel_id=1, source_target_pairs={{0,2},{2,0},{4,6},{6,4},{8,10},{10,8},{12,14},{14,12},{16,18},{18,... | collective-permute-start | bytes 983048 | tf_op jit(solution)/shard_map/ppermute | solution.py:22
  5.9 1.8 %bitcast_convert_fusion.2 = (f32[8,5120]{1,0:T(8,128)S(1)}, f32[8,5120]{1,0:T(8,128)}, f32[8,5120]{1,0:T(8,128)}) fusion(bf16[4,1,1,32,5120]{4,3,2,1,0:T(8,128)(2,1)} %param.11, s32[]{:T(128)S(6)} %select_n.41, s32[]{:T(128)S(6)} %select_n.40), kind=kLoop, calls=%fused_computation.73 | loop fusion | flops 122880 | bytes 737288 | tf_op jit(solution)/shard_map/convert_element_type | solution.py:48
  7.8 0.5 collective-permute-start.4
  8.3 1.5 %collective-permute-start.5 = (f32[8,5120]{1,0:T(8,128)}, f32[8,5120]{1,0:T(8,128)S(1)}, u32[]{:S(2)}, u32[]{:S(2)}) collective-permute-start(f32[8,5120]{1,0:T(8,128)} %get-tuple-element.36), channel_id=1, source_target_pairs={{0,1},{1,0},{2,3},{3,2},{4,5},{5,4},{6,7},{7,6},{8,9},{9,8},{10,11... | collective-permute-start | bytes 491528 | tf_op jit(solution)/shard_map/ppermute | solution.py:16
  9.8 1.1 %multiply_subtract_fusion = f32[16,5120]{1,0:T(8,128)S(1)} fusion(f32[16,5120]{1,0:T(8,128)} %bitcast.100, f32[1,16,5120]{2,1,0:T(8,128)} %param.7), kind=kLoop, calls=%fused_computation.6 | loop fusion | flops 163840 | bytes 983040 | tf_op jit(solution)/shard_map/sub | solution.py:93
  10.9 0.2 collective-permute-done.1
  11.1 0.0 collective-permute-done.2
  11.2 0.0 copy-start
  11.2 0.0 copy-start.3
  11.2 1.4 %collective-permute-start.3 = (f32[8,5120]{1,0:T(8,128)S(1)}, f32[8,5120]{1,0:T(8,128)S(1)}, u32[]{:S(2)}, u32[]{:S(2)}) collective-permute-start(f32[8,5120]{1,0:T(8,128)S(1)} %fusion.22), channel_id=1, source_target_pairs={{0,4},{2,6},{4,8},{6,10},{8,12},{10,14},{12,16},{14,18},{16,20},{1... | collective-permute-start | bytes 491528 | tf_op jit(solution)/shard_map/ppermute | solution.py:16
  12.7 2.4 %collective-permute-done.4 = f32[8,5120]{1,0:T(8,128)S(1)} collective-permute-done((f32[8,5120]{1,0:T(8,128)}, f32[8,5120]{1,0:T(8,128)S(1)}, u32[]{:S(2)}, u32[]{:S(2)}) %collective-permute-start.4) | collective-permute-done | bytes 163872 | tf_op jit(solution)/shard_map/ppermute | solution.py:16
  15.1 1.6 %collective-permute-start.8 = (f32[8,5120]{1,0:T(8,128)S(1)}, f32[8,5120]{1,0:T(8,128)S(1)}, u32[]{:S(2)}, u32[]{:S(2)}) collective-permute-start(f32[8,5120]{1,0:T(8,128)S(1)} %fusion.23), channel_id=1, source_target_pairs={{0,4},{2,6},{4,8},{6,10},{8,12},{10,14},{12,16},{14,18},{16,20},{1... | collective-permute-start | bytes 491528 | tf_op jit(solution)/shard_map/ppermute | solution.py:16
  16.7 0.6 %collective-permute-start.9 = (f32[8,5120]{1,0:T(8,128)S(1)}, f32[8,5120]{1,0:T(8,128)S(1)}, u32[]{:S(2)}, u32[]{:S(2)}) collective-permute-start(f32[8,5120]{1,0:T(8,128)S(1)} %get-tuple-element.47), channel_id=1, source_target_pairs={{0,1},{1,0},{2,3},{3,2},{4,5},{5,4},{6,7},{7,6},{8,9},{9,8},{10,11... | collective-permute-start | bytes 491528 | tf_op jit(solution)/shard_map/ppermute | solution.py:16
  17.3 1.5 %collective-permute-start.10 = (f32[16,5120]{1,0:T(8,128)S(1)}, f32[16,5120]{1,0:T(8,128)S(1)}, u32[]{:S(2)}, u32[]{:S(2)}) collective-permute-start(f32[16,5120]{1,0:T(8,128)S(1)} %bitcast_convert_fusion.1), channel_id=1, source_target_pairs={{0,1},{1,0},{2,3},{3,2},{4,5},{5,4},{6,7},{7,6},{8,9},{9,8},{10,11... | collective-permute-start | bytes 983048 | tf_op jit(solution)/shard_map/ppermute | solution.py:16
  18.8 1.3 %collective-permute-done.3 = f32[8,5120]{1,0:T(8,128)S(1)} collective-permute-done((f32[8,5120]{1,0:T(8,128)S(1)}, f32[8,5120]{1,0:T(8,128)S(1)}, u32[]{:S(2)}, u32[]{:S(2)}) %collective-permute-start.3) | collective-permute-done | bytes 163872 | tf_op jit(solution)/shard_map/ppermute | solution.py:16
  20.1 0.1 add_subtract_fusion.3
  20.2 0.3 collective-permute-start.7
  20.5 0.2 add_divide_fusion.2
  20.7 0.1 maximum_subtract_fusion
  20.8 1.6 %collective-permute-start.6 = (f32[16,5120]{1,0:T(8,128)S(1)}, f32[16,5120]{1,0:T(8,128)S(1)}, u32[]{:S(2)}, u32[]{:S(2)}) collective-permute-start(f32[16,5120]{1,0:T(8,128)S(1)} %maximum_subtract_fusion), channel_id=1, source_target_pairs={{0,4},{2,6},{4,0},{6,2},{8,12},{10,14},{12,8},{14,10},{16,20},{18,... | collective-permute-start | bytes 983048 | tf_op jit(solution)/shard_map/ppermute | solution.py:22
  22.3 1.8 %collective-permute-done.8 = f32[8,5120]{1,0:T(8,128)S(1)} collective-permute-done((f32[8,5120]{1,0:T(8,128)S(1)}, f32[8,5120]{1,0:T(8,128)S(1)}, u32[]{:S(2)}, u32[]{:S(2)}) %collective-permute-start.8) | collective-permute-done | bytes 163872 | tf_op jit(solution)/shard_map/ppermute | solution.py:16
  24.1 0.1 add_subtract_fusion.2
  24.2 1.3 %collective-permute-start.12 = (f32[8,5120]{1,0:T(8,128)S(1)}, f32[8,5120]{1,0:T(8,128)S(1)}, u32[]{:S(2)}, u32[]{:S(2)}) collective-permute-start(f32[8,5120]{1,0:T(8,128)S(1)} %add_subtract_fusion.2), channel_id=1, source_target_pairs={{0,8},{2,10},{4,12},{6,14},{8,16},{10,18},{12,20},{14,22},{16,24},... | collective-permute-start | bytes 491528 | tf_op jit(solution)/shard_map/ppermute | solution.py:16
  25.5 3.5 %collective-permute-done.7 = f32[8,5120]{1,0:T(8,128)S(1)} collective-permute-done((f32[8,5120]{1,0:T(8,128)S(1)}, f32[8,5120]{1,0:T(8,128)S(1)}, u32[]{:S(2)}, u32[]{:S(2)}) %collective-permute-start.7) | collective-permute-done | bytes 163872 | tf_op jit(solution)/shard_map/ppermute | solution.py:16
  29.0 0.1 add_subtract_fusion.1
  29.0 1.8 %collective-permute-start.13 = (f32[8,5120]{1,0:T(8,128)S(1)}, f32[8,5120]{1,0:T(8,128)S(1)}, u32[]{:S(2)}, u32[]{:S(2)}) collective-permute-start(f32[8,5120]{1,0:T(8,128)S(1)} %add_subtract_fusion.1), channel_id=1, source_target_pairs={{0,16},{2,18},{4,20},{6,22},{8,24},{10,26},{12,28},{14,30},{16,0},... | collective-permute-start | bytes 491528 | tf_op jit(solution)/shard_map/ppermute | solution.py:16
  30.9 0.3 add_divide_fusion
  31.2 1.3 %collective-permute-start.15 = (f32[16,5120]{1,0:T(8,128)S(1)}, f32[16,5120]{1,0:T(8,128)S(1)}, u32[]{:S(2)}, u32[]{:S(2)}) collective-permute-start(f32[16,5120]{1,0:T(8,128)S(1)} %bitcast_convert_fusion), channel_id=1, source_target_pairs={{0,1},{1,0},{2,3},{3,2},{4,5},{5,4},{6,7},{7,6},{8,9},{9,8},{10,11... | collective-permute-start | bytes 983048 | tf_op jit(solution)/shard_map/ppermute | solution.py:16
  32.6 1.6 %collective-permute-start.11 = (f32[8,5120]{1,0:T(8,128)S(1)}, f32[8,5120]{1,0:T(8,128)S(1)}, u32[]{:S(2)}, u32[]{:S(2)}) collective-permute-start(f32[8,5120]{1,0:T(8,128)S(1)} %get-tuple-element.55), channel_id=1, source_target_pairs={{0,8},{2,10},{4,12},{6,14},{8,0},{10,2},{12,4},{14,6},{16,24},{18,... | collective-permute-start | bytes 491528 | tf_op jit(solution)/shard_map/ppermute | solution.py:22
  34.1 0.1 add_subtract_fusion
  34.2 0.6 collective-permute-start.14
  34.8 1.6 %collective-permute-start.16 = (f32[8,5120]{1,0:T(8,128)S(1)}, f32[8,5120]{1,0:T(8,128)S(1)}, u32[]{:S(2)}, u32[]{:S(2)}) collective-permute-start(f32[8,5120]{1,0:T(8,128)S(1)} %add_subtract_fusion), channel_id=1, source_target_pairs={{0,16},{2,18},{4,20},{6,22},{8,24},{10,26},{12,28},{14,30},{16,0},... | collective-permute-start | bytes 491528 | tf_op jit(solution)/shard_map/ppermute | solution.py:16
  36.4 8.8 %collective-permute-done.11 = f32[8,5120]{1,0:T(8,128)S(1)} collective-permute-done((f32[8,5120]{1,0:T(8,128)S(1)}, f32[8,5120]{1,0:T(8,128)S(1)}, u32[]{:S(2)}, u32[]{:S(2)}) %collective-permute-start.11) | collective-permute-done | bytes 163872 | tf_op jit(solution)/shard_map/ppermute | solution.py:22
  45.2 0.2 divide_subtract_fusion.1
  45.3 0.1 collective-permute-start.17
  45.4 1.7 %collective-permute-done.14 = f32[8,5120]{1,0:T(8,128)S(1)} collective-permute-done((f32[8,5120]{1,0:T(8,128)S(1)}, f32[8,5120]{1,0:T(8,128)S(1)}, u32[]{:S(2)}, u32[]{:S(2)}) %collective-permute-start.14) | collective-permute-done | bytes 163872 | tf_op jit(solution)/shard_map/ppermute | solution.py:22
  47.1 0.2 divide_subtract_fusion
  47.2 1.4 %collective-permute-start.18 = (f32[8,5120]{1,0:T(8,128)S(1)}, f32[8,5120]{1,0:T(8,128)S(1)}, u32[]{:S(2)}, u32[]{:S(2)}) collective-permute-start(f32[8,5120]{1,0:T(8,128)S(1)} %divide_subtract_fusion), channel_id=1, source_target_pairs={{0,16},{2,18},{4,20},{6,22},{8,24},{10,26},{12,28},{14,30},{16,0},... | collective-permute-start | bytes 491528 | tf_op jit(solution)/shard_map/ppermute | solution.py:22
  48.6 0.1 fusion.13
  48.7 0.1 fusion.10
  48.8 0.4 bitcast_subtract_fusion
  49.2 0.9 %maximum_bitcast_fusion.1 = (f32[1,16,5120]{2,1,0:T(8,128)}, f32[1,16,5120]{2,1,0:T(8,128)}) fusion(f32[8,5120]{1,0:T(8,128)S(1)} %get-tuple-element.66, f32[8,5120]{1,0:T(8,128)S(1)} %get-tuple-element.80, f32[8,5120]{1,0:T(8,128)S(1)} %get-tuple-element.67, f32[8,5120]{1,0:T(8,128)S(1)} %get-tuple-element.79), kind=kLoop, calls=%fused_computation.3 | loop fusion | flops 163840 | bytes 1310720 | tf_op jit(solution)/shard_map/broadcast_in_dim | solution.py:158
  50.0 7.4 %collective-permute-done.17 = f32[8,5120]{1,0:T(8,128)S(1)} collective-permute-done((f32[8,5120]{1,0:T(8,128)S(1)}, f32[8,5120]{1,0:T(8,128)S(1)}, u32[]{:S(2)}, u32[]{:S(2)}) %collective-permute-start.17) | collective-permute-done | bytes 163872 | tf_op jit(solution)/shard_map/ppermute | solution.py:22
  57.4 1.7 %collective-permute-done.18 = f32[8,5120]{1,0:T(8,128)S(1)} collective-permute-done((f32[8,5120]{1,0:T(8,128)S(1)}, f32[8,5120]{1,0:T(8,128)S(1)}, u32[]{:S(2)}, u32[]{:S(2)}) %collective-permute-start.18) | collective-permute-done | bytes 163872 | tf_op jit(solution)/shard_map/ppermute | solution.py:22
  59.2 0.7 %maximum_bitcast_fusion = f32[1,16,5120]{2,1,0:T(8,128)} fusion(f32[8,5120]{1,0:T(8,128)S(1)} %add_multiply_fusion.1, f32[8,5120]{1,0:T(8,128)S(1)} %add_multiply_fusion.2), kind=kLoop, calls=%fused_computation.2 | loop fusion | flops 81920 | bytes 655360 | tf_op jit(solution)/shard_map/broadcast_in_dim | solution.py:158
  (25 shorter events, 0.3 us)
Async XLA Ops:
  0.6 10.5 %collective-permute-start.1 = (f32[16,5120]{1,0:T(8,128)}, f32[16,5120]{1,0:T(8,128)S(1)}, u32[]{:S(2)}, u32[]{:S(2)}) collective-permute-start(f32[16,5120]{1,0:T(8,128)} %bitcast.101), channel_id=1, source_target_pairs={{0,2},{2,4},{4,6},{6,8},{8,10},{10,12},{12,14},{14,16},{16,18},{18... | collective-permute-start | bytes 983048 | tf_op jit(solution)/shard_map/ppermute | solution.py:16
  2.0 9.1 %collective-permute-start.2 = (f32[8,5120]{1,0:T(8,128)S(1)}, f32[8,5120]{1,0:T(8,128)S(1)}, u32[]{:S(2)}, u32[]{:S(2)}) collective-permute-start(f32[8,5120]{1,0:T(8,128)S(1)} %bitcast_convert_fusion.5), channel_id=1, source_target_pairs={{0,1},{1,0},{2,3},{3,2},{4,5},{5,4},{6,7},{7,6},{8,9},{9,8},{10,11... | collective-permute-start | bytes 491528 | tf_op jit(solution)/shard_map/ppermute | solution.py:16
  4.6 8.0 %collective-permute-start = (f32[16,5120]{1,0:T(8,128)}, f32[16,5120]{1,0:T(8,128)S(1)}, u32[]{:S(2)}, u32[]{:S(2)}) collective-permute-start(f32[16,5120]{1,0:T(8,128)} %bitcast.99), channel_id=1, source_target_pairs={{0,2},{2,0},{4,6},{6,4},{8,10},{10,8},{12,14},{14,12},{16,18},{18,... | collective-permute-start | bytes 983048 | tf_op jit(solution)/shard_map/ppermute | solution.py:22
  5.9 5.2 %copy-start.1 = (bf16[4,1,1,32,5120]{4,3,2,1,0:T(8,128)(2,1)S(1)}, bf16[4,1,1,32,5120]{4,3,2,1,0:T(8,128)(2,1)}, u32[]{:S(2)}) copy-start(bf16[4,1,1,32,5120]{4,3,2,1,0:T(8,128)(2,1)} %param.11) | copy-start | bytes 3932164
  7.8 4.9 %copy-start.2 = (f32[1,16,5120]{2,1,0:T(8,128)S(1)}, f32[1,16,5120]{2,1,0:T(8,128)}, u32[]{:S(2)}) copy-start(f32[1,16,5120]{2,1,0:T(8,128)} %param.6) | copy-start | bytes 983044
  7.8 7.3 %collective-permute-start.4 = (f32[8,5120]{1,0:T(8,128)}, f32[8,5120]{1,0:T(8,128)S(1)}, u32[]{:S(2)}, u32[]{:S(2)}) collective-permute-start(f32[8,5120]{1,0:T(8,128)} %get-tuple-element.35), channel_id=1, source_target_pairs={{0,1},{1,0},{2,3},{3,2},{4,5},{5,4},{6,7},{7,6},{8,9},{9,8},{10,11... | collective-permute-start | bytes 491528 | tf_op jit(solution)/shard_map/ppermute | solution.py:16
  8.3 11.8 %collective-permute-start.5 = (f32[8,5120]{1,0:T(8,128)}, f32[8,5120]{1,0:T(8,128)S(1)}, u32[]{:S(2)}, u32[]{:S(2)}) collective-permute-start(f32[8,5120]{1,0:T(8,128)} %get-tuple-element.36), channel_id=1, source_target_pairs={{0,1},{1,0},{2,3},{3,2},{4,5},{5,4},{6,7},{7,6},{8,9},{9,8},{10,11... | collective-permute-start | bytes 491528 | tf_op jit(solution)/shard_map/ppermute | solution.py:16
  11.2 9.3 %copy-start = (f32[1,16,5120]{2,1,0:T(8,128)S(1)}, f32[1,16,5120]{2,1,0:T(8,128)}, u32[]{:S(2)}) copy-start(f32[1,16,5120]{2,1,0:T(8,128)} %param.9) | copy-start | bytes 983044
  11.2 9.3 %copy-start.3 = (f32[1,16,5120]{2,1,0:T(8,128)S(1)}, f32[1,16,5120]{2,1,0:T(8,128)}, u32[]{:S(2)}) copy-start(f32[1,16,5120]{2,1,0:T(8,128)} %param.10) | copy-start | bytes 983044
  11.2 8.8 %collective-permute-start.3 = (f32[8,5120]{1,0:T(8,128)S(1)}, f32[8,5120]{1,0:T(8,128)S(1)}, u32[]{:S(2)}, u32[]{:S(2)}) collective-permute-start(f32[8,5120]{1,0:T(8,128)S(1)} %fusion.22), channel_id=1, source_target_pairs={{0,4},{2,6},{4,8},{6,10},{8,12},{10,14},{12,16},{14,18},{16,20},{1... | collective-permute-start | bytes 491528 | tf_op jit(solution)/shard_map/ppermute | solution.py:16
  15.1 9.0 %collective-permute-start.8 = (f32[8,5120]{1,0:T(8,128)S(1)}, f32[8,5120]{1,0:T(8,128)S(1)}, u32[]{:S(2)}, u32[]{:S(2)}) collective-permute-start(f32[8,5120]{1,0:T(8,128)S(1)} %fusion.23), channel_id=1, source_target_pairs={{0,4},{2,6},{4,8},{6,10},{8,12},{10,14},{12,16},{14,18},{16,20},{1... | collective-permute-start | bytes 491528 | tf_op jit(solution)/shard_map/ppermute | solution.py:16
  16.7 7.4 %collective-permute-start.9 = (f32[8,5120]{1,0:T(8,128)S(1)}, f32[8,5120]{1,0:T(8,128)S(1)}, u32[]{:S(2)}, u32[]{:S(2)}) collective-permute-start(f32[8,5120]{1,0:T(8,128)S(1)} %get-tuple-element.47), channel_id=1, source_target_pairs={{0,1},{1,0},{2,3},{3,2},{4,5},{5,4},{6,7},{7,6},{8,9},{9,8},{10,11... | collective-permute-start | bytes 491528 | tf_op jit(solution)/shard_map/ppermute | solution.py:16
  17.3 11.7 %collective-permute-start.10 = (f32[16,5120]{1,0:T(8,128)S(1)}, f32[16,5120]{1,0:T(8,128)S(1)}, u32[]{:S(2)}, u32[]{:S(2)}) collective-permute-start(f32[16,5120]{1,0:T(8,128)S(1)} %bitcast_convert_fusion.1), channel_id=1, source_target_pairs={{0,1},{1,0},{2,3},{3,2},{4,5},{5,4},{6,7},{7,6},{8,9},{9,8},{10,11... | collective-permute-start | bytes 983048 | tf_op jit(solution)/shard_map/ppermute | solution.py:16
  20.2 8.8 %collective-permute-start.7 = (f32[8,5120]{1,0:T(8,128)S(1)}, f32[8,5120]{1,0:T(8,128)S(1)}, u32[]{:S(2)}, u32[]{:S(2)}) collective-permute-start(f32[8,5120]{1,0:T(8,128)S(1)} %add_subtract_fusion.3), channel_id=1, source_target_pairs={{0,8},{2,10},{4,12},{6,14},{8,16},{10,18},{12,20},{14,22},{16,24},... | collective-permute-start | bytes 491528 | tf_op jit(solution)/shard_map/ppermute | solution.py:16
  20.8 11.7 %collective-permute-start.6 = (f32[16,5120]{1,0:T(8,128)S(1)}, f32[16,5120]{1,0:T(8,128)S(1)}, u32[]{:S(2)}, u32[]{:S(2)}) collective-permute-start(f32[16,5120]{1,0:T(8,128)S(1)} %maximum_subtract_fusion), channel_id=1, source_target_pairs={{0,4},{2,6},{4,0},{6,2},{8,12},{10,14},{12,8},{14,10},{16,20},{18,... | collective-permute-start | bytes 983048 | tf_op jit(solution)/shard_map/ppermute | solution.py:22
  24.2 8.4 %collective-permute-start.12 = (f32[8,5120]{1,0:T(8,128)S(1)}, f32[8,5120]{1,0:T(8,128)S(1)}, u32[]{:S(2)}, u32[]{:S(2)}) collective-permute-start(f32[8,5120]{1,0:T(8,128)S(1)} %add_subtract_fusion.2), channel_id=1, source_target_pairs={{0,8},{2,10},{4,12},{6,14},{8,16},{10,18},{12,20},{14,22},{16,24},... | collective-permute-start | bytes 491528 | tf_op jit(solution)/shard_map/ppermute | solution.py:16
  29.0 19.6 %collective-permute-start.13 = (f32[8,5120]{1,0:T(8,128)S(1)}, f32[8,5120]{1,0:T(8,128)S(1)}, u32[]{:S(2)}, u32[]{:S(2)}) collective-permute-start(f32[8,5120]{1,0:T(8,128)S(1)} %add_subtract_fusion.1), channel_id=1, source_target_pairs={{0,16},{2,18},{4,20},{6,22},{8,24},{10,26},{12,28},{14,30},{16,0},... | collective-permute-start | bytes 491528 | tf_op jit(solution)/shard_map/ppermute | solution.py:16
  31.2 17.4 %collective-permute-start.15 = (f32[16,5120]{1,0:T(8,128)S(1)}, f32[16,5120]{1,0:T(8,128)S(1)}, u32[]{:S(2)}, u32[]{:S(2)}) collective-permute-start(f32[16,5120]{1,0:T(8,128)S(1)} %bitcast_convert_fusion), channel_id=1, source_target_pairs={{0,1},{1,0},{2,3},{3,2},{4,5},{5,4},{6,7},{7,6},{8,9},{9,8},{10,11... | collective-permute-start | bytes 983048 | tf_op jit(solution)/shard_map/ppermute | solution.py:16
  32.6 12.6 %collective-permute-start.11 = (f32[8,5120]{1,0:T(8,128)S(1)}, f32[8,5120]{1,0:T(8,128)S(1)}, u32[]{:S(2)}, u32[]{:S(2)}) collective-permute-start(f32[8,5120]{1,0:T(8,128)S(1)} %get-tuple-element.55), channel_id=1, source_target_pairs={{0,8},{2,10},{4,12},{6,14},{8,0},{10,2},{12,4},{14,6},{16,24},{18,... | collective-permute-start | bytes 491528 | tf_op jit(solution)/shard_map/ppermute | solution.py:22
  34.2 12.9 %collective-permute-start.14 = (f32[8,5120]{1,0:T(8,128)S(1)}, f32[8,5120]{1,0:T(8,128)S(1)}, u32[]{:S(2)}, u32[]{:S(2)}) collective-permute-start(f32[8,5120]{1,0:T(8,128)S(1)} %get-tuple-element.58), channel_id=1, source_target_pairs={{0,8},{2,10},{4,12},{6,14},{8,0},{10,2},{12,4},{14,6},{16,24},{18,... | collective-permute-start | bytes 491528 | tf_op jit(solution)/shard_map/ppermute | solution.py:22
  34.8 13.9 %collective-permute-start.16 = (f32[8,5120]{1,0:T(8,128)S(1)}, f32[8,5120]{1,0:T(8,128)S(1)}, u32[]{:S(2)}, u32[]{:S(2)}) collective-permute-start(f32[8,5120]{1,0:T(8,128)S(1)} %add_subtract_fusion), channel_id=1, source_target_pairs={{0,16},{2,18},{4,20},{6,22},{8,24},{10,26},{12,28},{14,30},{16,0},... | collective-permute-start | bytes 491528 | tf_op jit(solution)/shard_map/ppermute | solution.py:16
  45.3 12.1 %collective-permute-start.17 = (f32[8,5120]{1,0:T(8,128)S(1)}, f32[8,5120]{1,0:T(8,128)S(1)}, u32[]{:S(2)}, u32[]{:S(2)}) collective-permute-start(f32[8,5120]{1,0:T(8,128)S(1)} %divide_subtract_fusion.1), channel_id=1, source_target_pairs={{0,16},{2,18},{4,20},{6,22},{8,24},{10,26},{12,28},{14,30},{16,0},... | collective-permute-start | bytes 491528 | tf_op jit(solution)/shard_map/ppermute | solution.py:22
  47.2 11.9 %collective-permute-start.18 = (f32[8,5120]{1,0:T(8,128)S(1)}, f32[8,5120]{1,0:T(8,128)S(1)}, u32[]{:S(2)}, u32[]{:S(2)}) collective-permute-start(f32[8,5120]{1,0:T(8,128)S(1)} %divide_subtract_fusion), channel_id=1, source_target_pairs={{0,16},{2,18},{4,20},{6,22},{8,24},{10,26},{12,28},{14,30},{16,0},... | collective-permute-start | bytes 491528 | tf_op jit(solution)/shard_map/ppermute | solution.py:22
